TPU v7x, 256 devices: a whole 4x4x8 slice. The times are simulated.
256 devices in a mesh: pb: 8 (over y, core), ka: 32 (over x, z).
Axes of the slice: x: 4, y: 4, z: 8, core: 2. Of those that a mesh axis runs over, the one named last changes fastest.
Arguments:
- query_vectors: bfloat16 [32768, 1024], P(('pb', 'ka')), may hold values from -1.5 to 1.5
- key_vectors: bfloat16 [16384, 1024], P(('ka', 'pb')), may hold values from -1.5 to 1.5
- value_vectors: bfloat16 [16384, 1024], P(('ka', 'pb')), may hold values from -4 to 4
- forward_out: bfloat16 [32768, 1024], P(('pb', 'ka')), may hold values from -4 to 4
- grad_out: bfloat16 [32768, 1024], P(('pb', 'ka')), may hold values from -4 to 4
- logsumexp: float32 [16, 32768], P(None, ('pb', 'ka')), may hold values from 2 to 4
- block_pairs: int32 [8, 32, 2, 24], P('pb'), may hold values from 0 to 31, as said below
- counts: int32 [8, 32], P('pb'), may hold values from 1 to 24, as said below
Outputs:
- grad_queries: bfloat16 [32768, 1024], P(('pb', 'ka'))
- grad_keys: bfloat16 [16384, 1024], P(('ka', 'pb'))
- grad_values: bfloat16 [16384, 1024], P(('ka', 'pb'))
Inputs may be any that keep to these rules, and one draw needn't show every extreme that they name: `block_pairs`: the 24 pairs of one query shard with one key shard are distinct; entry 0 is a query block below 32, entry 1 a key block below 4; slots at or after the count are to be ignored. `counts`: some query shard and key shard have exactly 24 used slots in every draw.
All inputs are finite; a program needn't handle non-finite values.
Results may differ from a plain program's by a relative error of at most 0.005.
Values may be sent and summed in bfloat16 or wider, within the bound.
A program may use at most 128 MiB of HBM per device.

v0:
```python
import jax
import jax.numpy as jnp
from jax import lax
from jax.sharding import PartitionSpec as P

HEADS = 16
HEAD_DIM = 64
BLK = 128


def head_grads(query_block, dout_block, stat_block, key_block, value_block):
    count_rows = query_block.shape[0]
    model_width = query_block.shape[1]
    score_scale = HEAD_DIM ** (-0.5)
    query_heads = query_block.reshape(count_rows, HEADS, HEAD_DIM)
    dout_heads = dout_block.reshape(count_rows, HEADS, HEAD_DIM)
    key_heads = key_block.reshape(count_rows, HEADS, HEAD_DIM)
    value_heads = value_block.reshape(count_rows, HEADS, HEAD_DIM)
    scores = (
        jnp.einsum("qhd,khd->hqk", query_heads, key_heads, preferred_element_type=jnp.float32)
        * score_scale
    )
    attn_prob = jnp.exp(scores - stat_block[0][:, :, None])
    prob_half = attn_prob.astype(jnp.bfloat16)
    value_add = jnp.einsum(
        "hqk,qhd->khd", prob_half, dout_heads, preferred_element_type=jnp.float32
    )
    dprob = jnp.einsum("qhd,khd->hqk", dout_heads, value_heads, preferred_element_type=jnp.float32)
    dscore = (attn_prob * (dprob - stat_block[1][:, :, None])).astype(jnp.bfloat16)
    query_add = (
        jnp.einsum("hqk,khd->qhd", dscore, key_heads, preferred_element_type=jnp.float32)
        * score_scale
    )
    key_add = (
        jnp.einsum("hqk,qhd->khd", dscore, query_heads, preferred_element_type=jnp.float32)
        * score_scale
    )
    return (
        query_add.reshape(count_rows, model_width),
        key_add.reshape(count_rows, model_width),
        value_add.reshape(count_rows, model_width),
    )


def apply_pair(
    totals, query_block, key_block, key_side, query_all, dout_all, stats_all, key_stack, value_stack
):
    query_grad, key_grad, value_grad = totals
    model_width = query_all.shape[1]
    query_row = query_block * BLK
    key_row = key_block * BLK
    q_rows = lax.dynamic_slice_in_dim(query_all, query_row, BLK, 0)
    d_rows = lax.dynamic_slice_in_dim(dout_all, query_row, BLK, 0)
    s_rows = lax.dynamic_slice_in_dim(stats_all, query_row, BLK, 2)
    k_rows = lax.dynamic_slice(key_stack, (key_side, key_row, 0), (1, BLK, model_width))[0]
    v_rows = lax.dynamic_slice(value_stack, (key_side, key_row, 0), (1, BLK, model_width))[0]
    query_add, key_add, value_add = head_grads(q_rows, d_rows, s_rows, k_rows, v_rows)
    query_grad = lax.dynamic_update_slice_in_dim(
        query_grad,
        lax.dynamic_slice_in_dim(query_grad, query_row, BLK, 0) + query_add,
        query_row,
        0,
    )
    old_key = lax.dynamic_slice(key_grad, (key_side, key_row, 0), (1, BLK, model_width))
    key_grad = lax.dynamic_update_slice(key_grad, old_key + key_add[None], (key_side, key_row, 0))
    old_value = lax.dynamic_slice(value_grad, (key_side, key_row, 0), (1, BLK, model_width))
    value_grad = lax.dynamic_update_slice(
        value_grad, old_value + value_add[None], (key_side, key_row, 0)
    )
    return (query_grad, key_grad, value_grad)


def body(
    query_vectors, key_vectors, value_vectors, forward_out, grad_out, logsumexp, block_pairs, counts
):
    local_rows = query_vectors.shape[0]
    model_width = query_vectors.shape[1]
    products = grad_out.astype(jnp.float32) * forward_out.astype(jnp.float32)
    row_delta = jnp.sum(products.reshape(local_rows, HEADS, HEAD_DIM), axis=2).T
    local_stats = jnp.stack([logsumexp, row_delta], axis=0)
    query_all, dout_all = (
        lax.all_gather(query_vectors, "ka", axis=0, tiled=True),
        lax.all_gather(grad_out, "ka", axis=0, tiled=True),
    )
    stats_all = lax.all_gather(local_stats, "ka", axis=2, tiled=True)
    key_all, value_all = (
        lax.all_gather(key_vectors, "pb", axis=0, tiled=True),
        lax.all_gather(value_vectors, "pb", axis=0, tiled=True),
    )
    shard_rows = key_all.shape[0]
    row_pairs = block_pairs[0]
    row_counts = counts[0]
    own_index = lax.axis_index("ka")
    query_zero = jnp.zeros((query_all.shape[0], model_width), jnp.float32)
    own_pairs = lax.dynamic_index_in_dim(row_pairs, own_index, 0, keepdims=False)
    own_count = row_counts[own_index]
    key_stack = key_all[None]
    value_stack = value_all[None]

    def pair_step(slot_index, totals):
        return apply_pair(
            totals,
            own_pairs[0, slot_index],
            own_pairs[1, slot_index],
            0,
            query_all,
            dout_all,
            stats_all,
            key_stack,
            value_stack,
        )

    key_zero = jnp.zeros((1, shard_rows, model_width), jnp.float32)
    query_grad, key_grad, value_grad = lax.fori_loop(
        0, own_count, pair_step, (query_zero, key_zero, key_zero)
    )
    key_own = key_grad[0]
    value_own = value_grad[0]
    grad_queries = lax.psum_scatter(query_grad, "ka", scatter_dimension=0, tiled=True).astype(
        jnp.bfloat16
    )
    key_sum, value_sum = (
        lax.psum_scatter(key_own, "pb", scatter_dimension=0, tiled=True),
        lax.psum_scatter(value_own, "pb", scatter_dimension=0, tiled=True),
    )
    return (grad_queries, key_sum.astype(jnp.bfloat16), value_sum.astype(jnp.bfloat16))


def solution(mesh):
    placed = (
        P(("pb", "ka"), None),
        P(("ka", "pb"), None),
        P(("ka", "pb"), None),
        P(("pb", "ka"), None),
        P(("pb", "ka"), None),
        P(None, ("pb", "ka")),
        P("pb", None, None, None),
        P("pb", None),
    )
    return jax.shard_map(
        body,
        mesh=mesh,
        in_specs=placed,
        out_specs=(P(("pb", "ka"), None), P(("ka", "pb"), None), P(("ka", "pb"), None)),
        check_vma=False,
    )
```

profile of v0, /device:TPU:1, one launch (start us, length us, event | category | flops | bytes accessed | tf_op | source)
XLA Modules:
  0.0 988.8 jit_solution(11806698275893660828)
XLA Ops:
  8.7 1.8 copy.28
  10.6 1.8 copy.27
  12.5 1.1 copy.29
  15.5 39.6 %all_gather.17 = f32[2,16,4096]{2,1,0:T(8,128)S(1)} all-gather(f32[2,16,128]{2,1,0:T(8,128)S(1)} %pad_maximum_fusion), channel_id=1, replica_groups=mesh['pb'=8,'ka'=32] {'ka'}, dimensions={2}, use_global_device_ids=true | all-gather | bytes 540672 | tf_op jit(solution)/shard_map/all_gather | solution.py:85
  55.1 12.7 %all-gather.11.cloned.1.call-done = bf16[512,1024]{1,0:T(8,128)(2,1)} async-done(((bf16[64,1024]{1,0:T(8,128)(2,1)}), bf16[512,1024]{1,0:T(8,128)(2,1)}) %all-gather.11.cloned.1.call-update) | async-done | bytes 1048592 | tf_op jit(solution)/shard_map/all_gather | solution.py:88
  67.8 103.1 %all-gather.9.cloned.1.call-done = bf16[4096,1024]{0,1:T(8,128)(2,1)} async-done(((bf16[128,1024]{0,1:T(8,128)(2,1)}), bf16[4096,1024]{0,1:T(8,128)(2,1)}) %all-gather.9.cloned.1.call-update) | async-done | bytes 8388624 | tf_op jit(solution)/shard_map/all_gather | solution.py:83
  170.9 104.2 %all-gather.7.cloned.1.call-done = bf16[4096,1024]{0,1:T(8,128)(2,1)} async-done(((bf16[128,1024]{0,1:T(8,128)(2,1)}), bf16[4096,1024]{0,1:T(8,128)(2,1)}) %all-gather.7.cloned.1.call-update) | async-done | bytes 8388624 | tf_op jit(solution)/shard_map/all_gather | solution.py:82
  275.1 1.6 broadcast_in_dim.13.clone2
  276.8 1.6 broadcast_in_dim.13.clone
  278.3 7.9 broadcast_in_dim.12.clone
  286.2 79.2 %while.14 = (s32[]{:T(128)}, f32[4096,1024]{1,0:T(8,128)}, f32[1,512,1024]{2,1,0:T(8,128)}, f32[1,512,1024]{2,1,0:T(8,128)}, s32[]{:T(128)}, /*index=5*/s32[2,24...) while((s32[]{:T(128)}, f32[4096,1024]{1,0:T(8,128)}, ...), condition=%wide.region_2.3_spmd, body=%wide.region_1.2_spmd.sunk | while | flops 170000400 | bytes 32817584 | solution.py:114
  294.5 1.1 constant_dynamic-slice_fusion.25
  300.0 1.1 constant_dynamic-update-slice_fusion.6
  310.3 1.1 constant_dynamic-slice_fusion.25
  315.7 1.1 constant_dynamic-update-slice_fusion.6
  324.7 1.1 constant_dynamic-slice_fusion.19
  331.5 1.1 constant_dynamic-update-slice_fusion.6
  362.8 1.1 constant_dynamic-update-slice_fusion.6
  366.8 329.5 %reduce-scatter.8.cloned.1.call-done = f32[64,1024]{1,0:T(8,128)} async-done(((f32[512,1024]{1,0:T(8,128)}), f32[64,1024]{1,0:T(8,128)}) %reduce-scatter.8.cloned.1.call-update) | async-done | bytes 262160 | tf_op jit(solution)/shard_map/reduce_scatter | solution.py:124
  696.3 1.6 convert_element_type.25
  698.0 35.9 %reduce-scatter.6.cloned.1.call-done = f32[64,1024]{1,0:T(8,128)} async-done(((f32[512,1024]{1,0:T(8,128)}), f32[64,1024]{1,0:T(8,128)}) %reduce-scatter.6.cloned.1.call-update) | async-done | bytes 262160 | tf_op jit(solution)/shard_map/reduce_scatter | solution.py:123
  733.8 1.6 convert_element_type.24
  735.4 244.7 %reduce-scatter.4.cloned.1.call-done = f32[128,1024]{1,0:T(8,128)} async-done(((f32[4096,1024]{1,0:T(8,128)}), f32[128,1024]{1,0:T(8,128)}) %reduce-scatter.4.cloned.1.call-update) | async-done | bytes 524304 | tf_op jit(solution)/shard_map/reduce_scatter | solution.py:119
  980.2 1.8 convert_element_type.23
  (173 shorter events, 64.9 us)
Async XLA Ops:
  7.2 7.0 copy-start
  7.2 6.4 copy-start.4
  7.2 8.2 copy-start.3
  7.2 47.9 %all-gather.5.cloned.1.call-start = ((), (), s32[]{:S(2)}) async-start(), calls=%async_computation.3 | async-start | bytes 1179648 | tf_op jit(solution)/shard_map/all_gather | solution.py:87
  7.9 59.9 %all-gather.11.cloned.1.call-start = ((), (), s32[]{:S(2)}) async-start(), calls=%async_computation.6 | async-start | bytes 1179648 | tf_op jit(solution)/shard_map/all_gather | solution.py:88
  8.7 162.2 %all-gather.9.cloned.1.call-start = ((), (), s32[]{:S(2)}) async-start(), calls=%async_computation.5 | async-start | bytes 8650752 | tf_op jit(solution)/shard_map/all_gather | solution.py:83
  10.5 264.6 %all-gather.7.cloned.1.call-start = ((), (), s32[]{:S(2)}) async-start(), calls=%async_computation.4 | async-start | bytes 8650752 | tf_op jit(solution)/shard_map/all_gather | solution.py:82
  12.4 683.9 %reduce-scatter.8.cloned.1.call-start = ((), (), s32[]{:S(2)}) async-start(), calls=%async_computation.9 | async-start | bytes 2359296 | tf_op jit(solution)/shard_map/reduce_scatter | solution.py:124
  286.9 5.2 copy-start.1
  299.8 2.2 copy-start.2
  302.6 5.2 copy-start.1
  315.5 2.2 copy-start.2
  318.3 5.2 copy-start.1
  331.2 2.2 copy-start.2
  334.1 5.2 copy-start.1
  347.0 2.1 copy-start.2
  349.7 5.2 copy-start.1
  362.6 2.2 copy-start.2
  365.5 368.3 %reduce-scatter.6.cloned.1.call-start = ((), (), s32[]{:S(2)}) async-start(), calls=%async_computation.8 | async-start | bytes 2359296 | tf_op jit(solution)/shard_map/reduce_scatter | solution.py:123
  366.1 614.1 %reduce-scatter.4.cloned.1.call-start = ((), (), s32[]{:S(2)}) async-start(), calls=%async_computation.7 | async-start | bytes 17301504 | tf_op jit(solution)/shard_map/reduce_scatter | solution.py:119
Sparse Core Ops, SparseCore 0:
  9.9 30.1 all-gather.4
  42.0 25.7 all-gather.10
  70.3 100.6 all-gather.8
  173.8 101.2 all-gather.6
  365.6 330.6 reduce-scatter.7
  698.7 35.0 reduce-scatter.5
  737.9 242.1 reduce-scatter.3
where the time goes:
time: 1000 us; the launch traced here: 989 us
  waiting for transfers between devices  833 us (83%)
  local copies, waits for them, and re-layouts  73.3 us (7%)
  blocking collectives  39.6 us (4%)
  between operations  14.2 us (1%)
  loops' own time  11.4 us (1%)
  matrix products  10.3 us (1%)
    reduce_scatter x1, waiting for transfers between devices, body(): lax.psum_scatter(value_own, 'pb', scatter_dimension=0, tiled=True)  330 us
    reduce_scatter x1, waiting for transfers between devices, body(): lax.psum_scatter(query_grad, 'ka', scatter_dimension=0, tiled=True)  245 us
    all_gather x1, waiting for transfers between devices, body(): lax.all_gather(query_vectors, 'ka', axis=0, tiled=True)  104 us
    all_gather x1, waiting for transfers between devices, body(): lax.all_gather(grad_out, 'ka', axis=0, tiled=True)  103 us
    all_gather x1, blocking collectives, body(): stats_all = lax.all_gather(local_stats, 'ka', axis=2, tiled=True)  39.6 us
    reduce_scatter x1, waiting for transfers between devices, body(): lax.psum_scatter(key_own, 'pb', scatter_dimension=0, tiled=True)  35.9 us
  transfers between devices with their start and end apart: 7, of which 6 were waited for; matrix products, arithmetic and copies ran while one was open for 1% of the time, Pallas kernels for 0%

commit v1 on v0

v1 whole, which is shorter than its diff:
```python
import jax
import jax.numpy as jnp
from jax import lax
from jax.experimental import pallas as pl
from jax.experimental.pallas import tpu as pltpu
from jax.sharding import PartitionSpec as P

NX, NY, NZ = 4, 4, 8
HEADS = 16
BLK = 128
HALF = BLK // 2
WIDTH = 1024
HEAD_PAIRS = WIDTH // 128
KEY_BLOCKS = NX * NY
BUCKET = 16
SCALE = 64**-0.5
LOG2E = 1.4426950408889634
MESH = pl.DeviceIdType.MESH
ANY = pl.BlockSpec(memory_space=pl.ANY)
F32 = jnp.float32
BF16 = jnp.bfloat16


class Place:
    def __init__(self):
        pb = lax.axis_index("pb")
        ka = lax.axis_index("ka")
        self.y = lax.div(pb, 2)
        self.core = lax.rem(pb, 2)
        self.x = lax.div(ka, NZ)
        self.z = lax.rem(ka, NZ)
        self.sibling = (self.y * 2 + 1 - self.core, ka)

    def over_x(self, step):
        return (self.y * 2 + self.core, self.xs(step) * NZ + self.z)

    def over_y(self, step):
        return (self.ys(step) * 2 + self.core, self.x * NZ + self.z)

    def over_z(self, step):
        return (self.y * 2 + self.core, self.x * NZ + self.zs(step))

    def xs(self, step):
        return lax.rem(self.x + step + NX, NX)

    def ys(self, step):
        return lax.rem(self.y + step + NY, NY)

    def zs(self, step):
        return lax.rem(self.z + step + NZ, NZ)

    def greet(self):
        barrier = pltpu.get_barrier_semaphore()
        neighbours = [self.sibling]
        for step in (1, -1):
            neighbours += [self.over_x(step), self.over_y(step), self.over_z(step)]
        for neighbour in neighbours:
            pl.semaphore_signal(barrier, inc=1, device_id=neighbour, device_id_type=MESH)
        pl.semaphore_wait(barrier, len(neighbours))


class Sender:
    def __init__(self, send_sems, recv_sems):
        self.send_sems = send_sems
        self.recv_sems = recv_sems
        self.copies = []

    def __call__(self, source, target, device):
        index = len(self.copies)
        copy = pltpu.make_async_remote_copy(
            src_ref=source,
            dst_ref=target,
            send_sem=self.send_sems.at[index],
            recv_sem=self.recv_sems.at[index],
            device_id=device,
            device_id_type=MESH,
        )
        copy.start()
        self.copies.append(copy)
        return copy

    def finish(self):
        for copy in self.copies:
            copy.wait_send()


GATHER_COPIES = 45


def gather_kernel(
    q_ref, do_ref, k_ref, v_ref, out_ref, lse_ref,
    q_all, do_all, st_all, k_all, v_all,
    do_buf, out_buf, st_buf, send_sems, recv_sems, local_sems,
):
    me = Place()
    x, y, z = me.x, me.y, me.z
    rows = pl.ds(pl.multiple_of(me.core * HALF, HALF), HALF)

    def part(which):
        return pl.ds(pl.multiple_of(me.core * HALF + which * (HALF // 2), HALF // 2), HALF // 2)

    loads = [
        pltpu.make_async_copy(do_ref, do_buf, local_sems.at[0]),
        pltpu.make_async_copy(out_ref, out_buf, local_sems.at[1]),
        pltpu.make_async_copy(lse_ref, st_buf.at[pl.ds(0, HEADS)], local_sems.at[2]),
    ]
    for load in loads:
        load.start()
    owns = [
        pltpu.make_async_copy(k_ref, k_all.at[y, x, rows], local_sems.at[3]),
        pltpu.make_async_copy(v_ref, v_all.at[x, y, rows], local_sems.at[4]),
        pltpu.make_async_copy(q_ref, q_all.at[z], local_sems.at[5]),
        pltpu.make_async_copy(do_ref, do_all.at[z], local_sems.at[6]),
    ]
    for own in owns:
        own.start()
    me.greet()
    send = Sender(send_sems, recv_sems)
    up, down = me.over_z(1), me.over_z(-1)
    q_up = [send(q_ref, q_all.at[z], up)]
    do_down = [send(do_ref, do_all.at[z], down)]
    k_right = send(k_ref, k_all.at[y, x, rows], me.over_x(1))
    k_left = send(k_ref, k_all.at[y, x, rows], me.over_x(-1))
    v_right = send(v_ref, v_all.at[x, y, rows], me.over_y(1))
    v_left = send(v_ref, v_all.at[x, y, rows], me.over_y(-1))
    do_up = [send(do_ref, do_all.at[z], up)]
    q_down = [send(q_ref, q_all.at[z], down)]

    for load in loads:
        load.wait()
    products = do_buf[...].astype(F32) * out_buf[...].astype(F32)
    high = products.astype(BF16)
    low = (products - high.astype(F32)).astype(BF16)
    head = lax.broadcasted_iota(jnp.int32, (HEADS, WIDTH), 0) * 64
    feature = lax.broadcasted_iota(jnp.int32, (HEADS, WIDTH), 1)
    member = jnp.where((feature >= head) & (feature < head + 64), 1.0, 0.0).astype(BF16)
    over_features = (((1,), (1,)), ((), ()))
    delta = lax.dot_general(member, high, over_features, preferred_element_type=F32)
    delta = delta + lax.dot_general(member, low, over_features, preferred_element_type=F32)
    st_buf[pl.ds(0, HEADS), :] = st_buf[pl.ds(0, HEADS), :] * LOG2E
    st_buf[pl.ds(HEADS, HEADS), :] = delta
    st_own = pltpu.make_async_copy(st_buf, st_all.at[z], local_sems.at[7])
    st_own.start()
    st_up = [send(st_buf, st_all.at[z], up)]
    st_down = [send(st_buf, st_all.at[z], down)]

    k_right.wait_recv()
    k_far = [send(k_all.at[y, me.xs(-1), part(0)], k_all.at[y, me.xs(-1), part(0)], me.over_x(1))]
    v_right.wait_recv()
    v_far = [send(v_all.at[x, me.ys(-1), part(0)], v_all.at[x, me.ys(-1), part(0)], me.over_y(1))]
    k_left.wait_recv()
    k_far.append(send(k_all.at[y, me.xs(1), part(1)], k_all.at[y, me.xs(1), part(1)], me.over_x(-1)))
    v_left.wait_recv()
    v_far.append(send(v_all.at[x, me.ys(1), part(1)], v_all.at[x, me.ys(1), part(1)], me.over_y(-1)))

    for own in owns:
        own.wait()
    every = slice(None)
    for copy in k_far:
        copy.wait_recv()
    k_own = k_all.at[y, every, rows]
    k_right = send(k_own, k_own, me.over_y(1))
    k_left = send(k_own, k_own, me.over_y(-1))
    for copy in v_far:
        copy.wait_recv()
    v_own = v_all.at[x, every, rows]
    v_right = send(v_own, v_own, me.over_x(1))
    v_left = send(v_own, v_own, me.over_x(-1))
    from_sibling = [send(k_own, k_own, me.sibling), send(v_own, v_own, me.sibling)]

    def forward_up(hop, which, blocks, copies):
        copies[hop - 1].wait_recv()
        block = blocks.at[me.zs(-hop)]
        copies.append(send(block, block, up))

    def forward_down(hop, which, blocks, copies):
        copies[hop - 1].wait_recv()
        block = blocks.at[me.zs(hop)]
        copies.append(send(block, block, down))

    def hop_first(hop):
        forward_up(hop, 0, q_all, q_up)
        forward_down(hop, 0, do_all, do_down)

    def hop_second(hop):
        forward_up(hop, 1, do_all, do_up)
        forward_down(hop, 1, q_all, q_down)
        forward_up(hop, 2, st_all, st_up)
        forward_down(hop, 2, st_all, st_down)

    hop_first(1)
    hop_second(1)

    def across(blocks, line, step, low, device):
        part = blocks.at[line(step), pl.ds(low, 2), rows]
        return send(part, part, device)

    k_right.wait_recv()
    k_far = [across(k_all, me.ys, -1, 0, me.over_y(1))]
    v_right.wait_recv()
    v_far = [across(v_all, me.xs, -1, 0, me.over_x(1))]
    k_left.wait_recv()
    k_far.append(across(k_all, me.ys, 1, 2, me.over_y(-1)))
    v_left.wait_recv()
    v_far.append(across(v_all, me.xs, 1, 2, me.over_x(-1)))
    for step in (-1, 1):
        k_near = k_all.at[me.ys(step), every, rows]
        from_sibling.append(send(k_near, k_near, me.sibling))
        v_near = v_all.at[me.xs(step), every, rows]
        from_sibling.append(send(v_near, v_near, me.sibling))

    hop_first(2)
    for copy in k_far + v_far:
        copy.wait_recv()
    k_last = k_all.at[me.ys(2), every, rows]
    from_sibling.append(send(k_last, k_last, me.sibling))
    v_last = v_all.at[me.xs(2), every, rows]
    from_sibling.append(send(v_last, v_last, me.sibling))
    hop_second(2)

    forward_up(3, 0, q_all, q_up)
    forward_down(3, 0, do_all, do_down)
    do_up[2].wait_recv()
    q_down[2].wait_recv()
    forward_up(3, 2, st_all, st_up)
    st_down[2].wait_recv()
    for copy in from_sibling:
        copy.wait_recv()
    st_own.wait()
    q_up[3].wait_recv()
    do_down[3].wait_recv()
    st_up[3].wait_recv()
    send.finish()
    assert len(send.copies) == GATHER_COPIES, len(send.copies)


def gather(q, do, k, v, out, lse):
    return pl.pallas_call(
        gather_kernel,
        out_shape=[
            jax.ShapeDtypeStruct((NZ, BLK, WIDTH), BF16),
            jax.ShapeDtypeStruct((NZ, BLK, WIDTH), BF16),
            jax.ShapeDtypeStruct((NZ, 2 * HEADS, BLK), F32),
            jax.ShapeDtypeStruct((NY, NX, BLK, WIDTH), BF16),
            jax.ShapeDtypeStruct((NX, NY, BLK, WIDTH), BF16),
        ],
        in_specs=[ANY] * 6,
        out_specs=[ANY] * 5,
        scratch_shapes=[
            pltpu.VMEM((BLK, WIDTH), BF16),
            pltpu.VMEM((BLK, WIDTH), BF16),
            pltpu.VMEM((2 * HEADS, BLK), F32),
            pltpu.SemaphoreType.DMA((GATHER_COPIES,)),
            pltpu.SemaphoreType.DMA((GATHER_COPIES,)),
            pltpu.SemaphoreType.DMA((8,)),
        ],
        compiler_params=pltpu.CompilerParams(
            collective_id=0, has_side_effects=True, vmem_limit_bytes=16 << 20
        ),
        name="gather_blocks",
    )(q, do, k, v, out, lse)


def pair_kernel(
    pairs, counts, place, q_all, do_all, st_all, k_all, v_all,
    dq_out, dk_out, dv_out,
    q_buf, do_buf, st_buf, k_buf, v_buf, k_turned, dq_sum, dk_sum, dv_sum, dq_stage, dk_stage, dv_stage, zeros,
    listed, filled, flat, in_sems, out_sems, zero_sems, dq_sems,
):
    x = place[0]
    z = place[1]
    for block in range(KEY_BLOCKS):
        filled[block] = 0
    for column in range(NX):
        shard = column * NZ + z

        def enlist(slot, carry, column=column, shard=shard):
            query = pairs[0, shard, 0, slot]
            block = pairs[0, shard, 1, slot] * NX + column
            have = filled[block]
            listed[block * BUCKET + have] = block * NZ + lax.rem(query, NZ)
            filled[block] = have + jnp.where(lax.div(query, NZ) == x, 1, 0)
            return carry

        lax.fori_loop(0, counts[0, shard], enlist, 0)
    zeros[...] = jnp.zeros_like(zeros)
    total = jnp.int32(0)
    for block in range(KEY_BLOCKS):

        def append(slot, position, block=block):
            flat[position] = listed[block * BUCKET + slot]
            return position + 1

        total = lax.fori_loop(0, filled[block], append, total)
        empty = filled[block] == 0
        up, across = divmod(block, NX)

        @pl.when(empty)
        def _(up=up, across=across):
            pltpu.make_async_copy(zeros, dk_out.at[up, across], zero_sems.at[0]).start()
            pltpu.make_async_copy(zeros, dv_out.at[across, up], zero_sems.at[1]).start()

    def fetches(index, slot):
        entry = flat[index]
        block = lax.div(entry, NZ)
        query = lax.rem(entry, NZ)
        up, across = lax.div(block, NX), lax.rem(block, NX)
        return [
            pltpu.make_async_copy(k_all.at[up, across], k_buf.at[slot], in_sems.at[slot, 0]),
            pltpu.make_async_copy(q_all.at[query], q_buf.at[slot], in_sems.at[slot, 1]),
            pltpu.make_async_copy(st_all.at[query], st_buf.at[slot], in_sems.at[slot, 2]),
            pltpu.make_async_copy(v_all.at[across, up], v_buf.at[slot], in_sems.at[slot, 3]),
            pltpu.make_async_copy(do_all.at[query], do_buf.at[slot], in_sems.at[slot, 4]),
        ]

    @pl.when(total > 0)
    def _():
        for fetch in fetches(0, 0):
            fetch.start()

    def clear(query, carry):
        dq_sum[query] = jnp.zeros((WIDTH, BLK), F32)
        return carry

    lax.fori_loop(0, NZ, clear, 0)

    lane = lax.broadcasted_iota(jnp.int32, (1, 128), 1)
    first_half = jnp.where(lane < 64, 1.0, 0.0).astype(BF16)
    second_half = jnp.where(lane < 64, 0.0, 1.0).astype(BF16)
    nt = (((1,), (1,)), ((), ()))
    nn = (((1,), (0,)), ((), ()))

    def flush_copies(slot, block):
        up, across = lax.div(block, NX), lax.rem(block, NX)
        return [
            pltpu.make_async_copy(dk_stage.at[slot], dk_out.at[up, across], out_sems.at[slot, 0]),
            pltpu.make_async_copy(dv_stage.at[slot], dv_out.at[across, up], out_sems.at[slot, 1]),
        ]

    def step(index, flushed):
        slot = lax.rem(index, 2)
        block = lax.div(flat[index], NZ)
        query = lax.rem(flat[index], NZ)
        before = jnp.where(index > 0, lax.div(flat[jnp.maximum(index - 1, 0)], NZ), -1)
        after = jnp.where(
            index + 1 < total, lax.div(flat[jnp.minimum(index + 1, total - 1)], NZ), -1
        )

        @pl.when(index + 1 < total)
        def _():
            for fetch in fetches(index + 1, 1 - slot):
                fetch.start()

        for fetch in fetches(index, slot):
            fetch.wait()

        @pl.when(before != block)
        def _():
            dk_sum[...] = jnp.zeros_like(dk_sum)
            dv_sum[...] = jnp.zeros_like(dv_sum)
            for pair in range(HEAD_PAIRS):
                lanes = slice(pair * 128, pair * 128 + 128)
                turned = jnp.transpose(k_buf[slot, :, lanes].astype(F32)).astype(BF16)
                k_turned[lanes, :] = turned

        for pair in range(HEAD_PAIRS):
            lanes = slice(pair * 128, pair * 128 + 128)
            keys = k_buf[slot, :, lanes]
            values = v_buf[slot, :, lanes]
            queries = q_buf[slot, :, lanes]
            douts = do_buf[slot, :, lanes]
            q_two = jnp.concatenate([queries * first_half, queries * second_half], axis=0)
            do_two = jnp.concatenate([douts * first_half, douts * second_half], axis=0)
            scores = lax.dot_general(keys, q_two, nt, preferred_element_type=F32)
            dprob = lax.dot_general(values, do_two, nt, preferred_element_type=F32)
            probs, dscores = [], []
            for side in range(2):
                head = 2 * pair + side
                cut = slice(side * BLK, side * BLK + BLK)
                lse = st_buf[slot, head : head + 1, :]
                delta = st_buf[slot, HEADS + head : HEADS + head + 1, :]
                prob = jnp.exp2(scores[:, cut] * (SCALE * LOG2E) - lse)
                probs.append(prob.astype(BF16))
                dscores.append((prob * (dprob[:, cut] - delta)).astype(BF16))
            dv_sum[:, lanes] += lax.dot_general(
                jnp.concatenate(probs, axis=1), do_two, nn, preferred_element_type=F32
            )
            dk_sum[:, lanes] += lax.dot_general(
                jnp.concatenate(dscores, axis=1), q_two, nn, preferred_element_type=F32
            )
            turned = k_turned[lanes, :]
            for side in range(2):
                low = pair * 128 + side * 64
                dq_sum[query, low : low + 64, :] += lax.dot_general(
                    turned[side * 64 : side * 64 + 64], dscores[side], nn, preferred_element_type=F32
                )

        @pl.when(after != block)
        def _():
            stage = lax.rem(flushed, 2)

            @pl.when(flushed >= 2)
            def _():
                for copy in flush_copies(stage, block):
                    copy.wait()

            dk_stage[stage] = (dk_sum[...] * SCALE).astype(BF16)
            dv_stage[stage] = dv_sum[...].astype(BF16)
            for copy in flush_copies(stage, block):
                copy.start()

        return flushed + jnp.where(after != block, 1, 0)

    flushed = lax.fori_loop(0, total, step, 0)

    def turn_in(query, carry):
        dq_stage[query] = (dq_sum[query] * SCALE).astype(BF16)
        pltpu.make_async_copy(dq_stage.at[query], dq_out.at[query], dq_sems.at[query]).start()
        return carry

    lax.fori_loop(0, NZ, turn_in, 0)
    for slot in range(2):

        @pl.when(flushed > slot)
        def _(slot=slot):
            for copy in flush_copies(slot, 0):
                copy.wait()

    for block in range(KEY_BLOCKS):
        up, across = divmod(block, NX)

        @pl.when(filled[block] == 0)
        def _(up=up, across=across):
            pltpu.make_async_copy(zeros, dk_out.at[up, across], zero_sems.at[0]).wait()
            pltpu.make_async_copy(zeros, dv_out.at[across, up], zero_sems.at[1]).wait()

    def finish(query, carry):
        pltpu.make_async_copy(dq_stage.at[query], dq_out.at[query], dq_sems.at[query]).wait()
        return carry

    lax.fori_loop(0, NZ, finish, 0)


def pairs_over_blocks(pairs, counts, place, q_all, do_all, st_all, k_all, v_all):
    smem = pl.BlockSpec(memory_space=pltpu.SMEM)
    return pl.pallas_call(
        pair_kernel,
        out_shape=[
            jax.ShapeDtypeStruct((NZ, WIDTH, BLK), BF16),
            jax.ShapeDtypeStruct((NY, NX, BLK, WIDTH), BF16),
            jax.ShapeDtypeStruct((NX, NY, BLK, WIDTH), BF16),
        ],
        in_specs=[smem] * 3 + [ANY] * 5,
        out_specs=[ANY] * 3,
        scratch_shapes=[
            pltpu.VMEM((2, BLK, WIDTH), BF16),
            pltpu.VMEM((2, BLK, WIDTH), BF16),
            pltpu.VMEM((2, 2 * HEADS, BLK), F32),
            pltpu.VMEM((2, BLK, WIDTH), BF16),
            pltpu.VMEM((2, BLK, WIDTH), BF16),
            pltpu.VMEM((WIDTH, BLK), BF16),
            pltpu.VMEM((NZ, WIDTH, BLK), F32),
            pltpu.VMEM((BLK, WIDTH), F32),
            pltpu.VMEM((BLK, WIDTH), F32),
            pltpu.VMEM((NZ, WIDTH, BLK), BF16),
            pltpu.VMEM((2, BLK, WIDTH), BF16),
            pltpu.VMEM((2, BLK, WIDTH), BF16),
            pltpu.VMEM((BLK, WIDTH), BF16),
            pltpu.SMEM((KEY_BLOCKS * BUCKET,), jnp.int32),
            pltpu.SMEM((KEY_BLOCKS,), jnp.int32),
            pltpu.SMEM((KEY_BLOCKS * NZ,), jnp.int32),
            pltpu.SemaphoreType.DMA((2, 5)),
            pltpu.SemaphoreType.DMA((2, 2)),
            pltpu.SemaphoreType.DMA((2,)),
            pltpu.SemaphoreType.DMA((NZ,)),
        ],
        compiler_params=pltpu.CompilerParams(vmem_limit_bytes=48 << 20),
        name="used_pairs",
    )(pairs, counts, place, q_all, do_all, st_all, k_all, v_all)


REDUCE_COPIES = 38
ROW_STEP = 16


def reduce_kernel(
    dq_part, dk_part, dv_part,
    gq_out, gk_out, gv_out,
    dq_own, dq_in_up, dq_in_down, k_own, v_own, k_sib, v_sib,
    k_far_a, k_far_b, v_far_a, v_far_b, k_near_a, k_near_b, v_near_a, v_near_b,
    k_mid, v_mid, k_end_far_a, k_end_far_b, v_end_far_a, v_end_far_b,
    k_end_a, k_end_b, v_end_a, v_end_b,
    send_sems, recv_sems, local_sems,
):
    me = Place()
    x, y, z = me.x, me.y, me.z
    mine = pl.ds(pl.multiple_of(me.core * HALF, HALF), HALF)
    other = pl.ds(pl.multiple_of((1 - me.core) * HALF, HALF), HALF)
    every = slice(None)
    line = (2, 1, -1, 0)
    loads = {}
    for order, step in enumerate((4, -1, 1, -2, 2, -3, 3, 0)):
        loads["q", step] = pltpu.make_async_copy(
            dq_part.at[me.zs(step)], dq_own.at[me.zs(step)], local_sems.at[8 + order]
        )
    for order, step in enumerate(line):
        loads["k", step] = pltpu.make_async_copy(
            dk_part.at[me.ys(step), every, mine], k_own.at[me.ys(step)], local_sems.at[order]
        )
        loads["v", step] = pltpu.make_async_copy(
            dv_part.at[me.xs(step), every, mine], v_own.at[me.xs(step)], local_sems.at[4 + order]
        )
    for load in loads.values():
        load.start()
    me.greet()
    send = Sender(send_sems, recv_sems)
    up, down = me.over_z(1), me.over_z(-1)
    upper, lower = pl.ds(0, WIDTH // 2), pl.ds(WIDTH // 2, WIDTH // 2)

    loads["q", 4].wait()
    far = me.zs(4)
    arrive = {}
    arrive["up", 0, 1] = send(dq_own.at[far, upper], dq_in_up.at[0, upper], up)
    arrive["down", 1, 1] = send(dq_own.at[far, lower], dq_in_down.at[0, lower], down)

    sib = {}
    for step in line:
        sib["k", step] = send(dk_part.at[me.ys(step), every, other], k_sib.at[me.ys(step)], me.sibling)
        sib["v", step] = send(dv_part.at[me.xs(step), every, other], v_sib.at[me.xs(step)], me.sibling)

    def add_rows(total, terms, count):
        def one(index, carry):
            at = pl.ds(pl.multiple_of(index * ROW_STEP, ROW_STEP), ROW_STEP)
            value = terms[0][at, :].astype(F32)
            for term in terms[1:]:
                value = value + term[at, :].astype(F32)
            total[at, :] = value.astype(total.dtype)
            return carry

        lax.fori_loop(0, count // ROW_STEP, one, 0, unroll=4)

    def hop_q(direction, half, hop):
        side = upper if half == 0 else lower
        if direction == "up":
            step, inbox, device, sign = 4 - hop, dq_in_up, up, 1
        else:
            step, inbox, device, sign = hop - 4, dq_in_down, down, -1
        target = me.zs(step)
        key = (direction, half, hop)
        if key in arrive:
            arrive[key].wait_recv()
            add_rows(
                dq_own.at[target, side],
                [dq_own.at[target, side], inbox.at[hop - 1, side]],
                WIDTH // 2,
            )
        if step:
            arrive[direction, half, hop + 1] = send(
                dq_own.at[target, side], inbox.at[hop, side], device
            )

    for step in (-1, 1, -2, 2, -3, 3, 0):
        loads["q", step].wait()
    hop_q("up", 1, 1)
    hop_q("down", 0, 1)

    def join(name, own, other_core, step, place):
        loads[name, step].wait()
        sib[name, step].wait_recv()
        for row in range(4):
            add_rows(
                own.at[place, row], [own.at[place, row], other_core.at[place, row]], HALF
            )

    far_y, far_x = me.ys(2), me.xs(2)
    join("k", k_own, k_sib, 2, far_y)
    kf_a = send(k_own.at[far_y, pl.ds(0, 2)], k_far_a, me.over_y(1))
    kf_b = send(k_own.at[far_y, pl.ds(2, 2)], k_far_b, me.over_y(-1))
    join("v", v_own, v_sib, 2, far_x)
    vf_a = send(v_own.at[far_x, pl.ds(0, 2)], v_far_a, me.over_x(1))
    vf_b = send(v_own.at[far_x, pl.ds(2, 2)], v_far_b, me.over_x(-1))

    hop_q("up", 0, 1)
    hop_q("down", 1, 1)

    for step in (1, -1):
        join("k", k_own, k_sib, step, me.ys(step))
        join("v", v_own, v_sib, step, me.xs(step))
    hop_q("up", 1, 2)
    hop_q("down", 0, 2)

    def onward(own, place, base, inbox, arrival):
        arrival.wait_recv()
        for row in range(2):
            add_rows(
                own.at[place, base + row], [own.at[place, base + row], inbox.at[row]], HALF
            )

    onward(k_own, me.ys(1), 0, k_far_a, kf_a)
    kn_a = send(k_own.at[me.ys(1)], k_near_a, me.over_y(1))
    onward(v_own, me.xs(1), 0, v_far_a, vf_a)
    vn_a = send(v_own.at[me.xs(1)], v_near_a, me.over_x(1))
    onward(k_own, me.ys(-1), 2, k_far_b, kf_b)
    kn_b = send(k_own.at[me.ys(-1)], k_near_b, me.over_y(-1))
    onward(v_own, me.xs(-1), 2, v_far_b, vf_b)
    vn_b = send(v_own.at[me.xs(-1)], v_near_b, me.over_x(-1))
    hop_q("up", 0, 2)
    hop_q("down", 1, 2)
    join("k", k_own, k_sib, 0, y)
    join("v", v_own, v_sib, 0, x)
    hop_q("up", 1, 3)
    hop_q("down", 0, 3)
    hop_q("up", 0, 3)
    hop_q("down", 1, 3)

    def settle(own, place, near_a, near_b, arrivals, middle, row, far_place):
        at = row
        add_rows(
            middle.at[at],
            [own.at[place, at], near_a.at[at], near_b.at[at]],
            HALF,
        )

    for arrival in (kn_a, kn_b):
        arrival.wait_recv()
    for row in range(4):
        settle(k_own, y, k_near_a, k_near_b, None, k_mid, row, None)
    half_rows = (pl.ds(0, HALF // 2), pl.ds(HALF // 2, HALF // 2))
    ke_a = send(k_mid.at[far_x, half_rows[0]], k_end_far_a, me.over_x(1))
    ke_b = send(k_mid.at[far_x, half_rows[1]], k_end_far_b, me.over_x(-1))
    for arrival in (vn_a, vn_b):
        arrival.wait_recv()
    for row in range(4):
        settle(v_own, x, v_near_a, v_near_b, None, v_mid, row, None)
    ve_a = send(v_mid.at[far_y, half_rows[0]], v_end_far_a, me.over_y(1))
    ve_b = send(v_mid.at[far_y, half_rows[1]], v_end_far_b, me.over_y(-1))

    def last(middle, place, half, inbox, arrival, target, device):
        arrival.wait_recv()
        part = middle.at[place, half_rows[half]]
        add_rows(part, [part, inbox], HALF // 2)
        return send(middle.at[place], target, device)

    kz_a = last(k_mid, me.xs(1), 0, k_end_far_a, ke_a, k_end_a, me.over_x(1))
    kz_b = last(k_mid, me.xs(-1), 1, k_end_far_b, ke_b, k_end_b, me.over_x(-1))
    vz_a = last(v_mid, me.ys(1), 0, v_end_far_a, ve_a, v_end_a, me.over_y(1))
    vz_b = last(v_mid, me.ys(-1), 1, v_end_far_b, ve_b, v_end_b, me.over_y(-1))

    for direction in ("up", "down"):
        for half in range(2):
            arrive[direction, half, 4].wait_recv()
    for tile in range(WIDTH // 128):
        at = pl.ds(tile * 128, 128)
        value = (
            dq_own[z, at, :].astype(F32)
            + dq_in_up[3, at, :].astype(F32)
            + dq_in_down[3, at, :].astype(F32)
        )
        gq_out[:, at] = jnp.transpose(value).astype(BF16)

    for arrival in (kz_a, kz_b):
        arrival.wait_recv()
    add_rows(gk_out, [k_mid.at[x], k_end_a, k_end_b], HALF)
    for arrival in (vz_a, vz_b):
        arrival.wait_recv()
    add_rows(gv_out, [v_mid.at[y], v_end_a, v_end_b], HALF)
    send.finish()
    assert len(send.copies) == REDUCE_COPIES, len(send.copies)


def reduce_parts(dq_part, dk_part, dv_part):
    vmem = pl.BlockSpec(memory_space=pltpu.VMEM)
    line = pltpu.VMEM((4, 4, HALF, WIDTH), BF16)
    two = pltpu.VMEM((2, HALF, WIDTH), BF16)
    four = pltpu.VMEM((4, HALF, WIDTH), BF16)
    quarter = pltpu.VMEM((HALF // 2, WIDTH), BF16)
    one = pltpu.VMEM((HALF, WIDTH), BF16)
    return pl.pallas_call(
        reduce_kernel,
        out_shape=[
            jax.ShapeDtypeStruct((BLK, WIDTH), BF16),
            jax.ShapeDtypeStruct((HALF, WIDTH), BF16),
            jax.ShapeDtypeStruct((HALF, WIDTH), BF16),
        ],
        in_specs=[ANY] * 3,
        out_specs=[vmem] * 3,
        scratch_shapes=[
            pltpu.VMEM((NZ, WIDTH, BLK), BF16),
            pltpu.VMEM((4, WIDTH, BLK), BF16),
            pltpu.VMEM((4, WIDTH, BLK), BF16),
            line, line, line, line,
            two, two, two, two,
            four, four, four, four,
            four, four,
            quarter, quarter, quarter, quarter,
            one, one, one, one,
            pltpu.SemaphoreType.DMA((REDUCE_COPIES,)),
            pltpu.SemaphoreType.DMA((REDUCE_COPIES,)),
            pltpu.SemaphoreType.DMA((16,)),
        ],
        compiler_params=pltpu.CompilerParams(
            collective_id=1, has_side_effects=True, vmem_limit_bytes=48 << 20
        ),
        name="reduce_parts",
    )(dq_part, dk_part, dv_part)


def body(q, k, v, out, do, lse, block_pairs, counts):
    ka = lax.axis_index("ka")
    place = jnp.stack([ka // NZ, ka % NZ]).astype(jnp.int32)
    gathered = gather(q, do, k, v, out, lse)
    parts = pairs_over_blocks(block_pairs, counts, place, *gathered)
    return tuple(reduce_parts(*parts))


def solution(mesh):
    placed = (
        P(("pb", "ka"), None),
        P(("ka", "pb"), None),
        P(("ka", "pb"), None),
        P(("pb", "ka"), None),
        P(("pb", "ka"), None),
        P(None, ("pb", "ka")),
        P("pb", None, None, None),
        P("pb", None),
    )
    return jax.shard_map(
        body,
        mesh=mesh,
        in_specs=placed,
        out_specs=(P(("pb", "ka"), None), P(("ka", "pb"), None), P(("ka", "pb"), None)),
        check_vma=False,
    )
```

time: 1000 us -> 143 us (0.14)
  the two profiles are of different devices: /device:TPU:1 before, /device:TPU:168 now
where the time goes in v1:
time: 143 us; the launch traced here: 142 us
  Pallas kernels  127 us (89%)
  local copies, waits for them, and re-layouts  14.1 us (10%)
    pallas_call x1, Pallas kernels, reduce_parts(): pl.pallas_call(reduce_kernel, out_shape=[jax.ShapeDtypeStruct((BLK, WIDTH...  48.7 us
    pallas_call x1, Pallas kernels, gather(): pl.pallas_call(gather_kernel, out_shape=[jax.ShapeDtypeStruct((NZ, BLK, W...  46.3 us
    pallas_call x1, Pallas kernels, pairs_over_blocks(): pl.pallas_call(pair_kernel, out_shape=[jax.ShapeDtypeStruct((NZ, WIDTH, B...  32.4 us
    unnamed x24, local copies, waits for them, and re-layouts  14.1 us

profile of v1, /device:TPU:168, one launch (start us, length us, event | category | flops | bytes accessed | tf_op | source)
XLA Modules:
  0.0 142.2 jit_solution(4958481061004781019)
XLA Ops:
  0.7 0.1 pad_add_fusion.place
  0.7 0.8 copy.11.pairs
  1.5 0.0 copy-start.3
  1.5 1.0 copy-done.3
  2.5 0.0 copy-start.4
  2.5 0.9 copy-done.4
  3.4 0.0 copy-start.5
  3.5 0.9 copy-done.5
  4.4 0.0 copy-start.6
  4.4 0.9 copy-done.6
  5.3 0.0 copy-start.7
  5.3 0.9 copy-done.7
  6.2 0.7 copy-done.8
  6.9 46.3 %gather_blocks.1 = (bf16[8,128,1024]{2,1,0:T(8,128)(2,1)S(1)}, bf16[8,128,1024]{2,1,0:T(8,128)(2,1)S(1)}, f32[8,32,128]{2,1,0:T(8,128)S(1)}, bf16[4,4,128,1024]{...) custom-call(bf16[128,1024]{1,0:T(8,128)(2,1)S(1)} %copy-done.3, bf16[128,1024]{1,0:T(8,128)(2,1)S(1)} %copy-done.4, ...), custom_call_target="tpu_custom_call" | custom-call | tf_op jit(solution)/shard_map/gather_blocks/pallas_call | solution.py:238
  53.2 0.0 copy-start
  53.2 1.9 %copy-done = bf16[4,4,128,1024]{3,2,1,0:T(8,128)(2,1)} copy-done((bf16[4,4,128,1024]{3,2,1,0:T(8,128)(2,1)}, bf16[4,4,128,1024]{3,2,1,0:T(8,128)(2,1)S(1)}, u32[]{:S(2)}) %copy-start) | copy-done | bytes 4194328
  55.2 2.0 %copy-done.1 = bf16[4,4,128,1024]{3,2,1,0:T(8,128)(2,1)} copy-done((bf16[4,4,128,1024]{3,2,1,0:T(8,128)(2,1)}, bf16[4,4,128,1024]{3,2,1,0:T(8,128)(2,1)S(1)}, u32[]{:S(2)}) %copy-start.1) | copy-done | bytes 4194328
  57.1 1.3 copy-done.2
  58.4 0.7 copy-done.9
  59.1 32.4 %used_pairs.1 = (bf16[8,1024,128]{2,1,0:T(8,128)(2,1)S(1)}, bf16[4,4,128,1024]{3,2,1,0:T(8,128)(2,1)}, bf16[4,4,128,1024]{3,2,1,0:T(8,128)(2,1)}) custom-call(s32[1,32,2,24]{3,2,1,0:T(2,128)S(1)} %copy.11.pairs, s32[1,32]{1,0:T(1,128)S(1)} %copy-done.9, s32[2]{0:T(128)S(1)} %pad_add_fusion.place, bf16[8,128,1024]{2,1,0:T(8,128)(2,1)S(1)} %get-tuple-element.11.q_all, ...), custom_call_target="tpu_custom_call" | custom-call | tf_op jit(solution)/shard_map/used_pairs/pallas_call | solution.py:446
  91.5 48.7 %reduce_parts.1 = (bf16[128,1024]{1,0:T(8,128)(2,1)S(1)}, bf16[64,1024]{1,0:T(8,128)(2,1)S(1)}, bf16[64,1024]{1,0:T(8,128)(2,1)S(1)}) custom-call(bf16[8,1024,128]{2,1,0:T(8,128)(2,1)S(1)} %get-tuple-element.16.dq_part, bf16[4,4,128,1024]{3,2,1,0:T(8,128)(2,1)} %get-tuple-element.17.dk_part, bf16[4,4,128,1024]{3,2,1,0:T(8,128)(2,1)} %get-tuple-element.18.dv_part), custom_call_target="tpu_custom_call" | custom-call | tf_op jit(solution)/shard_map/reduce_parts/pallas_call | solution.py:678
  140.2 0.7 copy.15
  140.9 0.7 copy.16
  141.6 0.7 copy.17
  (4 shorter events, 0.0 us)
Async XLA Ops:
  1.5 1.0 copy-start.3
  2.5 0.9 copy-start.4
  3.4 0.9 copy-start.5
  4.4 0.9 copy-start.6
  5.3 0.9 copy-start.7
  6.2 0.7 copy-start.8
  53.2 2.0 %copy-start = (bf16[4,4,128,1024]{3,2,1,0:T(8,128)(2,1)}, bf16[4,4,128,1024]{3,2,1,0:T(8,128)(2,1)S(1)}, u32[]{:S(2)}) copy-start(bf16[4,4,128,1024]{3,2,1,0:T(8,128)(2,1)S(1)} %get-tuple-element.14.k_all) | copy-start | bytes 12582916
  55.2 2.0 %copy-start.1 = (bf16[4,4,128,1024]{3,2,1,0:T(8,128)(2,1)}, bf16[4,4,128,1024]{3,2,1,0:T(8,128)(2,1)S(1)}, u32[]{:S(2)}) copy-start(bf16[4,4,128,1024]{3,2,1,0:T(8,128)(2,1)S(1)} %get-tuple-element.15.v_all) | copy-start | bytes 12582916
  57.1 1.3 copy-start.2
  58.4 0.7 copy-start.9

commit v2 on v1

v2 whole, which is shorter than its diff:
```python
import jax
import jax.numpy as jnp
from jax import lax
from jax.experimental import pallas as pl
from jax.experimental.pallas import tpu as pltpu
from jax.sharding import PartitionSpec as P

NX, NY, NZ, CORES = 4, 4, 8, 2
HEADS = 16
OWN_HEADS = HEADS // CORES
BLK = 128
HALF = BLK // 2
WIDTH = 1024
COLS = WIDTH // CORES
HEAD_PAIRS = COLS // 128
SLOTS = 24
KEY_SHARDS = NX * NZ
QUERY_BLOCKS = NZ * CORES
KEY_BLOCKS = NX * NY
BUCKET = 32
SCALE = 64**-0.5
LOG2E = 1.4426950408889634
VMEM_LIMIT = 60 << 20
MESH = pl.DeviceIdType.MESH
ANY = pl.BlockSpec(memory_space=pl.ANY)
F32 = jnp.float32
BF16 = jnp.bfloat16


class Place:
    def __init__(self):
        pb = lax.axis_index("pb")
        ka = lax.axis_index("ka")
        self.y = lax.div(pb, CORES)
        self.core = lax.rem(pb, CORES)
        self.x = lax.div(ka, NZ)
        self.z = lax.rem(ka, NZ)
        self.sibling = (self.y * CORES + 1 - self.core, ka)

    def over_x(self, step):
        return (self.y * CORES + self.core, self.xs(step) * NZ + self.z)

    def over_y(self, step):
        return (self.ys(step) * CORES + self.core, self.x * NZ + self.z)

    def over_z(self, step):
        return (self.y * CORES + self.core, self.x * NZ + self.zs(step))

    def xs(self, step):
        return lax.rem(self.x + step + NX, NX)

    def ys(self, step):
        return lax.rem(self.y + step + NY, NY)

    def zs(self, step):
        return lax.rem(self.z + step + NZ, NZ)

    def greet(self):
        barrier = pltpu.get_barrier_semaphore()
        neighbours = [self.sibling]
        for step in (1, -1):
            neighbours += [self.over_x(step), self.over_y(step), self.over_z(step)]
        for neighbour in neighbours:
            pl.semaphore_signal(barrier, inc=1, device_id=neighbour, device_id_type=MESH)
        pl.semaphore_wait(barrier, len(neighbours))


class Sender:
    def __init__(self, send_sems, recv_sems):
        self.send_sems = send_sems
        self.recv_sems = recv_sems
        self.copies = []

    def __call__(self, source, target, device):
        index = len(self.copies)
        copy = pltpu.make_async_remote_copy(
            src_ref=source,
            dst_ref=target,
            send_sem=self.send_sems.at[index],
            recv_sem=self.recv_sems.at[index],
            device_id=device,
            device_id_type=MESH,
        )
        copy.start()
        self.copies.append(copy)
        return copy

    def finish(self):
        for copy in self.copies:
            copy.wait_send()


def half_of(core, size):
    return pl.ds(pl.multiple_of(core * size, size), size)


GATHER_COPIES = 46


def gather_kernel(
    q_ref, do_ref, k_ref, v_ref, out_ref, lse_ref, list_ref, count_ref,
    q_all, do_all, st_all, k_all, v_all, list_all, count_all,
    do_buf, out_buf, lse_buf, st_buf, send_sems, recv_sems, local_sems,
):
    me = Place()
    x, y, z, core = me.x, me.y, me.z, me.core
    every = slice(None)
    rows = half_of(core, HALF)
    mine = half_of(core, COLS)
    theirs = half_of(1 - core, COLS)

    owns = [
        pltpu.make_async_copy(q_ref.at[every, mine], q_all.at[z, core], local_sems.at[0]),
        pltpu.make_async_copy(do_ref.at[every, mine], do_all.at[z, core], local_sems.at[1]),
        pltpu.make_async_copy(k_ref.at[every, mine], k_all.at[y, x, rows], local_sems.at[2]),
        pltpu.make_async_copy(v_ref.at[every, mine], v_all.at[x, y, rows], local_sems.at[3]),
        pltpu.make_async_copy(list_ref, list_all.at[core], local_sems.at[4]),
        pltpu.make_async_copy(count_ref, count_all.at[core], local_sems.at[8]),
    ]
    for own in owns:
        own.start()
    loads = [
        pltpu.make_async_copy(do_ref, do_buf, local_sems.at[5]),
        pltpu.make_async_copy(out_ref, out_buf, local_sems.at[6]),
        pltpu.make_async_copy(lse_ref, lse_buf, local_sems.at[7]),
    ]
    for load in loads:
        load.start()
    me.greet()
    send = Sender(send_sems, recv_sems)
    up, down = me.over_z(1), me.over_z(-1)

    k_swap = send(k_ref.at[every, theirs], k_all.at[y, x, rows], me.sibling)
    v_swap = send(v_ref.at[every, theirs], v_all.at[x, y, rows], me.sibling)
    q_swap = send(q_ref.at[every, theirs], q_all.at[z, core], me.sibling)
    do_swap = send(do_ref.at[every, theirs], do_all.at[z, core], me.sibling)
    list_swap = send(list_ref, list_all.at[core], me.sibling)
    count_swap = send(count_ref, count_all.at[core], me.sibling)

    q_first = [send(q_ref.at[every, mine], q_all.at[z, core], up)]
    do_first = [send(do_ref.at[every, mine], do_all.at[z, core], down)]
    for own in owns:
        own.wait()
    k_swap.wait_recv()
    k_right = send(k_all.at[y, x], k_all.at[y, x], me.over_x(1))
    k_left = send(k_all.at[y, x], k_all.at[y, x], me.over_x(-1))
    v_swap.wait_recv()
    v_right = send(v_all.at[x, y], v_all.at[x, y], me.over_y(1))
    v_left = send(v_all.at[x, y], v_all.at[x, y], me.over_y(-1))
    q_swap.wait_recv()
    other_q = q_all.at[z, 1 - core]
    q_first.append(send(other_q, other_q, up))
    do_swap.wait_recv()
    other_do = do_all.at[z, 1 - core]
    do_first.append(send(other_do, other_do, down))
    do_up = [send(do_all.at[z], do_all.at[z], up)]
    q_down = [send(q_all.at[z], q_all.at[z], down)]

    for load in loads:
        load.wait()
    products = do_buf[...].astype(F32) * out_buf[...].astype(F32)
    high = products.astype(BF16)
    low = (products - high.astype(F32)).astype(BF16)
    head = lax.broadcasted_iota(jnp.int32, (HEADS, WIDTH), 0) * 64
    feature = lax.broadcasted_iota(jnp.int32, (HEADS, WIDTH), 1)
    member = jnp.where((feature >= head) & (feature < head + 64), 1.0, 0.0).astype(BF16)
    over_features = (((1,), (1,)), ((), ()))
    delta = lax.dot_general(member, high, over_features, preferred_element_type=F32)
    delta = delta + lax.dot_general(member, low, over_features, preferred_element_type=F32)
    for side in range(CORES):
        heads = slice(side * OWN_HEADS, side * OWN_HEADS + OWN_HEADS)
        st_buf[side, 0:OWN_HEADS, :] = lse_buf[heads, :] * LOG2E
        st_buf[side, OWN_HEADS : 2 * OWN_HEADS, :] = delta[heads, :]
    st_own = pltpu.make_async_copy(st_buf.at[core], st_all.at[z, core], local_sems.at[0])
    st_own.start()
    st_swap = send(st_buf.at[1 - core], st_all.at[z, core], me.sibling)

    upper, lower = pl.ds(0, HALF), pl.ds(HALF, HALF)
    k_right.wait_recv()
    k_far = [k_all.at[y, me.xs(-1), upper]]
    k_far = [send(k_far[0], k_far[0], me.over_x(1))]
    v_right.wait_recv()
    v_part = v_all.at[x, me.ys(-1), upper]
    v_far = [send(v_part, v_part, me.over_y(1))]
    k_left.wait_recv()
    k_part = k_all.at[y, me.xs(1), lower]
    k_far.append(send(k_part, k_part, me.over_x(-1)))
    v_left.wait_recv()
    v_part = v_all.at[x, me.ys(1), lower]
    v_far.append(send(v_part, v_part, me.over_y(-1)))

    st_swap.wait_recv()
    st_own.wait()
    st_up = [send(st_all.at[z], st_all.at[z], up)]
    st_down = [send(st_all.at[z], st_all.at[z], down)]

    for copy in k_far:
        copy.wait_recv()
    k_right = send(k_all.at[y], k_all.at[y], me.over_y(1))
    k_left = send(k_all.at[y], k_all.at[y], me.over_y(-1))
    for copy in v_far:
        copy.wait_recv()
    v_right = send(v_all.at[x], v_all.at[x], me.over_x(1))
    v_left = send(v_all.at[x], v_all.at[x], me.over_x(-1))

    def forward_up(hop, blocks, copies):
        for copy in copies[hop - 1] if isinstance(copies[hop - 1], list) else [copies[hop - 1]]:
            copy.wait_recv()
        block = blocks.at[me.zs(-hop)]
        copies.append(send(block, block, up))

    def forward_down(hop, blocks, copies):
        for copy in copies[hop - 1] if isinstance(copies[hop - 1], list) else [copies[hop - 1]]:
            copy.wait_recv()
        block = blocks.at[me.zs(hop)]
        copies.append(send(block, block, down))

    q_up, do_down = [q_first], [do_first]
    forward_up(1, q_all, q_up)
    forward_down(1, do_all, do_down)
    forward_up(1, do_all, do_up)
    forward_down(1, q_all, q_down)
    forward_up(1, st_all, st_up)
    forward_down(1, st_all, st_down)

    def across(blocks, start, low, device):
        part = blocks.at[start, pl.ds(low, 2)]
        return send(part, part, device)

    k_right.wait_recv()
    k_far = [across(k_all, me.ys(-1), 0, me.over_y(1))]
    v_right.wait_recv()
    v_far = [across(v_all, me.xs(-1), 0, me.over_x(1))]
    k_left.wait_recv()
    k_far.append(across(k_all, me.ys(1), 2, me.over_y(-1)))
    v_left.wait_recv()
    v_far.append(across(v_all, me.xs(1), 2, me.over_x(-1)))

    forward_up(2, q_all, q_up)
    forward_down(2, do_all, do_down)
    forward_up(2, do_all, do_up)
    forward_down(2, q_all, q_down)
    forward_up(2, st_all, st_up)
    forward_down(2, st_all, st_down)

    forward_up(3, q_all, q_up)
    forward_down(3, do_all, do_down)
    forward_up(3, st_all, st_up)
    for copy in k_far + v_far:
        copy.wait_recv()
    do_up[2].wait_recv()
    q_down[2].wait_recv()
    st_down[2].wait_recv()
    list_swap.wait_recv()
    count_swap.wait_recv()
    q_up[3].wait_recv()
    do_down[3].wait_recv()
    st_up[3].wait_recv()
    send.finish()
    assert len(send.copies) == GATHER_COPIES, len(send.copies)


def gather(q, do, k, v, out, lse, lists, counts):
    return pl.pallas_call(
        gather_kernel,
        out_shape=[
            jax.ShapeDtypeStruct((NZ, CORES, BLK, COLS), BF16),
            jax.ShapeDtypeStruct((NZ, CORES, BLK, COLS), BF16),
            jax.ShapeDtypeStruct((NZ, CORES, 2 * OWN_HEADS, BLK), F32),
            jax.ShapeDtypeStruct((NY, NX, BLK, COLS), BF16),
            jax.ShapeDtypeStruct((NX, NY, BLK, COLS), BF16),
            jax.ShapeDtypeStruct((CORES, 2 * SLOTS, KEY_SHARDS), jnp.int32),
            jax.ShapeDtypeStruct((CORES, 1, KEY_SHARDS), jnp.int32),
        ],
        in_specs=[ANY] * 8,
        out_specs=[ANY] * 7,
        scratch_shapes=[
            pltpu.VMEM((BLK, WIDTH), BF16),
            pltpu.VMEM((BLK, WIDTH), BF16),
            pltpu.VMEM((HEADS, BLK), F32),
            pltpu.VMEM((CORES, 2 * OWN_HEADS, BLK), F32),
            pltpu.SemaphoreType.DMA((GATHER_COPIES,)),
            pltpu.SemaphoreType.DMA((GATHER_COPIES,)),
            pltpu.SemaphoreType.DMA((9,)),
        ],
        compiler_params=pltpu.CompilerParams(
            collective_id=0, has_side_effects=True, vmem_limit_bytes=VMEM_LIMIT
        ),
        name="gather_blocks",
    )(q, do, k, v, out, lse, lists, counts)


def pair_kernel(
    lists, counts, place, q_all, do_all, st_all, k_all, v_all,
    dq_out, dk_out, dv_out,
    q_buf, do_buf, st_buf, k_buf, v_buf, k_turned, dq_sum, dk_sum, dv_sum, dq_stage, dk_stage, dv_stage, zeros,
    listed, filled, flat, in_sems, out_sems, zero_sems, dq_sems,
):
    x = place[0]
    z = place[1]
    for block in range(KEY_BLOCKS):
        filled[block] = 0
    for owner in range(CORES):
        for column in range(NX):
            shard = column * NZ + z

            def enlist(slot, carry, owner=owner, column=column, shard=shard):
                query = lists[owner, slot, shard]
                block = lists[owner, SLOTS + slot, shard] * NX + column
                have = filled[block]
                where = lax.rem(query, NZ) * CORES + owner
                listed[block * BUCKET + have] = block * QUERY_BLOCKS + where
                filled[block] = have + jnp.where(lax.div(query, NZ) == x, 1, 0)
                return carry

            lax.fori_loop(0, counts[owner, 0, shard], enlist, 0)
    zeros[...] = jnp.zeros_like(zeros)
    total = jnp.int32(0)
    for block in range(KEY_BLOCKS):

        def append(slot, position, block=block):
            flat[position] = listed[block * BUCKET + slot]
            return position + 1

        total = lax.fori_loop(0, filled[block], append, total)
        up, across = divmod(block, NX)

        @pl.when(filled[block] == 0)
        def _(up=up, across=across):
            pltpu.make_async_copy(zeros, dk_out.at[up, across], zero_sems.at[0]).start()
            pltpu.make_async_copy(zeros, dv_out.at[across, up], zero_sems.at[1]).start()

    def fetches(index, slot):
        entry = flat[index]
        block = lax.div(entry, QUERY_BLOCKS)
        up, across = lax.div(block, NX), lax.rem(block, NX)
        query = lax.rem(entry, QUERY_BLOCKS)
        return [
            pltpu.make_async_copy(k_all.at[up, across], k_buf.at[slot], in_sems.at[slot, 0]),
            pltpu.make_async_copy(q_all.at[query], q_buf.at[slot], in_sems.at[slot, 1]),
            pltpu.make_async_copy(st_all.at[query], st_buf.at[slot], in_sems.at[slot, 2]),
            pltpu.make_async_copy(v_all.at[across, up], v_buf.at[slot], in_sems.at[slot, 3]),
            pltpu.make_async_copy(do_all.at[query], do_buf.at[slot], in_sems.at[slot, 4]),
        ]

    @pl.when(total > 0)
    def _():
        for fetch in fetches(0, 0):
            fetch.start()

    def clear(query, carry):
        dq_sum[query] = jnp.zeros((COLS, BLK), F32)
        return carry

    lax.fori_loop(0, QUERY_BLOCKS, clear, 0)

    lane = lax.broadcasted_iota(jnp.int32, (1, 128), 1)
    first_half = jnp.where(lane < 64, 1.0, 0.0).astype(BF16)
    second_half = jnp.where(lane < 64, 0.0, 1.0).astype(BF16)
    nt = (((1,), (1,)), ((), ()))
    nn = (((1,), (0,)), ((), ()))

    def flush_copies(slot, block):
        up, across = lax.div(block, NX), lax.rem(block, NX)
        return [
            pltpu.make_async_copy(dk_stage.at[slot], dk_out.at[up, across], out_sems.at[slot, 0]),
            pltpu.make_async_copy(dv_stage.at[slot], dv_out.at[across, up], out_sems.at[slot, 1]),
        ]

    def step(index, flushed):
        slot = lax.rem(index, 2)
        block = lax.div(flat[index], QUERY_BLOCKS)
        query = lax.rem(flat[index], QUERY_BLOCKS)
        before = jnp.where(index > 0, lax.div(flat[jnp.maximum(index - 1, 0)], QUERY_BLOCKS), -1)
        after = jnp.where(
            index + 1 < total, lax.div(flat[jnp.minimum(index + 1, total - 1)], QUERY_BLOCKS), -1
        )

        @pl.when(index + 1 < total)
        def _():
            for fetch in fetches(index + 1, 1 - slot):
                fetch.start()

        for fetch in fetches(index, slot):
            fetch.wait()

        @pl.when(before != block)
        def _():
            dk_sum[...] = jnp.zeros_like(dk_sum)
            dv_sum[...] = jnp.zeros_like(dv_sum)
            for pair in range(HEAD_PAIRS):
                lanes = slice(pair * 128, pair * 128 + 128)
                turned = jnp.transpose(k_buf[slot, :, lanes].astype(F32)).astype(BF16)
                k_turned[lanes, :] = turned

        for pair in range(HEAD_PAIRS):
            lanes = slice(pair * 128, pair * 128 + 128)
            keys = k_buf[slot, :, lanes]
            values = v_buf[slot, :, lanes]
            queries = q_buf[slot, :, lanes]
            douts = do_buf[slot, :, lanes]
            q_two = jnp.concatenate([queries * first_half, queries * second_half], axis=0)
            do_two = jnp.concatenate([douts * first_half, douts * second_half], axis=0)
            scores = lax.dot_general(keys, q_two, nt, preferred_element_type=F32)
            dprob = lax.dot_general(values, do_two, nt, preferred_element_type=F32)
            probs, dscores = [], []
            for side in range(2):
                head = 2 * pair + side
                cut = slice(side * BLK, side * BLK + BLK)
                lse = st_buf[slot, head : head + 1, :]
                delta = st_buf[slot, OWN_HEADS + head : OWN_HEADS + head + 1, :]
                prob = jnp.exp2(scores[:, cut] * (SCALE * LOG2E) - lse)
                probs.append(prob.astype(BF16))
                dscores.append((prob * (dprob[:, cut] - delta)).astype(BF16))
            dv_sum[:, lanes] += lax.dot_general(
                jnp.concatenate(probs, axis=1), do_two, nn, preferred_element_type=F32
            )
            dk_sum[:, lanes] += lax.dot_general(
                jnp.concatenate(dscores, axis=1), q_two, nn, preferred_element_type=F32
            )
            turned = k_turned[lanes, :]
            for side in range(2):
                low = pair * 128 + side * 64
                dq_sum[query, low : low + 64, :] += lax.dot_general(
                    turned[side * 64 : side * 64 + 64], dscores[side], nn, preferred_element_type=F32
                )

        @pl.when(after != block)
        def _():
            stage = lax.rem(flushed, 2)

            @pl.when(flushed >= 2)
            def _():
                for copy in flush_copies(stage, block):
                    copy.wait()

            dk_stage[stage] = (dk_sum[...] * SCALE).astype(BF16)
            dv_stage[stage] = dv_sum[...].astype(BF16)
            for copy in flush_copies(stage, block):
                copy.start()

        return flushed + jnp.where(after != block, 1, 0)

    flushed = lax.fori_loop(0, total, step, 0)

    def turn_in(query, carry):
        dq_stage[query] = (dq_sum[query] * SCALE).astype(BF16)
        pltpu.make_async_copy(dq_stage.at[query], dq_out.at[query], dq_sems.at[query]).start()
        return carry

    lax.fori_loop(0, QUERY_BLOCKS, turn_in, 0)
    for slot in range(2):

        @pl.when(flushed > slot)
        def _(slot=slot):
            for copy in flush_copies(slot, 0):
                copy.wait()

    for block in range(KEY_BLOCKS):
        up, across = divmod(block, NX)

        @pl.when(filled[block] == 0)
        def _(up=up, across=across):
            pltpu.make_async_copy(zeros, dk_out.at[up, across], zero_sems.at[0]).wait()
            pltpu.make_async_copy(zeros, dv_out.at[across, up], zero_sems.at[1]).wait()

    def finish(query, carry):
        pltpu.make_async_copy(dq_stage.at[query], dq_out.at[query], dq_sems.at[query]).wait()
        return carry

    lax.fori_loop(0, QUERY_BLOCKS, finish, 0)


def pairs_over_blocks(q_all, do_all, st_all, k_all, v_all, lists, counts, place):
    smem = pl.BlockSpec(memory_space=pltpu.SMEM)
    block_pair = pltpu.VMEM((2, BLK, COLS), BF16)
    return pl.pallas_call(
        pair_kernel,
        out_shape=[
            jax.ShapeDtypeStruct((QUERY_BLOCKS, COLS, BLK), BF16),
            jax.ShapeDtypeStruct((NY, NX, BLK, COLS), BF16),
            jax.ShapeDtypeStruct((NX, NY, BLK, COLS), BF16),
        ],
        in_specs=[smem] * 3 + [ANY] * 5,
        out_specs=[ANY] * 3,
        scratch_shapes=[
            block_pair,
            block_pair,
            pltpu.VMEM((2, 2 * OWN_HEADS, BLK), F32),
            block_pair,
            block_pair,
            pltpu.VMEM((COLS, BLK), BF16),
            pltpu.VMEM((QUERY_BLOCKS, COLS, BLK), F32),
            pltpu.VMEM((BLK, COLS), F32),
            pltpu.VMEM((BLK, COLS), F32),
            pltpu.VMEM((QUERY_BLOCKS, COLS, BLK), BF16),
            block_pair,
            block_pair,
            pltpu.VMEM((BLK, COLS), BF16),
            pltpu.SMEM((KEY_BLOCKS * BUCKET,), jnp.int32),
            pltpu.SMEM((KEY_BLOCKS,), jnp.int32),
            pltpu.SMEM((KEY_BLOCKS * QUERY_BLOCKS,), jnp.int32),
            pltpu.SemaphoreType.DMA((2, 5)),
            pltpu.SemaphoreType.DMA((2, 2)),
            pltpu.SemaphoreType.DMA((2,)),
            pltpu.SemaphoreType.DMA((QUERY_BLOCKS,)),
        ],
        compiler_params=pltpu.CompilerParams(vmem_limit_bytes=VMEM_LIMIT),
        name="used_pairs",
    )(
        lists,
        counts,
        place,
        q_all.reshape(QUERY_BLOCKS, BLK, COLS),
        do_all.reshape(QUERY_BLOCKS, BLK, COLS),
        st_all.reshape(QUERY_BLOCKS, 2 * OWN_HEADS, BLK),
        k_all,
        v_all,
    )


REDUCE_COPIES = 33
ROW_STEP = 16


def reduce_kernel(
    dq_part, dk_part, dv_part,
    gq_out, gk_out, gv_out,
    dq_own, dq_in_up, dq_in_down, k_own, v_own,
    k_far_a, k_far_b, v_far_a, v_far_b, k_near_a, k_near_b, v_near_a, v_near_b,
    k_mid, v_mid, k_end_far_a, k_end_far_b, v_end_far_a, v_end_far_b,
    k_end_a, k_end_b, v_end_a, v_end_b, gq_buf, gk_buf, gv_buf,
    send_sems, recv_sems, local_sems,
):
    me = Place()
    x, y, z, core = me.x, me.y, me.z, me.core
    every = slice(None)
    loads = {}
    for order, step in enumerate((3, -3, 2, -2, 1, -1, 0)):
        loads["q", step] = pltpu.make_async_copy(
            dq_part.at[me.zs(step)], dq_own.at[me.zs(step)], local_sems.at[order]
        )
    for order, step in enumerate((1, -1, 0)):
        loads["k", step] = pltpu.make_async_copy(
            dk_part.at[me.ys(step)], k_own.at[me.ys(step)], local_sems.at[7 + order]
        )
        loads["v", step] = pltpu.make_async_copy(
            dv_part.at[me.xs(step)], v_own.at[me.xs(step)], local_sems.at[10 + order]
        )
    for load in loads.values():
        load.start()
    me.greet()
    send = Sender(send_sems, recv_sems)
    up, down = me.over_z(1), me.over_z(-1)

    def add_rows(total, terms, count):
        def one(index, carry):
            at = pl.ds(pl.multiple_of(index * ROW_STEP, ROW_STEP), ROW_STEP)
            value = terms[0][at, :].astype(F32)
            for term in terms[1:]:
                value = value + term[at, :].astype(F32)
            total[at, :] = value.astype(total.dtype)
            return carry

        lax.fori_loop(0, count // ROW_STEP, one, 0, unroll=4)

    far = me.zs(4)
    arrive = {
        ("up", 0, 1): send(dq_part.at[far, 0], dq_in_up.at[0, 0], up),
        ("down", 1, 1): send(dq_part.at[far, 1], dq_in_down.at[0, 1], down),
    }
    far_y, far_x = me.ys(2), me.xs(2)
    kf_a = send(dk_part.at[far_y, pl.ds(0, 2)], k_far_a, me.over_y(1))
    kf_b = send(dk_part.at[far_y, pl.ds(2, 2)], k_far_b, me.over_y(-1))
    vf_a = send(dv_part.at[far_x, pl.ds(0, 2)], v_far_a, me.over_x(1))
    vf_b = send(dv_part.at[far_x, pl.ds(2, 2)], v_far_b, me.over_x(-1))
    arrive["up", 1, 2] = send(dq_part.at[me.zs(3), 1], dq_in_up.at[1, 1], up)
    arrive["down", 0, 2] = send(dq_part.at[me.zs(-3), 0], dq_in_down.at[1, 0], down)

    def hop_q(direction, shard, hop):
        if direction == "up":
            step, inbox, device = 4 - hop, dq_in_up, up
        else:
            step, inbox, device = hop - 4, dq_in_down, down
        own = dq_own.at[me.zs(step), shard]
        arrive[direction, shard, hop].wait_recv()
        add_rows(own, [own, inbox.at[hop - 1, shard]], COLS)
        arrive[direction, shard, hop + 1] = send(own, inbox.at[hop, shard], device)

    for load in loads.values():
        load.wait()
    hop_q("up", 0, 1)
    hop_q("down", 1, 1)

    def onward(own, place, base, inbox, arrival):
        arrival.wait_recv()
        for row in range(2):
            part = own.at[place, base + row]
            add_rows(part, [part, inbox.at[row]], BLK)

    onward(k_own, me.ys(1), 0, k_far_a, kf_a)
    kn_a = send(k_own.at[me.ys(1)], k_near_a, me.over_y(1))
    onward(v_own, me.xs(1), 0, v_far_a, vf_a)
    vn_a = send(v_own.at[me.xs(1)], v_near_a, me.over_x(1))
    onward(k_own, me.ys(-1), 2, k_far_b, kf_b)
    kn_b = send(k_own.at[me.ys(-1)], k_near_b, me.over_y(-1))
    onward(v_own, me.xs(-1), 2, v_far_b, vf_b)
    vn_b = send(v_own.at[me.xs(-1)], v_near_b, me.over_x(-1))
    hop_q("up", 1, 2)
    hop_q("down", 0, 2)
    hop_q("up", 0, 2)
    hop_q("down", 1, 2)
    hop_q("up", 1, 3)
    hop_q("down", 0, 3)
    hop_q("up", 0, 3)
    hop_q("down", 1, 3)

    for arrival in (kn_a, kn_b):
        arrival.wait_recv()
    for row in range(4):
        add_rows(k_mid.at[row], [k_own.at[y, row], k_near_a.at[row], k_near_b.at[row]], BLK)
    half_rows = (pl.ds(0, HALF), pl.ds(HALF, HALF))
    ke_a = send(k_mid.at[far_x, half_rows[0]], k_end_far_a, me.over_x(1))
    ke_b = send(k_mid.at[far_x, half_rows[1]], k_end_far_b, me.over_x(-1))
    for arrival in (vn_a, vn_b):
        arrival.wait_recv()
    for row in range(4):
        add_rows(v_mid.at[row], [v_own.at[x, row], v_near_a.at[row], v_near_b.at[row]], BLK)
    ve_a = send(v_mid.at[far_y, half_rows[0]], v_end_far_a, me.over_y(1))
    ve_b = send(v_mid.at[far_y, half_rows[1]], v_end_far_b, me.over_y(-1))

    def last(middle, place, half, inbox, arrival, target, device):
        arrival.wait_recv()
        part = middle.at[place, half_rows[half]]
        add_rows(part, [part, inbox], HALF)
        return send(middle.at[place], target, device)

    kz_a = last(k_mid, me.xs(1), 0, k_end_far_a, ke_a, k_end_a, me.over_x(1))
    kz_b = last(k_mid, me.xs(-1), 1, k_end_far_b, ke_b, k_end_b, me.over_x(-1))
    vz_a = last(v_mid, me.ys(1), 0, v_end_far_a, ve_a, v_end_a, me.over_y(1))
    vz_b = last(v_mid, me.ys(-1), 1, v_end_far_b, ve_b, v_end_b, me.over_y(-1))

    mine = half_of(core, COLS)
    swaps, stores = [], []
    for direction in ("up", "down"):
        for shard in range(CORES):
            arrive[direction, shard, 4].wait_recv()
    for shard in range(CORES):
        for tile in range(COLS // 128):
            at = pl.ds(tile * 128, 128)
            value = (
                dq_own[z, shard, at, :].astype(F32)
                + dq_in_up[3, shard, at, :].astype(F32)
                + dq_in_down[3, shard, at, :].astype(F32)
            )
            gq_buf[shard, :, at] = jnp.transpose(value).astype(BF16)
    swaps.append(send(gq_buf.at[1 - core], gq_out.at[every, mine], me.sibling))
    stores.append(pltpu.make_async_copy(gq_buf.at[core], gq_out.at[every, mine], local_sems.at[0]))
    stores[-1].start()

    own_rows, other_rows = half_of(core, HALF), half_of(1 - core, HALF)
    for arrival in (kz_a, kz_b):
        arrival.wait_recv()
    add_rows(gk_buf, [k_mid.at[x], k_end_a, k_end_b], BLK)
    swaps.append(send(gk_buf.at[other_rows], gk_out.at[every, mine], me.sibling))
    stores.append(pltpu.make_async_copy(gk_buf.at[own_rows], gk_out.at[every, mine], local_sems.at[1]))
    stores[-1].start()
    for arrival in (vz_a, vz_b):
        arrival.wait_recv()
    add_rows(gv_buf, [v_mid.at[y], v_end_a, v_end_b], BLK)
    swaps.append(send(gv_buf.at[other_rows], gv_out.at[every, mine], me.sibling))
    stores.append(pltpu.make_async_copy(gv_buf.at[own_rows], gv_out.at[every, mine], local_sems.at[2]))
    stores[-1].start()
    for store in stores:
        store.wait()
    for swap in swaps:
        swap.wait_recv()
    send.finish()
    assert len(send.copies) == REDUCE_COPIES, len(send.copies)


def reduce_parts(dq_part, dk_part, dv_part):
    line = pltpu.VMEM((4, 4, BLK, COLS), BF16)
    two = pltpu.VMEM((2, BLK, COLS), BF16)
    four = pltpu.VMEM((4, BLK, COLS), BF16)
    half = pltpu.VMEM((HALF, COLS), BF16)
    one = pltpu.VMEM((BLK, COLS), BF16)
    inbox = pltpu.VMEM((4, CORES, COLS, BLK), BF16)
    return pl.pallas_call(
        reduce_kernel,
        out_shape=[
            jax.ShapeDtypeStruct((BLK, WIDTH), BF16),
            jax.ShapeDtypeStruct((HALF, WIDTH), BF16),
            jax.ShapeDtypeStruct((HALF, WIDTH), BF16),
        ],
        in_specs=[ANY] * 3,
        out_specs=[ANY] * 3,
        scratch_shapes=[
            pltpu.VMEM((NZ, CORES, COLS, BLK), BF16),
            inbox, inbox,
            line, line,
            two, two, two, two,
            four, four, four, four,
            four, four,
            half, half, half, half,
            one, one, one, one,
            pltpu.VMEM((CORES, BLK, COLS), BF16), one, one,
            pltpu.SemaphoreType.DMA((REDUCE_COPIES,)),
            pltpu.SemaphoreType.DMA((REDUCE_COPIES,)),
            pltpu.SemaphoreType.DMA((13,)),
        ],
        compiler_params=pltpu.CompilerParams(
            collective_id=1, has_side_effects=True, vmem_limit_bytes=VMEM_LIMIT
        ),
        name="reduce_parts",
    )(dq_part.reshape(NZ, CORES, COLS, BLK), dk_part, dv_part)


def body(q, k, v, out, do, lse, block_pairs, counts):
    ka = lax.axis_index("ka")
    place = jnp.stack([ka // NZ, ka % NZ]).astype(jnp.int32)
    lists = block_pairs.transpose(0, 2, 3, 1).reshape(2 * SLOTS, KEY_SHARDS)
    gathered = gather(q, do, k, v, out, lse, lists, counts)
    parts = pairs_over_blocks(*gathered, place)
    return tuple(reduce_parts(*parts))


def solution(mesh):
    placed = (
        P(("pb", "ka"), None),
        P(("ka", "pb"), None),
        P(("ka", "pb"), None),
        P(("pb", "ka"), None),
        P(("pb", "ka"), None),
        P(None, ("pb", "ka")),
        P("pb", None, None, None),
        P("pb", None),
    )
    return jax.shard_map(
        body,
        mesh=mesh,
        in_specs=placed,
        out_specs=(P(("pb", "ka"), None), P(("ka", "pb"), None), P(("ka", "pb"), None)),
        check_vma=False,
    )
```

time: 143 us -> 144 us (level)
  the two profiles are of different devices: /device:TPU:168 before, /device:TPU:1 now
where the time goes in v2:
time: 144 us; the launch traced here: 143 us
  Pallas kernels  137 us (95%)
  local copies, waits for them, and re-layouts  4.8 us (3%)
    pallas_call x1, Pallas kernels, gather(): pl.pallas_call(gather_kernel, out_shape=[jax.ShapeDtypeStruct((NZ, CORES,...  59.9 us
    pallas_call x1, Pallas kernels, reduce_parts(): pl.pallas_call(reduce_kernel, out_shape=[jax.ShapeDtypeStruct((BLK, WIDTH...  52.2 us
    pallas_call x1, Pallas kernels, pairs_over_blocks(): pl.pallas_call(pair_kernel, out_shape=[jax.ShapeDtypeStruct((QUERY_BLOCKS...  24.5 us
    unnamed x3, local copies, waits for them, and re-layouts  4.8 us

profile of v2, /device:TPU:1, one launch (start us, length us, event | category | flops | bytes accessed | tf_op | source)
XLA Modules:
  0.0 142.7 jit_solution(16686814717579000815)
XLA Ops:
  0.6 0.6 pad_add_fusion.place
  1.2 59.9 %gather_blocks.1 = (bf16[8,2,128,512]{3,2,1,0:T(8,128)(2,1)}, bf16[8,2,128,512]{3,2,1,0:T(8,128)(2,1)}, f32[8,2,16,128]{3,2,1,0:T(8,128)}, bf16[4,4,128,512]{3,2...) custom-call(bf16[128,1024]{1,0:T(8,128)(2,1)} %q_ref.1, ...), custom_call_target="tpu_custom_call" | custom-call | tf_op jit(solution)/shard_map/gather_blocks/pallas_call | solution.py:264
  61.2 24.5 %used_pairs.1 = (bf16[16,512,128]{2,1,0:T(8,128)(2,1)}, bf16[4,4,128,512]{3,2,1,0:T(8,128)(2,1)}, bf16[4,4,128,512]{3,2,1,0:T(8,128)(2,1)}) custom-call(s32[2,48,32]{2,1,0:T(8,128)} %get-tuple-element.13.lists, s32[2,1,32]{2,1,0:T(1,128)} %get-tuple-element.14.counts, s32[2]{0:T(128)} %pad_add_fusion.place, bf16[16,128,512]{2,1,0:T(8,128)(2,1)} %bitcast.10, ...), custom_call_target="tpu_custom_call" | custom-call | tf_op jit(solution)/shard_map/used_pairs/pallas_call | solution.py:477
  85.7 52.2 %reduce_parts.1 = (bf16[128,1024]{1,0:T(8,128)(2,1)}, bf16[64,1024]{1,0:T(8,128)(2,1)}, bf16[64,1024]{1,0:T(8,128)(2,1)}) custom-call(bf16[8,2,512,128]{3,2,1,0:T(8,128)(2,1)} %bitcast.9, bf16[4,4,128,512]{3,2,1,0:T(8,128)(2,1)} %get-tuple-element.21.dk_part, bf16[4,4,128,512]{3,2,1,0:T(8,128)(2,1)} %get-tuple-element.22.dv_part), custom_call_target="tpu_custom_call" | custom-call | tf_op jit(solution)/shard_map/reduce_parts/pallas_call | solution.py:689
  137.9 1.7 %copy.14 = bf16[128,1024]{1,0:T(8,128)(2,1)} copy(bf16[128,1024]{1,0:T(8,128)(2,1)} %get-tuple-element.26) | data formatting | bytes 524288
  139.6 1.6 %copy.15 = bf16[64,1024]{1,0:T(8,128)(2,1)} copy(bf16[64,1024]{1,0:T(8,128)(2,1)} %get-tuple-element.27) | data formatting | bytes 262144
  141.1 1.6 %copy.16 = bf16[64,1024]{1,0:T(8,128)(2,1)} copy(bf16[64,1024]{1,0:T(8,128)(2,1)} %get-tuple-element.28) | data formatting | bytes 262144

commit v3 on v2

--- a/solution.py
+++ b/solution.py
@@ -37,14 +37,19 @@
         self.z = lax.rem(ka, NZ)
         self.sibling = (self.y * CORES + 1 - self.core, ka)
 
-    def over_x(self, step):
-        return (self.y * CORES + self.core, self.xs(step) * NZ + self.z)
-
-    def over_y(self, step):
-        return (self.ys(step) * CORES + self.core, self.x * NZ + self.z)
-
-    def over_z(self, step):
-        return (self.y * CORES + self.core, self.x * NZ + self.zs(step))
+    def aim(self, crossed, owner):
+        if owner is not None:
+            return owner
+        return 1 - self.core if crossed else self.core
+
+    def over_x(self, step, crossed=0, owner=None):
+        return (self.y * CORES + self.aim(crossed, owner), self.xs(step) * NZ + self.z)
+
+    def over_y(self, step, crossed=0, owner=None):
+        return (self.ys(step) * CORES + self.aim(crossed, owner), self.x * NZ + self.z)
+
+    def over_z(self, step, crossed=0, owner=None):
+        return (self.y * CORES + self.aim(crossed, owner), self.x * NZ + self.zs(step))
 
     def xs(self, step):
         return lax.rem(self.x + step + NX, NX)
@@ -55,11 +60,13 @@
     def zs(self, step):
         return lax.rem(self.z + step + NZ, NZ)
 
-    def greet(self):
+    def greet(self, both_cores=False):
         barrier = pltpu.get_barrier_semaphore()
         neighbours = [self.sibling]
         for step in (1, -1):
-            neighbours += [self.over_x(step), self.over_y(step), self.over_z(step)]
+            for crossed in (0, 1) if both_cores else (0,):
+                for over in (self.over_x, self.over_y, self.over_z):
+                    neighbours.append(over(step, crossed))
         for neighbour in neighbours:
             pl.semaphore_signal(barrier, inc=1, device_id=neighbour, device_id_type=MESH)
         pl.semaphore_wait(barrier, len(neighbours))
@@ -71,13 +78,13 @@
         self.recv_sems = recv_sems
         self.copies = []
 
-    def __call__(self, source, target, device):
+    def __call__(self, source, target, device, recv_sem=None):
         index = len(self.copies)
         copy = pltpu.make_async_remote_copy(
             src_ref=source,
             dst_ref=target,
             send_sem=self.send_sems.at[index],
-            recv_sem=self.recv_sems.at[index],
+            recv_sem=self.recv_sems.at[index] if recv_sem is None else recv_sem,
             device_id=device,
             device_id_type=MESH,
         )
@@ -94,7 +101,7 @@
     return pl.ds(pl.multiple_of(core * size, size), size)
 
 
-GATHER_COPIES = 46
+GATHER_COPIES = 54
 
 
 def gather_kernel(
@@ -109,6 +116,13 @@
     mine = half_of(core, COLS)
     theirs = half_of(1 - core, COLS)
 
+    loads = [
+        pltpu.make_async_copy(do_ref, do_buf, local_sems.at[5]),
+        pltpu.make_async_copy(out_ref, out_buf, local_sems.at[6]),
+        pltpu.make_async_copy(lse_ref, lse_buf, local_sems.at[7]),
+    ]
+    for load in loads:
+        load.start()
     owns = [
         pltpu.make_async_copy(q_ref.at[every, mine], q_all.at[z, core], local_sems.at[0]),
         pltpu.make_async_copy(do_ref.at[every, mine], do_all.at[z, core], local_sems.at[1]),
@@ -119,42 +133,33 @@
     ]
     for own in owns:
         own.start()
-    loads = [
-        pltpu.make_async_copy(do_ref, do_buf, local_sems.at[5]),
-        pltpu.make_async_copy(out_ref, out_buf, local_sems.at[6]),
-        pltpu.make_async_copy(lse_ref, lse_buf, local_sems.at[7]),
-    ]
-    for load in loads:
-        load.start()
-    me.greet()
+    me.greet(both_cores=True)
     send = Sender(send_sems, recv_sems)
     up, down = me.over_z(1), me.over_z(-1)
 
+    def to_both(ref, target, straight, crossed):
+        return [
+            send(ref.at[every, mine], target, straight),
+            send(ref.at[every, theirs], target, crossed),
+        ]
+
+    cross_up, cross_down = me.over_z(1, 1), me.over_z(-1, 1)
+    q_up = [to_both(q_ref, q_all.at[z, core], up, cross_up)]
+    do_down = [to_both(do_ref, do_all.at[z, core], down, cross_down)]
     k_swap = send(k_ref.at[every, theirs], k_all.at[y, x, rows], me.sibling)
     v_swap = send(v_ref.at[every, theirs], v_all.at[x, y, rows], me.sibling)
-    q_swap = send(q_ref.at[every, theirs], q_all.at[z, core], me.sibling)
-    do_swap = send(do_ref.at[every, theirs], do_all.at[z, core], me.sibling)
-    list_swap = send(list_ref, list_all.at[core], me.sibling)
-    count_swap = send(count_ref, count_all.at[core], me.sibling)
-
-    q_first = [send(q_ref.at[every, mine], q_all.at[z, core], up)]
-    do_first = [send(do_ref.at[every, mine], do_all.at[z, core], down)]
-    for own in owns:
-        own.wait()
-    k_swap.wait_recv()
-    k_right = send(k_all.at[y, x], k_all.at[y, x], me.over_x(1))
-    k_left = send(k_all.at[y, x], k_all.at[y, x], me.over_x(-1))
-    v_swap.wait_recv()
-    v_right = send(v_all.at[x, y], v_all.at[x, y], me.over_y(1))
-    v_left = send(v_all.at[x, y], v_all.at[x, y], me.over_y(-1))
-    q_swap.wait_recv()
-    other_q = q_all.at[z, 1 - core]
-    q_first.append(send(other_q, other_q, up))
-    do_swap.wait_recv()
-    other_do = do_all.at[z, 1 - core]
-    do_first.append(send(other_do, other_do, down))
-    do_up = [send(do_all.at[z], do_all.at[z], up)]
-    q_down = [send(q_all.at[z], q_all.at[z], down)]
+    k_right = to_both(k_ref, k_all.at[y, x, rows], me.over_x(1), me.over_x(1, 1))
+    k_left = to_both(k_ref, k_all.at[y, x, rows], me.over_x(-1), me.over_x(-1, 1))
+    v_right = to_both(v_ref, v_all.at[x, y, rows], me.over_y(1), me.over_y(1, 1))
+    v_left = to_both(v_ref, v_all.at[x, y, rows], me.over_y(-1), me.over_y(-1, 1))
+    do_up = [to_both(do_ref, do_all.at[z, core], up, cross_up)]
+    q_down = [to_both(q_ref, q_all.at[z, core], down, cross_down)]
+    swaps = [
+        send(q_ref.at[every, theirs], q_all.at[z, core], me.sibling),
+        send(do_ref.at[every, theirs], do_all.at[z, core], me.sibling),
+        send(list_ref, list_all.at[core], me.sibling),
+        send(count_ref, count_all.at[core], me.sibling),
+    ]
 
     for load in loads:
         load.wait()
@@ -171,91 +176,83 @@
         heads = slice(side * OWN_HEADS, side * OWN_HEADS + OWN_HEADS)
         st_buf[side, 0:OWN_HEADS, :] = lse_buf[heads, :] * LOG2E
         st_buf[side, OWN_HEADS : 2 * OWN_HEADS, :] = delta[heads, :]
+    for own in owns:
+        own.wait()
     st_own = pltpu.make_async_copy(st_buf.at[core], st_all.at[z, core], local_sems.at[0])
     st_own.start()
-    st_swap = send(st_buf.at[1 - core], st_all.at[z, core], me.sibling)
+    swaps.append(send(st_buf.at[1 - core], st_all.at[z, core], me.sibling))
+    st_up, st_down = [], []
+    for stats, straight, crossed in ((st_up, up, cross_up), (st_down, down, cross_down)):
+        stats.append(
+            [
+                send(st_buf.at[core], st_all.at[z, core], straight),
+                send(st_buf.at[1 - core], st_all.at[z, core], crossed),
+            ]
+        )
+
+    def arrived(*groups):
+        for group in groups:
+            for copy in group:
+                copy.wait_recv()
 
     upper, lower = pl.ds(0, HALF), pl.ds(HALF, HALF)
-    k_right.wait_recv()
-    k_far = [k_all.at[y, me.xs(-1), upper]]
-    k_far = [send(k_far[0], k_far[0], me.over_x(1))]
-    v_right.wait_recv()
+    arrived(k_right)
+    k_part = k_all.at[y, me.xs(-1), upper]
+    k_far = [send(k_part, k_part, me.over_x(1))]
+    arrived(v_right)
     v_part = v_all.at[x, me.ys(-1), upper]
     v_far = [send(v_part, v_part, me.over_y(1))]
-    k_left.wait_recv()
+    arrived(k_left)
     k_part = k_all.at[y, me.xs(1), lower]
     k_far.append(send(k_part, k_part, me.over_x(-1)))
-    v_left.wait_recv()
+    arrived(v_left)
     v_part = v_all.at[x, me.ys(1), lower]
     v_far.append(send(v_part, v_part, me.over_y(-1)))
 
-    st_swap.wait_recv()
-    st_own.wait()
-    st_up = [send(st_all.at[z], st_all.at[z], up)]
-    st_down = [send(st_all.at[z], st_all.at[z], down)]
-
-    for copy in k_far:
-        copy.wait_recv()
-    k_right = send(k_all.at[y], k_all.at[y], me.over_y(1))
-    k_left = send(k_all.at[y], k_all.at[y], me.over_y(-1))
-    for copy in v_far:
-        copy.wait_recv()
-    v_right = send(v_all.at[x], v_all.at[x], me.over_x(1))
-    v_left = send(v_all.at[x], v_all.at[x], me.over_x(-1))
-
-    def forward_up(hop, blocks, copies):
-        for copy in copies[hop - 1] if isinstance(copies[hop - 1], list) else [copies[hop - 1]]:
-            copy.wait_recv()
-        block = blocks.at[me.zs(-hop)]
-        copies.append(send(block, block, up))
-
-    def forward_down(hop, blocks, copies):
-        for copy in copies[hop - 1] if isinstance(copies[hop - 1], list) else [copies[hop - 1]]:
-            copy.wait_recv()
-        block = blocks.at[me.zs(hop)]
-        copies.append(send(block, block, down))
-
-    q_up, do_down = [q_first], [do_first]
-    forward_up(1, q_all, q_up)
-    forward_down(1, do_all, do_down)
-    forward_up(1, do_all, do_up)
-    forward_down(1, q_all, q_down)
-    forward_up(1, st_all, st_up)
-    forward_down(1, st_all, st_down)
+    arrived([k_swap], k_far)
+    k_right = [send(k_all.at[y], k_all.at[y], me.over_y(1))]
+    k_left = [send(k_all.at[y], k_all.at[y], me.over_y(-1))]
+    arrived([v_swap], v_far)
+    v_right = [send(v_all.at[x], v_all.at[x], me.over_x(1))]
+    v_left = [send(v_all.at[x], v_all.at[x], me.over_x(-1))]
+
+    def forward(hop, sign, blocks, copies):
+        arrived(copies[hop - 1])
+        block = blocks.at[me.zs(-sign * hop)]
+        copies.append([send(block, block, up if sign > 0 else down)])
+
+    forward(1, 1, q_all, q_up)
+    forward(1, -1, do_all, do_down)
+    forward(1, 1, do_all, do_up)
+    forward(1, -1, q_all, q_down)
+    forward(1, 1, st_all, st_up)
+    forward(1, -1, st_all, st_down)
 
     def across(blocks, start, low, device):
         part = blocks.at[start, pl.ds(low, 2)]
         return send(part, part, device)
 
-    k_right.wait_recv()
+    arrived(k_right)
     k_far = [across(k_all, me.ys(-1), 0, me.over_y(1))]
-    v_right.wait_recv()
+    arrived(v_right)
     v_far = [across(v_all, me.xs(-1), 0, me.over_x(1))]
-    k_left.wait_recv()
+    arrived(k_left)
     k_far.append(across(k_all, me.ys(1), 2, me.over_y(-1)))
-    v_left.wait_recv()
+    arrived(v_left)
     v_far.append(across(v_all, me.xs(1), 2, me.over_x(-1)))
 
-    forward_up(2, q_all, q_up)
-    forward_down(2, do_all, do_down)
-    forward_up(2, do_all, do_up)
-    forward_down(2, q_all, q_down)
-    forward_up(2, st_all, st_up)
-    forward_down(2, st_all, st_down)
-
-    forward_up(3, q_all, q_up)
-    forward_down(3, do_all, do_down)
-    forward_up(3, st_all, st_up)
-    for copy in k_far + v_far:
-        copy.wait_recv()
-    do_up[2].wait_recv()
-    q_down[2].wait_recv()
-    st_down[2].wait_recv()
-    list_swap.wait_recv()
-    count_swap.wait_recv()
-    q_up[3].wait_recv()
-    do_down[3].wait_recv()
-    st_up[3].wait_recv()
+    forward(2, 1, q_all, q_up)
+    forward(2, -1, do_all, do_down)
+    forward(2, 1, do_all, do_up)
+    forward(2, -1, q_all, q_down)
+    forward(2, 1, st_all, st_up)
+    forward(2, -1, st_all, st_down)
+
+    forward(3, 1, q_all, q_up)
+    forward(3, -1, do_all, do_down)
+    forward(3, 1, st_all, st_up)
+    arrived(k_far, v_far, swaps, do_up[2], q_down[2], st_down[2], q_up[3], do_down[3], st_up[3])
+    st_own.wait()
     send.finish()
     assert len(send.copies) == GATHER_COPIES, len(send.copies)
 
@@ -293,7 +290,7 @@
 def pair_kernel(
     lists, counts, place, q_all, do_all, st_all, k_all, v_all,
     dq_out, dk_out, dv_out,
-    q_buf, do_buf, st_buf, k_buf, v_buf, k_turned, dq_sum, dk_sum, dv_sum, dq_stage, dk_stage, dv_stage, zeros,
+    q_buf, do_buf, st_buf, k_buf, v_buf, k_turned, p_buf, ds_buf, dq_sum, dk_sum, dv_sum, dq_stage, dk_stage, dv_stage, zeros,
     listed, filled, flat, in_sems, out_sems, zero_sems, dq_sems,
 ):
     x = place[0]
@@ -393,7 +390,7 @@
                 turned = jnp.transpose(k_buf[slot, :, lanes].astype(F32)).astype(BF16)
                 k_turned[lanes, :] = turned
 
-        for pair in range(HEAD_PAIRS):
+        def forward(pair):
             lanes = slice(pair * 128, pair * 128 + 128)
             keys = k_buf[slot, :, lanes]
             values = v_buf[slot, :, lanes]
@@ -412,18 +409,29 @@
                 prob = jnp.exp2(scores[:, cut] * (SCALE * LOG2E) - lse)
                 probs.append(prob.astype(BF16))
                 dscores.append((prob * (dprob[:, cut] - delta)).astype(BF16))
-            dv_sum[:, lanes] += lax.dot_general(
-                jnp.concatenate(probs, axis=1), do_two, nn, preferred_element_type=F32
-            )
-            dk_sum[:, lanes] += lax.dot_general(
-                jnp.concatenate(dscores, axis=1), q_two, nn, preferred_element_type=F32
-            )
+            p_buf[pair] = jnp.concatenate(probs, axis=1)
+            ds_buf[pair] = jnp.concatenate(dscores, axis=1)
+
+        def backward(pair):
+            lanes = slice(pair * 128, pair * 128 + 128)
+            queries = q_buf[slot, :, lanes]
+            douts = do_buf[slot, :, lanes]
+            q_two = jnp.concatenate([queries * first_half, queries * second_half], axis=0)
+            do_two = jnp.concatenate([douts * first_half, douts * second_half], axis=0)
+            dv_sum[:, lanes] += lax.dot_general(p_buf[pair], do_two, nn, preferred_element_type=F32)
+            dk_sum[:, lanes] += lax.dot_general(ds_buf[pair], q_two, nn, preferred_element_type=F32)
             turned = k_turned[lanes, :]
+            both = lax.dot_general(turned, ds_buf[pair], nn, preferred_element_type=F32)
             for side in range(2):
                 low = pair * 128 + side * 64
-                dq_sum[query, low : low + 64, :] += lax.dot_general(
-                    turned[side * 64 : side * 64 + 64], dscores[side], nn, preferred_element_type=F32
-                )
+                dq_sum[query, low : low + 64, :] += both[
+                    side * 64 : side * 64 + 64, side * BLK : side * BLK + BLK
+                ]
+
+        for pair in range(HEAD_PAIRS):
+            forward(pair)
+        for pair in range(HEAD_PAIRS):
+            backward(pair)
 
         @pl.when(after != block)
         def _():
@@ -490,6 +498,8 @@
             block_pair,
             block_pair,
             pltpu.VMEM((COLS, BLK), BF16),
+            pltpu.VMEM((HEAD_PAIRS, BLK, 2 * BLK), BF16),
+            pltpu.VMEM((HEAD_PAIRS, BLK, 2 * BLK), BF16),
             pltpu.VMEM((QUERY_BLOCKS, COLS, BLK), F32),
             pltpu.VMEM((BLK, COLS), F32),
             pltpu.VMEM((BLK, COLS), F32),
@@ -519,37 +529,40 @@
     )
 
 
-REDUCE_COPIES = 33
+REDUCE_COPIES = 41
 ROW_STEP = 16
 
 
 def reduce_kernel(
     dq_part, dk_part, dv_part,
     gq_out, gk_out, gv_out,
-    dq_own, dq_in_up, dq_in_down, k_own, v_own,
-    k_far_a, k_far_b, v_far_a, v_far_b, k_near_a, k_near_b, v_near_a, v_near_b,
-    k_mid, v_mid, k_end_far_a, k_end_far_b, v_end_far_a, v_end_far_b,
-    k_end_a, k_end_b, v_end_a, v_end_b, gq_buf, gk_buf, gv_buf,
-    send_sems, recv_sems, local_sems,
+    dq_own, dq_in_up, dq_in_down, dq_end,
+    k_own, k_far, k_near, k_mid, k_mid_far, k_end,
+    v_own, v_far, v_near, v_mid, v_mid_far, v_end,
+    send_sems, recv_sems, local_sems, q_end_sems, k_end_sems, v_end_sems,
 ):
     me = Place()
     x, y, z, core = me.x, me.y, me.z, me.core
-    every = slice(None)
-    loads = {}
-    for order, step in enumerate((3, -3, 2, -2, 1, -1, 0)):
-        loads["q", step] = pltpu.make_async_copy(
-            dq_part.at[me.zs(step)], dq_own.at[me.zs(step)], local_sems.at[order]
-        )
-    for order, step in enumerate((1, -1, 0)):
-        loads["k", step] = pltpu.make_async_copy(
-            dk_part.at[me.ys(step)], k_own.at[me.ys(step)], local_sems.at[7 + order]
-        )
-        loads["v", step] = pltpu.make_async_copy(
-            dv_part.at[me.xs(step)], v_own.at[me.xs(step)], local_sems.at[10 + order]
-        )
-    for load in loads.values():
-        load.start()
-    me.greet()
+    loads = []
+
+    def load(source, target):
+        copy = pltpu.make_async_copy(source, target, local_sems.at[len(loads)])
+        copy.start()
+        loads.append(copy)
+
+    first, second = pl.ds(0, 2), pl.ds(2, 2)
+    load(dq_part.at[me.zs(3), 0], dq_own.at[me.zs(3), 0])
+    load(dq_part.at[me.zs(-3), 1], dq_own.at[me.zs(-3), 1])
+    load(dk_part.at[me.ys(1), first], k_own.at[me.ys(1), first])
+    load(dv_part.at[me.xs(1), first], v_own.at[me.xs(1), first])
+    load(dk_part.at[me.ys(-1), second], k_own.at[me.ys(-1), second])
+    load(dv_part.at[me.xs(-1), second], v_own.at[me.xs(-1), second])
+    for step in (2, -2, 1, -1):
+        load(dq_part.at[me.zs(step)], dq_own.at[me.zs(step)])
+    load(dk_part.at[y], k_own.at[y])
+    load(dv_part.at[x], v_own.at[x])
+    load(dq_part.at[z, core], dq_end.at[2, core])
+    me.greet(both_cores=True)
     send = Sender(send_sems, recv_sems)
     up, down = me.over_z(1), me.over_z(-1)
 
@@ -564,128 +577,132 @@
 
         lax.fori_loop(0, count // ROW_STEP, one, 0, unroll=4)
 
-    far = me.zs(4)
     arrive = {
-        ("up", 0, 1): send(dq_part.at[far, 0], dq_in_up.at[0, 0], up),
-        ("down", 1, 1): send(dq_part.at[far, 1], dq_in_down.at[0, 1], down),
+        ("up", 0, 1): send(dq_part.at[me.zs(4), 0], dq_in_up.at[0, 0], up),
+        ("down", 1, 1): send(dq_part.at[me.zs(4), 1], dq_in_down.at[0, 1], down),
     }
-    far_y, far_x = me.ys(2), me.xs(2)
-    kf_a = send(dk_part.at[far_y, pl.ds(0, 2)], k_far_a, me.over_y(1))
-    kf_b = send(dk_part.at[far_y, pl.ds(2, 2)], k_far_b, me.over_y(-1))
-    vf_a = send(dv_part.at[far_x, pl.ds(0, 2)], v_far_a, me.over_x(1))
-    vf_b = send(dv_part.at[far_x, pl.ds(2, 2)], v_far_b, me.over_x(-1))
+    k_a = send(dk_part.at[me.ys(2), first], k_far.at[0], me.over_y(1))
+    k_b = send(dk_part.at[me.ys(2), second], k_far.at[1], me.over_y(-1))
+    v_a = send(dv_part.at[me.xs(2), first], v_far.at[0], me.over_x(1))
+    v_b = send(dv_part.at[me.xs(2), second], v_far.at[1], me.over_x(-1))
     arrive["up", 1, 2] = send(dq_part.at[me.zs(3), 1], dq_in_up.at[1, 1], up)
     arrive["down", 0, 2] = send(dq_part.at[me.zs(-3), 0], dq_in_down.at[1, 0], down)
+    k_in = [
+        send(dk_part.at[me.ys(1), second], k_near.at[0, second], me.over_y(1)),
+        send(dk_part.at[me.ys(-1), first], k_near.at[1, first], me.over_y(-1)),
+    ]
+    v_in = [
+        send(dv_part.at[me.xs(1), second], v_near.at[0, second], me.over_x(1)),
+        send(dv_part.at[me.xs(-1), first], v_near.at[1, first], me.over_x(-1)),
+    ]
+    q_sib = send(dq_part.at[z, 1 - core], dq_end.at[2, core], me.sibling, q_end_sems.at[2, core])
 
     def hop_q(direction, shard, hop):
         if direction == "up":
-            step, inbox, device = 4 - hop, dq_in_up, up
+            side, step, inbox, way = 0, 4 - hop, dq_in_up, 1
         else:
-            step, inbox, device = hop - 4, dq_in_down, down
+            side, step, inbox, way = 1, hop - 4, dq_in_down, -1
         own = dq_own.at[me.zs(step), shard]
         arrive[direction, shard, hop].wait_recv()
         add_rows(own, [own, inbox.at[hop - 1, shard]], COLS)
-        arrive[direction, shard, hop + 1] = send(own, inbox.at[hop, shard], device)
-
-    for load in loads.values():
-        load.wait()
+        if hop < 3:
+            arrive[direction, shard, hop + 1] = send(own, inbox.at[hop, shard], me.over_z(way))
+        else:
+            send(own, dq_end.at[side, core], me.over_z(way, owner=shard), q_end_sems.at[side, core])
+
+    for copy in loads:
+        copy.wait()
     hop_q("up", 0, 1)
     hop_q("down", 1, 1)
 
-    def onward(own, place, base, inbox, arrival):
+    def onward(arrival, own, place, base, inbox):
         arrival.wait_recv()
         for row in range(2):
             part = own.at[place, base + row]
             add_rows(part, [part, inbox.at[row]], BLK)
 
-    onward(k_own, me.ys(1), 0, k_far_a, kf_a)
-    kn_a = send(k_own.at[me.ys(1)], k_near_a, me.over_y(1))
-    onward(v_own, me.xs(1), 0, v_far_a, vf_a)
-    vn_a = send(v_own.at[me.xs(1)], v_near_a, me.over_x(1))
-    onward(k_own, me.ys(-1), 2, k_far_b, kf_b)
-    kn_b = send(k_own.at[me.ys(-1)], k_near_b, me.over_y(-1))
-    onward(v_own, me.xs(-1), 2, v_far_b, vf_b)
-    vn_b = send(v_own.at[me.xs(-1)], v_near_b, me.over_x(-1))
-    hop_q("up", 1, 2)
-    hop_q("down", 0, 2)
-    hop_q("up", 0, 2)
-    hop_q("down", 1, 2)
-    hop_q("up", 1, 3)
-    hop_q("down", 0, 3)
-    hop_q("up", 0, 3)
-    hop_q("down", 1, 3)
-
-    for arrival in (kn_a, kn_b):
+    onward(k_a, k_own, me.ys(1), 0, k_far.at[0])
+    k_in.append(send(k_own.at[me.ys(1), first], k_near.at[0, first], me.over_y(1)))
+    onward(v_a, v_own, me.xs(1), 0, v_far.at[0])
+    v_in.append(send(v_own.at[me.xs(1), first], v_near.at[0, first], me.over_x(1)))
+    onward(k_b, k_own, me.ys(-1), 2, k_far.at[1])
+    k_in.append(send(k_own.at[me.ys(-1), second], k_near.at[1, second], me.over_y(-1)))
+    onward(v_b, v_own, me.xs(-1), 2, v_far.at[1])
+    v_in.append(send(v_own.at[me.xs(-1), second], v_near.at[1, second], me.over_x(-1)))
+    for hop, shard in ((2, 1), (2, 0), (3, 1), (3, 0)):
+        hop_q("up", shard, hop)
+        hop_q("down", 1 - shard, hop)
+
+    half_rows = (pl.ds(0, HALF), pl.ds(HALF, HALF))
+
+    def turn(arrivals, own, here, near, middle, far, end, sems, axis, over, place):
+        for arrival in arrivals:
+            arrival.wait_recv()
+        for row in range(4):
+            add_rows(middle.at[row], [own.at[here, row], near.at[0, row], near.at[1, row]], BLK)
+        ahead, back = axis(1), axis(-1)
+        farthest = axis(2)
+        far_a = send(middle.at[farthest, half_rows[0]], far.at[0], over(1))
+        far_b = send(middle.at[farthest, half_rows[1]], far.at[1], over(-1))
+        send(middle.at[ahead, half_rows[1]], end.at[0, core], over(1, owner=1), sems.at[0, core])
+        send(middle.at[back, half_rows[0]], end.at[1, core], over(-1, owner=0), sems.at[1, core])
+        send(middle.at[place, half_of(1 - core, HALF)], end.at[2, core], me.sibling, sems.at[2, core])
+        end[2, core] = middle[place, half_of(core, HALF), :]
+        return far_a, far_b
+
+    def last(arrival, middle, at, half, far, end, sems, side, device):
         arrival.wait_recv()
-    for row in range(4):
-        add_rows(k_mid.at[row], [k_own.at[y, row], k_near_a.at[row], k_near_b.at[row]], BLK)
-    half_rows = (pl.ds(0, HALF), pl.ds(HALF, HALF))
-    ke_a = send(k_mid.at[far_x, half_rows[0]], k_end_far_a, me.over_x(1))
-    ke_b = send(k_mid.at[far_x, half_rows[1]], k_end_far_b, me.over_x(-1))
-    for arrival in (vn_a, vn_b):
-        arrival.wait_recv()
-    for row in range(4):
-        add_rows(v_mid.at[row], [v_own.at[x, row], v_near_a.at[row], v_near_b.at[row]], BLK)
-    ve_a = send(v_mid.at[far_y, half_rows[0]], v_end_far_a, me.over_y(1))
-    ve_b = send(v_mid.at[far_y, half_rows[1]], v_end_far_b, me.over_y(-1))
-
-    def last(middle, place, half, inbox, arrival, target, device):
-        arrival.wait_recv()
-        part = middle.at[place, half_rows[half]]
-        add_rows(part, [part, inbox], HALF)
-        return send(middle.at[place], target, device)
-
-    kz_a = last(k_mid, me.xs(1), 0, k_end_far_a, ke_a, k_end_a, me.over_x(1))
-    kz_b = last(k_mid, me.xs(-1), 1, k_end_far_b, ke_b, k_end_b, me.over_x(-1))
-    vz_a = last(v_mid, me.ys(1), 0, v_end_far_a, ve_a, v_end_a, me.over_y(1))
-    vz_b = last(v_mid, me.ys(-1), 1, v_end_far_b, ve_b, v_end_b, me.over_y(-1))
-
-    mine = half_of(core, COLS)
-    swaps, stores = [], []
-    for direction in ("up", "down"):
-        for shard in range(CORES):
-            arrive[direction, shard, 4].wait_recv()
-    for shard in range(CORES):
+        part = middle.at[at, half_rows[half]]
+        add_rows(part, [part, far], HALF)
+        send(part, end.at[side, core], device, sems.at[side, core])
+
+    kx_a, kx_b = turn(
+        k_in, k_own, y, k_near, k_mid, k_mid_far, k_end, k_end_sems, me.xs, me.over_x, x
+    )
+    vy_a, vy_b = turn(
+        v_in, v_own, x, v_near, v_mid, v_mid_far, v_end, v_end_sems, me.ys, me.over_y, y
+    )
+    last(kx_a, k_mid, me.xs(1), 0, k_mid_far.at[0], k_end, k_end_sems, 0, me.over_x(1, owner=0))
+    last(kx_b, k_mid, me.xs(-1), 1, k_mid_far.at[1], k_end, k_end_sems, 1, me.over_x(-1, owner=1))
+    last(vy_a, v_mid, me.ys(1), 0, v_mid_far.at[0], v_end, v_end_sems, 0, me.over_y(1, owner=0))
+    last(vy_b, v_mid, me.ys(-1), 1, v_mid_far.at[1], v_end, v_end_sems, 1, me.over_y(-1, owner=1))
+
+    def ended(end, sems):
+        for side in range(2):
+            for column in range(CORES):
+                pltpu.make_async_copy(end.at[side, column], end.at[side, column], sems.at[side, column]).wait()
+        other = end.at[2, 1 - core]
+        pltpu.make_async_copy(other, other, sems.at[2, 1 - core]).wait()
+
+    ended(dq_end, q_end_sems)
+    for column in range(CORES):
         for tile in range(COLS // 128):
             at = pl.ds(tile * 128, 128)
             value = (
-                dq_own[z, shard, at, :].astype(F32)
-                + dq_in_up[3, shard, at, :].astype(F32)
-                + dq_in_down[3, shard, at, :].astype(F32)
+                dq_end[0, column, at, :].astype(F32)
+                + dq_end[1, column, at, :].astype(F32)
+                + dq_end[2, column, at, :].astype(F32)
             )
-            gq_buf[shard, :, at] = jnp.transpose(value).astype(BF16)
-    swaps.append(send(gq_buf.at[1 - core], gq_out.at[every, mine], me.sibling))
-    stores.append(pltpu.make_async_copy(gq_buf.at[core], gq_out.at[every, mine], local_sems.at[0]))
-    stores[-1].start()
-
-    own_rows, other_rows = half_of(core, HALF), half_of(1 - core, HALF)
-    for arrival in (kz_a, kz_b):
-        arrival.wait_recv()
-    add_rows(gk_buf, [k_mid.at[x], k_end_a, k_end_b], BLK)
-    swaps.append(send(gk_buf.at[other_rows], gk_out.at[every, mine], me.sibling))
-    stores.append(pltpu.make_async_copy(gk_buf.at[own_rows], gk_out.at[every, mine], local_sems.at[1]))
-    stores[-1].start()
-    for arrival in (vz_a, vz_b):
-        arrival.wait_recv()
-    add_rows(gv_buf, [v_mid.at[y], v_end_a, v_end_b], BLK)
-    swaps.append(send(gv_buf.at[other_rows], gv_out.at[every, mine], me.sibling))
-    stores.append(pltpu.make_async_copy(gv_buf.at[own_rows], gv_out.at[every, mine], local_sems.at[2]))
-    stores[-1].start()
-    for store in stores:
-        store.wait()
-    for swap in swaps:
-        swap.wait_recv()
+            gq_out[:, pl.ds(column * COLS + tile * 128, 128)] = jnp.transpose(value).astype(BF16)
+    for out, end, sems in ((gk_out, k_end, k_end_sems), (gv_out, v_end, v_end_sems)):
+        ended(end, sems)
+        for column in range(CORES):
+            target = out.at[:, pl.ds(column * COLS, COLS)]
+            add_rows(target, [end.at[side, column] for side in range(3)], HALF)
     send.finish()
     assert len(send.copies) == REDUCE_COPIES, len(send.copies)
 
 
 def reduce_parts(dq_part, dk_part, dv_part):
     line = pltpu.VMEM((4, 4, BLK, COLS), BF16)
-    two = pltpu.VMEM((2, BLK, COLS), BF16)
+    two = pltpu.VMEM((2, 2, BLK, COLS), BF16)
+    near = pltpu.VMEM((2, 4, BLK, COLS), BF16)
     four = pltpu.VMEM((4, BLK, COLS), BF16)
-    half = pltpu.VMEM((HALF, COLS), BF16)
-    one = pltpu.VMEM((BLK, COLS), BF16)
-    inbox = pltpu.VMEM((4, CORES, COLS, BLK), BF16)
+    half = pltpu.VMEM((2, HALF, COLS), BF16)
+    end = pltpu.VMEM((3, CORES, HALF, COLS), BF16)
+    inbox = pltpu.VMEM((3, CORES, COLS, BLK), BF16)
+    vmem = pl.BlockSpec(memory_space=pltpu.VMEM)
+    sems = pltpu.SemaphoreType.DMA((3, CORES))
     return pl.pallas_call(
         reduce_kernel,
         out_shape=[
@@ -694,20 +711,15 @@
             jax.ShapeDtypeStruct((HALF, WIDTH), BF16),
         ],
         in_specs=[ANY] * 3,
-        out_specs=[ANY] * 3,
+        out_specs=[vmem] * 3,
         scratch_shapes=[
-            pltpu.VMEM((NZ, CORES, COLS, BLK), BF16),
-            inbox, inbox,
-            line, line,
-            two, two, two, two,
-            four, four, four, four,
-            four, four,
-            half, half, half, half,
-            one, one, one, one,
-            pltpu.VMEM((CORES, BLK, COLS), BF16), one, one,
+            pltpu.VMEM((NZ, CORES, COLS, BLK), BF16), inbox, inbox, inbox,
+            line, two, near, four, half, end,
+            line, two, near, four, half, end,
             pltpu.SemaphoreType.DMA((REDUCE_COPIES,)),
             pltpu.SemaphoreType.DMA((REDUCE_COPIES,)),
             pltpu.SemaphoreType.DMA((13,)),
+            sems, sems, sems,
         ],
         compiler_params=pltpu.CompilerParams(
             collective_id=1, has_side_effects=True, vmem_limit_bytes=VMEM_LIMIT

time: 144 us -> 126 us (0.88)
  Pallas kernels: 137 us -> 118 us
    pallas_call x1, Pallas kernels: 52.2 us -> 44.4 us  [reduce_parts(): pl.pallas_call(reduce_kernel, out_shape=[jax.ShapeDtypeStruct((BLK, WIDTH...]
    pallas_call x1, Pallas kernels: 24.5 us -> 17.3 us  [pairs_over_blocks(): pl.pallas_call(pair_kernel, out_shape=[jax.ShapeDtypeStruct((QUERY_BLOCKS...]
    pallas_call x1, Pallas kernels: 59.9 us -> 56.2 us  [gather(): pl.pallas_call(gather_kernel, out_shape=[jax.ShapeDtypeStruct((NZ, CORES,...]
where the time goes in v3:
time: 126 us; the launch traced here: 124 us
  Pallas kernels  118 us (94%)
  local copies, waits for them, and re-layouts  4.8 us (4%)
    pallas_call x1, Pallas kernels, gather(): pl.pallas_call(gather_kernel, out_shape=[jax.ShapeDtypeStruct((NZ, CORES,...  56.2 us
    pallas_call x1, Pallas kernels, reduce_parts(): pl.pallas_call(reduce_kernel, out_shape=[jax.ShapeDtypeStruct((BLK, WIDTH...  44.4 us
    pallas_call x1, Pallas kernels, pairs_over_blocks(): pl.pallas_call(pair_kernel, out_shape=[jax.ShapeDtypeStruct((QUERY_BLOCKS...  17.3 us
    unnamed x3, local copies, waits for them, and re-layouts  4.8 us

profile of v3, /device:TPU:1, one launch (start us, length us, event | category | flops | bytes accessed | tf_op | source)
XLA Modules:
  0.0 123.9 jit_solution(99677231732492025)
XLA Ops:
  0.6 0.6 pad_add_fusion.place
  1.2 56.2 %gather_blocks.1 = (bf16[8,2,128,512]{3,2,1,0:T(8,128)(2,1)}, bf16[8,2,128,512]{3,2,1,0:T(8,128)(2,1)}, f32[8,2,16,128]{3,2,1,0:T(8,128)}, bf16[4,4,128,512]{3,2...) custom-call(bf16[128,1024]{1,0:T(8,128)(2,1)} %q_ref.1, ...), custom_call_target="tpu_custom_call" | custom-call | tf_op jit(solution)/shard_map/gather_blocks/pallas_call | solution.py:261
  57.4 17.3 %used_pairs.1 = (bf16[16,512,128]{2,1,0:T(8,128)(2,1)}, bf16[4,4,128,512]{3,2,1,0:T(8,128)(2,1)}, bf16[4,4,128,512]{3,2,1,0:T(8,128)(2,1)}) custom-call(s32[2,48,32]{2,1,0:T(8,128)} %get-tuple-element.13.lists, s32[2,1,32]{2,1,0:T(1,128)} %get-tuple-element.14.counts, s32[2]{0:T(128)} %pad_add_fusion.place, bf16[16,128,512]{2,1,0:T(8,128)(2,1)} %bitcast.10, ...), custom_call_target="tpu_custom_call" | custom-call | tf_op jit(solution)/shard_map/used_pairs/pallas_call | solution.py:485
  74.7 44.4 %reduce_parts.1 = (bf16[128,1024]{1,0:T(8,128)(2,1)}, bf16[64,1024]{1,0:T(8,128)(2,1)}, bf16[64,1024]{1,0:T(8,128)(2,1)}) custom-call(bf16[8,2,512,128]{3,2,1,0:T(8,128)(2,1)} %bitcast.9, bf16[4,4,128,512]{3,2,1,0:T(8,128)(2,1)} %get-tuple-element.21.dk_part, bf16[4,4,128,512]{3,2,1,0:T(8,128)(2,1)} %get-tuple-element.22.dv_part), custom_call_target="tpu_custom_call" | custom-call | tf_op jit(solution)/shard_map/reduce_parts/pallas_call | solution.py:706
  119.0 1.7 %copy.14 = bf16[128,1024]{1,0:T(8,128)(2,1)} copy(bf16[128,1024]{1,0:T(8,128)(2,1)} %get-tuple-element.26) | data formatting | bytes 524288
  120.7 1.6 %copy.15 = bf16[64,1024]{1,0:T(8,128)(2,1)} copy(bf16[64,1024]{1,0:T(8,128)(2,1)} %get-tuple-element.27) | data formatting | bytes 262144
  122.3 1.6 %copy.16 = bf16[64,1024]{1,0:T(8,128)(2,1)} copy(bf16[64,1024]{1,0:T(8,128)(2,1)} %get-tuple-element.28) | data formatting | bytes 262144

commit v4 on v3

--- a/solution.py
+++ b/solution.py
@@ -20,9 +20,11 @@
 BUCKET = 32
 SCALE = 64**-0.5
 LOG2E = 1.4426950408889634
-VMEM_LIMIT = 60 << 20
+VMEM_LIMIT = 24 << 20
+GATHER_LIMIT = 24 << 20
 MESH = pl.DeviceIdType.MESH
-ANY = pl.BlockSpec(memory_space=pl.ANY)
+HBM = pl.BlockSpec(memory_space=pltpu.HBM)
+VMEM = pl.BlockSpec(memory_space=pltpu.VMEM)
 F32 = jnp.float32
 BF16 = jnp.bfloat16
 
@@ -269,8 +271,8 @@
             jax.ShapeDtypeStruct((CORES, 2 * SLOTS, KEY_SHARDS), jnp.int32),
             jax.ShapeDtypeStruct((CORES, 1, KEY_SHARDS), jnp.int32),
         ],
-        in_specs=[ANY] * 8,
-        out_specs=[ANY] * 7,
+        in_specs=[HBM] * 8,
+        out_specs=[VMEM] * 5 + [HBM] * 2,
         scratch_shapes=[
             pltpu.VMEM((BLK, WIDTH), BF16),
             pltpu.VMEM((BLK, WIDTH), BF16),
@@ -281,7 +283,7 @@
             pltpu.SemaphoreType.DMA((9,)),
         ],
         compiler_params=pltpu.CompilerParams(
-            collective_id=0, has_side_effects=True, vmem_limit_bytes=VMEM_LIMIT
+            collective_id=0, has_side_effects=True, vmem_limit_bytes=GATHER_LIMIT
         ),
         name="gather_blocks",
     )(q, do, k, v, out, lse, lists, counts)
@@ -290,8 +292,7 @@
 def pair_kernel(
     lists, counts, place, q_all, do_all, st_all, k_all, v_all,
     dq_out, dk_out, dv_out,
-    q_buf, do_buf, st_buf, k_buf, v_buf, k_turned, p_buf, ds_buf, dq_sum, dk_sum, dv_sum, dq_stage, dk_stage, dv_stage, zeros,
-    listed, filled, flat, in_sems, out_sems, zero_sems, dq_sems,
+    k_turned, p_buf, ds_buf, dq_sum, dk_sum, dv_sum, listed, filled,
 ):
     x = place[0]
     z = place[1]
@@ -305,45 +306,11 @@
                 query = lists[owner, slot, shard]
                 block = lists[owner, SLOTS + slot, shard] * NX + column
                 have = filled[block]
-                where = lax.rem(query, NZ) * CORES + owner
-                listed[block * BUCKET + have] = block * QUERY_BLOCKS + where
+                listed[block * BUCKET + have] = lax.rem(query, NZ) * CORES + owner
                 filled[block] = have + jnp.where(lax.div(query, NZ) == x, 1, 0)
                 return carry
 
             lax.fori_loop(0, counts[owner, 0, shard], enlist, 0)
-    zeros[...] = jnp.zeros_like(zeros)
-    total = jnp.int32(0)
-    for block in range(KEY_BLOCKS):
-
-        def append(slot, position, block=block):
-            flat[position] = listed[block * BUCKET + slot]
-            return position + 1
-
-        total = lax.fori_loop(0, filled[block], append, total)
-        up, across = divmod(block, NX)
-
-        @pl.when(filled[block] == 0)
-        def _(up=up, across=across):
-            pltpu.make_async_copy(zeros, dk_out.at[up, across], zero_sems.at[0]).start()
-            pltpu.make_async_copy(zeros, dv_out.at[across, up], zero_sems.at[1]).start()
-
-    def fetches(index, slot):
-        entry = flat[index]
-        block = lax.div(entry, QUERY_BLOCKS)
-        up, across = lax.div(block, NX), lax.rem(block, NX)
-        query = lax.rem(entry, QUERY_BLOCKS)
-        return [
-            pltpu.make_async_copy(k_all.at[up, across], k_buf.at[slot], in_sems.at[slot, 0]),
-            pltpu.make_async_copy(q_all.at[query], q_buf.at[slot], in_sems.at[slot, 1]),
-            pltpu.make_async_copy(st_all.at[query], st_buf.at[slot], in_sems.at[slot, 2]),
-            pltpu.make_async_copy(v_all.at[across, up], v_buf.at[slot], in_sems.at[slot, 3]),
-            pltpu.make_async_copy(do_all.at[query], do_buf.at[slot], in_sems.at[slot, 4]),
-        ]
-
-    @pl.when(total > 0)
-    def _():
-        for fetch in fetches(0, 0):
-            fetch.start()
 
     def clear(query, carry):
         dq_sum[query] = jnp.zeros((COLS, BLK), F32)
@@ -357,131 +324,89 @@
     nt = (((1,), (1,)), ((), ()))
     nn = (((1,), (0,)), ((), ()))
 
-    def flush_copies(slot, block):
+    def key_block(block, carry):
         up, across = lax.div(block, NX), lax.rem(block, NX)
-        return [
-            pltpu.make_async_copy(dk_stage.at[slot], dk_out.at[up, across], out_sems.at[slot, 0]),
-            pltpu.make_async_copy(dv_stage.at[slot], dv_out.at[across, up], out_sems.at[slot, 1]),
-        ]
-
-    def step(index, flushed):
-        slot = lax.rem(index, 2)
-        block = lax.div(flat[index], QUERY_BLOCKS)
-        query = lax.rem(flat[index], QUERY_BLOCKS)
-        before = jnp.where(index > 0, lax.div(flat[jnp.maximum(index - 1, 0)], QUERY_BLOCKS), -1)
-        after = jnp.where(
-            index + 1 < total, lax.div(flat[jnp.minimum(index + 1, total - 1)], QUERY_BLOCKS), -1
-        )
-
-        @pl.when(index + 1 < total)
+        have = filled[block]
+
+        @pl.when(have == 0)
         def _():
-            for fetch in fetches(index + 1, 1 - slot):
-                fetch.start()
-
-        for fetch in fetches(index, slot):
-            fetch.wait()
-
-        @pl.when(before != block)
+            dk_out[up, across] = jnp.zeros((BLK, COLS), BF16)
+            dv_out[across, up] = jnp.zeros((BLK, COLS), BF16)
+
+        def used(slot, carry):
+            query = listed[block * BUCKET + slot]
+
+            def forward(pair):
+                lanes = slice(pair * 128, pair * 128 + 128)
+                keys = k_all[up, across, :, lanes]
+                values = v_all[across, up, :, lanes]
+                queries = q_all[query, :, lanes]
+                douts = do_all[query, :, lanes]
+                q_two = jnp.concatenate([queries * first_half, queries * second_half], axis=0)
+                do_two = jnp.concatenate([douts * first_half, douts * second_half], axis=0)
+                scores = lax.dot_general(keys, q_two, nt, preferred_element_type=F32)
+                dprob = lax.dot_general(values, do_two, nt, preferred_element_type=F32)
+                for side in range(2):
+                    head = 2 * pair + side
+                    cut = slice(side * BLK, side * BLK + BLK)
+                    lse = st_all[query, head : head + 1, :]
+                    delta = st_all[query, OWN_HEADS + head : OWN_HEADS + head + 1, :]
+                    prob = jnp.exp2(scores[:, cut] * (SCALE * LOG2E) - lse)
+                    p_buf[pair, :, cut] = prob.astype(BF16)
+                    ds_buf[pair, :, cut] = (prob * (dprob[:, cut] - delta)).astype(BF16)
+
+            def backward(pair):
+                lanes = slice(pair * 128, pair * 128 + 128)
+                queries = q_all[query, :, lanes]
+                douts = do_all[query, :, lanes]
+                q_two = jnp.concatenate([queries * first_half, queries * second_half], axis=0)
+                do_two = jnp.concatenate([douts * first_half, douts * second_half], axis=0)
+                dv_sum[:, lanes] += lax.dot_general(
+                    p_buf[pair], do_two, nn, preferred_element_type=F32
+                )
+                dk_sum[:, lanes] += lax.dot_general(
+                    ds_buf[pair], q_two, nn, preferred_element_type=F32
+                )
+                both = lax.dot_general(
+                    k_turned[lanes, :], ds_buf[pair], nn, preferred_element_type=F32
+                )
+                for side in range(2):
+                    low = pair * 128 + side * 64
+                    dq_sum[query, low : low + 64, :] += both[
+                        side * 64 : side * 64 + 64, side * BLK : side * BLK + BLK
+                    ]
+
+            for pair in range(HEAD_PAIRS):
+                forward(pair)
+            for pair in range(HEAD_PAIRS):
+                backward(pair)
+            return carry
+
+        @pl.when(have > 0)
         def _():
             dk_sum[...] = jnp.zeros_like(dk_sum)
             dv_sum[...] = jnp.zeros_like(dv_sum)
             for pair in range(HEAD_PAIRS):
                 lanes = slice(pair * 128, pair * 128 + 128)
-                turned = jnp.transpose(k_buf[slot, :, lanes].astype(F32)).astype(BF16)
+                turned = jnp.transpose(k_all[up, across, :, lanes].astype(F32)).astype(BF16)
                 k_turned[lanes, :] = turned
-
-        def forward(pair):
-            lanes = slice(pair * 128, pair * 128 + 128)
-            keys = k_buf[slot, :, lanes]
-            values = v_buf[slot, :, lanes]
-            queries = q_buf[slot, :, lanes]
-            douts = do_buf[slot, :, lanes]
-            q_two = jnp.concatenate([queries * first_half, queries * second_half], axis=0)
-            do_two = jnp.concatenate([douts * first_half, douts * second_half], axis=0)
-            scores = lax.dot_general(keys, q_two, nt, preferred_element_type=F32)
-            dprob = lax.dot_general(values, do_two, nt, preferred_element_type=F32)
-            probs, dscores = [], []
-            for side in range(2):
-                head = 2 * pair + side
-                cut = slice(side * BLK, side * BLK + BLK)
-                lse = st_buf[slot, head : head + 1, :]
-                delta = st_buf[slot, OWN_HEADS + head : OWN_HEADS + head + 1, :]
-                prob = jnp.exp2(scores[:, cut] * (SCALE * LOG2E) - lse)
-                probs.append(prob.astype(BF16))
-                dscores.append((prob * (dprob[:, cut] - delta)).astype(BF16))
-            p_buf[pair] = jnp.concatenate(probs, axis=1)
-            ds_buf[pair] = jnp.concatenate(dscores, axis=1)
-
-        def backward(pair):
-            lanes = slice(pair * 128, pair * 128 + 128)
-            queries = q_buf[slot, :, lanes]
-            douts = do_buf[slot, :, lanes]
-            q_two = jnp.concatenate([queries * first_half, queries * second_half], axis=0)
-            do_two = jnp.concatenate([douts * first_half, douts * second_half], axis=0)
-            dv_sum[:, lanes] += lax.dot_general(p_buf[pair], do_two, nn, preferred_element_type=F32)
-            dk_sum[:, lanes] += lax.dot_general(ds_buf[pair], q_two, nn, preferred_element_type=F32)
-            turned = k_turned[lanes, :]
-            both = lax.dot_general(turned, ds_buf[pair], nn, preferred_element_type=F32)
-            for side in range(2):
-                low = pair * 128 + side * 64
-                dq_sum[query, low : low + 64, :] += both[
-                    side * 64 : side * 64 + 64, side * BLK : side * BLK + BLK
-                ]
-
-        for pair in range(HEAD_PAIRS):
-            forward(pair)
-        for pair in range(HEAD_PAIRS):
-            backward(pair)
-
-        @pl.when(after != block)
-        def _():
-            stage = lax.rem(flushed, 2)
-
-            @pl.when(flushed >= 2)
-            def _():
-                for copy in flush_copies(stage, block):
-                    copy.wait()
-
-            dk_stage[stage] = (dk_sum[...] * SCALE).astype(BF16)
-            dv_stage[stage] = dv_sum[...].astype(BF16)
-            for copy in flush_copies(stage, block):
-                copy.start()
-
-        return flushed + jnp.where(after != block, 1, 0)
-
-    flushed = lax.fori_loop(0, total, step, 0)
+            lax.fori_loop(0, have, used, 0)
+            dk_out[up, across] = (dk_sum[...] * SCALE).astype(BF16)
+            dv_out[across, up] = dv_sum[...].astype(BF16)
+
+        return carry
+
+    lax.fori_loop(0, KEY_BLOCKS, key_block, 0)
 
     def turn_in(query, carry):
-        dq_stage[query] = (dq_sum[query] * SCALE).astype(BF16)
-        pltpu.make_async_copy(dq_stage.at[query], dq_out.at[query], dq_sems.at[query]).start()
+        dq_out[query] = (dq_sum[query] * SCALE).astype(BF16)
         return carry
 
     lax.fori_loop(0, QUERY_BLOCKS, turn_in, 0)
-    for slot in range(2):
-
-        @pl.when(flushed > slot)
-        def _(slot=slot):
-            for copy in flush_copies(slot, 0):
-                copy.wait()
-
-    for block in range(KEY_BLOCKS):
-        up, across = divmod(block, NX)
-
-        @pl.when(filled[block] == 0)
-        def _(up=up, across=across):
-            pltpu.make_async_copy(zeros, dk_out.at[up, across], zero_sems.at[0]).wait()
-            pltpu.make_async_copy(zeros, dv_out.at[across, up], zero_sems.at[1]).wait()
-
-    def finish(query, carry):
-        pltpu.make_async_copy(dq_stage.at[query], dq_out.at[query], dq_sems.at[query]).wait()
-        return carry
-
-    lax.fori_loop(0, QUERY_BLOCKS, finish, 0)
 
 
 def pairs_over_blocks(q_all, do_all, st_all, k_all, v_all, lists, counts, place):
     smem = pl.BlockSpec(memory_space=pltpu.SMEM)
-    block_pair = pltpu.VMEM((2, BLK, COLS), BF16)
     return pl.pallas_call(
         pair_kernel,
         out_shape=[
@@ -489,31 +414,17 @@
             jax.ShapeDtypeStruct((NY, NX, BLK, COLS), BF16),
             jax.ShapeDtypeStruct((NX, NY, BLK, COLS), BF16),
         ],
-        in_specs=[smem] * 3 + [ANY] * 5,
-        out_specs=[ANY] * 3,
+        in_specs=[smem] * 3 + [VMEM] * 5,
+        out_specs=[VMEM] * 3,
         scratch_shapes=[
-            block_pair,
-            block_pair,
-            pltpu.VMEM((2, 2 * OWN_HEADS, BLK), F32),
-            block_pair,
-            block_pair,
             pltpu.VMEM((COLS, BLK), BF16),
             pltpu.VMEM((HEAD_PAIRS, BLK, 2 * BLK), BF16),
             pltpu.VMEM((HEAD_PAIRS, BLK, 2 * BLK), BF16),
             pltpu.VMEM((QUERY_BLOCKS, COLS, BLK), F32),
             pltpu.VMEM((BLK, COLS), F32),
             pltpu.VMEM((BLK, COLS), F32),
-            pltpu.VMEM((QUERY_BLOCKS, COLS, BLK), BF16),
-            block_pair,
-            block_pair,
-            pltpu.VMEM((BLK, COLS), BF16),
             pltpu.SMEM((KEY_BLOCKS * BUCKET,), jnp.int32),
             pltpu.SMEM((KEY_BLOCKS,), jnp.int32),
-            pltpu.SMEM((KEY_BLOCKS * QUERY_BLOCKS,), jnp.int32),
-            pltpu.SemaphoreType.DMA((2, 5)),
-            pltpu.SemaphoreType.DMA((2, 2)),
-            pltpu.SemaphoreType.DMA((2,)),
-            pltpu.SemaphoreType.DMA((QUERY_BLOCKS,)),
         ],
         compiler_params=pltpu.CompilerParams(vmem_limit_bytes=VMEM_LIMIT),
         name="used_pairs",
@@ -537,31 +448,13 @@
     dq_part, dk_part, dv_part,
     gq_out, gk_out, gv_out,
     dq_own, dq_in_up, dq_in_down, dq_end,
-    k_own, k_far, k_near, k_mid, k_mid_far, k_end,
-    v_own, v_far, v_near, v_mid, v_mid_far, v_end,
-    send_sems, recv_sems, local_sems, q_end_sems, k_end_sems, v_end_sems,
+    k_out, k_far, k_near, k_mid, k_mid_far, k_end,
+    v_out, v_far, v_near, v_mid, v_mid_far, v_end,
+    send_sems, recv_sems, q_end_sems, k_end_sems, v_end_sems,
 ):
     me = Place()
     x, y, z, core = me.x, me.y, me.z, me.core
-    loads = []
-
-    def load(source, target):
-        copy = pltpu.make_async_copy(source, target, local_sems.at[len(loads)])
-        copy.start()
-        loads.append(copy)
-
     first, second = pl.ds(0, 2), pl.ds(2, 2)
-    load(dq_part.at[me.zs(3), 0], dq_own.at[me.zs(3), 0])
-    load(dq_part.at[me.zs(-3), 1], dq_own.at[me.zs(-3), 1])
-    load(dk_part.at[me.ys(1), first], k_own.at[me.ys(1), first])
-    load(dv_part.at[me.xs(1), first], v_own.at[me.xs(1), first])
-    load(dk_part.at[me.ys(-1), second], k_own.at[me.ys(-1), second])
-    load(dv_part.at[me.xs(-1), second], v_own.at[me.xs(-1), second])
-    for step in (2, -2, 1, -1):
-        load(dq_part.at[me.zs(step)], dq_own.at[me.zs(step)])
-    load(dk_part.at[y], k_own.at[y])
-    load(dv_part.at[x], v_own.at[x])
-    load(dq_part.at[z, core], dq_end.at[2, core])
     me.greet(both_cores=True)
     send = Sender(send_sems, recv_sems)
     up, down = me.over_z(1), me.over_z(-1)
@@ -604,31 +497,29 @@
             side, step, inbox, way = 1, hop - 4, dq_in_down, -1
         own = dq_own.at[me.zs(step), shard]
         arrive[direction, shard, hop].wait_recv()
-        add_rows(own, [own, inbox.at[hop - 1, shard]], COLS)
+        add_rows(own, [dq_part.at[me.zs(step), shard], inbox.at[hop - 1, shard]], COLS)
         if hop < 3:
             arrive[direction, shard, hop + 1] = send(own, inbox.at[hop, shard], me.over_z(way))
         else:
             send(own, dq_end.at[side, core], me.over_z(way, owner=shard), q_end_sems.at[side, core])
 
-    for copy in loads:
-        copy.wait()
+    add_rows(dq_end.at[2, core], [dq_part.at[z, core]], COLS)
     hop_q("up", 0, 1)
     hop_q("down", 1, 1)
 
-    def onward(arrival, own, place, base, inbox):
+    def onward(arrival, part, place, base, inbox, outbox):
         arrival.wait_recv()
         for row in range(2):
-            part = own.at[place, base + row]
-            add_rows(part, [part, inbox.at[row]], BLK)
-
-    onward(k_a, k_own, me.ys(1), 0, k_far.at[0])
-    k_in.append(send(k_own.at[me.ys(1), first], k_near.at[0, first], me.over_y(1)))
-    onward(v_a, v_own, me.xs(1), 0, v_far.at[0])
-    v_in.append(send(v_own.at[me.xs(1), first], v_near.at[0, first], me.over_x(1)))
-    onward(k_b, k_own, me.ys(-1), 2, k_far.at[1])
-    k_in.append(send(k_own.at[me.ys(-1), second], k_near.at[1, second], me.over_y(-1)))
-    onward(v_b, v_own, me.xs(-1), 2, v_far.at[1])
-    v_in.append(send(v_own.at[me.xs(-1), second], v_near.at[1, second], me.over_x(-1)))
+            add_rows(outbox.at[row], [part.at[place, base + row], inbox.at[row]], BLK)
+
+    onward(k_a, dk_part, me.ys(1), 0, k_far.at[0], k_out.at[0])
+    k_in.append(send(k_out.at[0], k_near.at[0, first], me.over_y(1)))
+    onward(v_a, dv_part, me.xs(1), 0, v_far.at[0], v_out.at[0])
+    v_in.append(send(v_out.at[0], v_near.at[0, first], me.over_x(1)))
+    onward(k_b, dk_part, me.ys(-1), 2, k_far.at[1], k_out.at[1])
+    k_in.append(send(k_out.at[1], k_near.at[1, second], me.over_y(-1)))
+    onward(v_b, dv_part, me.xs(-1), 2, v_far.at[1], v_out.at[1])
+    v_in.append(send(v_out.at[1], v_near.at[1, second], me.over_x(-1)))
     for hop, shard in ((2, 1), (2, 0), (3, 1), (3, 0)):
         hop_q("up", shard, hop)
         hop_q("down", 1 - shard, hop)
@@ -657,10 +548,10 @@
         send(part, end.at[side, core], device, sems.at[side, core])
 
     kx_a, kx_b = turn(
-        k_in, k_own, y, k_near, k_mid, k_mid_far, k_end, k_end_sems, me.xs, me.over_x, x
+        k_in, dk_part, y, k_near, k_mid, k_mid_far, k_end, k_end_sems, me.xs, me.over_x, x
     )
     vy_a, vy_b = turn(
-        v_in, v_own, x, v_near, v_mid, v_mid_far, v_end, v_end_sems, me.ys, me.over_y, y
+        v_in, dv_part, x, v_near, v_mid, v_mid_far, v_end, v_end_sems, me.ys, me.over_y, y
     )
     last(kx_a, k_mid, me.xs(1), 0, k_mid_far.at[0], k_end, k_end_sems, 0, me.over_x(1, owner=0))
     last(kx_b, k_mid, me.xs(-1), 1, k_mid_far.at[1], k_end, k_end_sems, 1, me.over_x(-1, owner=1))
@@ -694,14 +585,12 @@
 
 
 def reduce_parts(dq_part, dk_part, dv_part):
-    line = pltpu.VMEM((4, 4, BLK, COLS), BF16)
     two = pltpu.VMEM((2, 2, BLK, COLS), BF16)
     near = pltpu.VMEM((2, 4, BLK, COLS), BF16)
     four = pltpu.VMEM((4, BLK, COLS), BF16)
     half = pltpu.VMEM((2, HALF, COLS), BF16)
     end = pltpu.VMEM((3, CORES, HALF, COLS), BF16)
     inbox = pltpu.VMEM((3, CORES, COLS, BLK), BF16)
-    vmem = pl.BlockSpec(memory_space=pltpu.VMEM)
     sems = pltpu.SemaphoreType.DMA((3, CORES))
     return pl.pallas_call(
         reduce_kernel,
@@ -710,15 +599,14 @@
             jax.ShapeDtypeStruct((HALF, WIDTH), BF16),
             jax.ShapeDtypeStruct((HALF, WIDTH), BF16),
         ],
-        in_specs=[ANY] * 3,
-        out_specs=[vmem] * 3,
+        in_specs=[VMEM] * 3,
+        out_specs=[VMEM] * 3,
         scratch_shapes=[
             pltpu.VMEM((NZ, CORES, COLS, BLK), BF16), inbox, inbox, inbox,
-            line, two, near, four, half, end,
-            line, two, near, four, half, end,
+            two, two, near, four, half, end,
+            two, two, near, four, half, end,
             pltpu.SemaphoreType.DMA((REDUCE_COPIES,)),
             pltpu.SemaphoreType.DMA((REDUCE_COPIES,)),
-            pltpu.SemaphoreType.DMA((13,)),
             sems, sems, sems,
         ],
         compiler_params=pltpu.CompilerParams(
@@ -732,7 +620,8 @@
     ka = lax.axis_index("ka")
     place = jnp.stack([ka // NZ, ka % NZ]).astype(jnp.int32)
     lists = block_pairs.transpose(0, 2, 3, 1).reshape(2 * SLOTS, KEY_SHARDS)
-    gathered = gather(q, do, k, v, out, lse, lists, counts)
+    held = [pltpu.with_memory_space_constraint(array, pltpu.HBM) for array in (q, do, k, v, out, lse, lists, counts)]
+    gathered = gather(*held)
     parts = pairs_over_blocks(*gathered, place)
     return tuple(reduce_parts(*parts))
 

time: 126 us -> 105 us (0.83); the launches traced: 124 us -> 105 us
  Pallas kernels: 118 us -> 102 us
  local copies, waits for them, and re-layouts: 4.8 us -> 2.01 us
    pallas_call x1, Pallas kernels: 17.3 us -> 11.4 us  [pairs_over_blocks(): pl.pallas_call(pair_kernel, out_shape=[jax.ShapeDtypeStruct((QUERY_BLOCKS...]
    pallas_call x1, Pallas kernels: 44.4 us -> 39 us  [reduce_parts(): pl.pallas_call(reduce_kernel, out_shape=[jax.ShapeDtypeStruct((BLK, WIDTH...]
    pallas_call x1, Pallas kernels: 56.2 us -> 51.9 us  [gather(): pl.pallas_call(gather_kernel, out_shape=[jax.ShapeDtypeStruct((NZ, CORES,...]
    unnamed x3, local copies, waits for them, and re-layouts: 4.8 us -> 2.01 us
where the time goes in v4:
time: 105 us
  Pallas kernels  102 us (97%)
  local copies, waits for them, and re-layouts  2.01 us (2%)
    pallas_call x1, Pallas kernels, gather(): pl.pallas_call(gather_kernel, out_shape=[jax.ShapeDtypeStruct((NZ, CORES,...  51.9 us
    pallas_call x1, Pallas kernels, reduce_parts(): pl.pallas_call(reduce_kernel, out_shape=[jax.ShapeDtypeStruct((BLK, WIDTH...  39 us
    pallas_call x1, Pallas kernels, pairs_over_blocks(): pl.pallas_call(pair_kernel, out_shape=[jax.ShapeDtypeStruct((QUERY_BLOCKS...  11.4 us

profile of v4, /device:TPU:1, one launch (start us, length us, event | category | flops | bytes accessed | tf_op | source)
XLA Modules:
  0.0 105.0 jit_solution(448615416530138609)
XLA Ops:
  0.7 0.1 pad_add_fusion.place
  0.7 51.9 %gather_blocks.1 = (bf16[8,2,128,512]{3,2,1,0:T(8,128)(2,1)S(1)}, bf16[8,2,128,512]{3,2,1,0:T(8,128)(2,1)S(1)}, f32[8,2,16,128]{3,2,1,0:T(8,128)S(1)}, bf16[4,4,...) custom-call(bf16[128,1024]{1,0:T(8,128)(2,1)} %q_ref.1, ...), custom_call_target="tpu_custom_call" | custom-call | tf_op jit(solution)/shard_map/gather_blocks/pallas_call | solution.py:263
  52.6 11.4 %used_pairs.1 = (bf16[16,512,128]{2,1,0:T(8,128)(2,1)S(1)}, bf16[4,4,128,512]{3,2,1,0:T(8,128)(2,1)S(1)}, bf16[4,4,128,512]{3,2,1,0:T(8,128)(2,1)S(1)}) custom-call(s32[2,48,32]{2,1,0:T(8,128)S(1)} %get-tuple-element.13.lists, s32[2,1,32]{2,1,0:T(1,128)S(1)} %get-tuple-element.14.counts, s32[2]{0:T(128)S(1)} %pad_add_fusion.place, ...), custom_call_target="tpu_custom_call" | custom-call | tf_op jit(solution)/shard_map/used_pairs/pallas_call | solution.py:410
  64.0 39.0 %reduce_parts.1 = (bf16[128,1024]{1,0:T(8,128)(2,1)S(1)}, bf16[64,1024]{1,0:T(8,128)(2,1)S(1)}, bf16[64,1024]{1,0:T(8,128)(2,1)S(1)}) custom-call(bf16[8,2,512,128]{3,2,1,0:T(8,128)(2,1)S(1)} %bitcast.9, bf16[4,4,128,512]{3,2,1,0:T(8,128)(2,1)S(1)} %get-tuple-element.21.dk_part, bf16[4,4,128,512]{3,2,1,0:T(8,128)(2,1)S(1)} %get-tuple-element.22.dv_part), custom_call_target="tpu_custom_call" | custom-call | tf_op jit(solution)/shard_map/reduce_parts/pallas_call | solution.py:595
  103.0 0.7 copy.14
  103.7 0.7 copy.15
  104.4 0.7 copy.16

commit v5 on v4

--- a/solution.py
+++ b/solution.py
@@ -17,11 +17,16 @@
 KEY_SHARDS = NX * NZ
 QUERY_BLOCKS = NZ * CORES
 KEY_BLOCKS = NX * NY
-BUCKET = 32
+CELLS = KEY_BLOCKS * QUERY_BLOCKS
+NEAR = 5
+EARLY = 20
+FIRST_EARLY = 8
+TABLE = (8, 128)
 SCALE = 64**-0.5
 LOG2E = 1.4426950408889634
 VMEM_LIMIT = 24 << 20
-GATHER_LIMIT = 24 << 20
+GATHER_LIMIT = 16 << 20
+PAIR_LIMIT = 16 << 20
 MESH = pl.DeviceIdType.MESH
 HBM = pl.BlockSpec(memory_space=pltpu.HBM)
 VMEM = pl.BlockSpec(memory_space=pltpu.VMEM)
@@ -99,6 +104,119 @@
             copy.wait_send()
 
 
+NT = (((1,), (1,)), ((), ()))
+NN = (((1,), (0,)), ((), ()))
+
+
+def pair_lanes(pair):
+    return slice(pair * 128, pair * 128 + 128)
+
+
+def head_halves():
+    lane = lax.broadcasted_iota(jnp.int32, (1, 128), 1)
+    return (
+        jnp.where(lane < 64, 1.0, 0.0).astype(BF16),
+        jnp.where(lane < 64, 0.0, 1.0).astype(BF16),
+    )
+
+
+def both_heads(block, halves):
+    return jnp.concatenate([block * halves[0], block * halves[1]], axis=0)
+
+
+def turn_keys(keys, k_turned):
+    for pair in range(HEAD_PAIRS):
+        turned = jnp.transpose(keys(pair_lanes(pair)).astype(F32)).astype(BF16)
+        k_turned[pair_lanes(pair), :] = turned
+
+
+def pair_products(keys, values, queries, douts, stats, halves, p_buf, ds_buf, keep=None):
+    for pair in range(HEAD_PAIRS):
+        lanes = pair_lanes(pair)
+        scores = lax.dot_general(
+            keys(lanes), both_heads(queries(lanes), halves), NT, preferred_element_type=F32
+        )
+        dprob = lax.dot_general(
+            values(lanes), both_heads(douts(lanes), halves), NT, preferred_element_type=F32
+        )
+        for side in range(2):
+            head = 2 * pair + side
+            cut = slice(side * BLK, side * BLK + BLK)
+            prob = jnp.exp2(scores[:, cut] * (SCALE * LOG2E) - stats(head))
+            if keep is not None:
+                prob = jnp.where(keep, prob, 0.0)
+            p_buf[pair, :, cut] = prob.astype(BF16)
+            ds_buf[pair, :, cut] = (prob * (dprob[:, cut] - stats(OWN_HEADS + head))).astype(BF16)
+
+
+def pair_gradients(queries, douts, halves, p_buf, ds_buf, k_turned, add_dv, add_dk, add_dq):
+    for pair in range(HEAD_PAIRS):
+        lanes = pair_lanes(pair)
+        add_dv(
+            lanes,
+            lax.dot_general(
+                p_buf[pair], both_heads(douts(lanes), halves), NN, preferred_element_type=F32
+            ),
+        )
+        add_dk(
+            lanes,
+            lax.dot_general(
+                ds_buf[pair], both_heads(queries(lanes), halves), NN, preferred_element_type=F32
+            ),
+        )
+        both = lax.dot_general(k_turned[lanes, :], ds_buf[pair], NN, preferred_element_type=F32)
+        for side in range(2):
+            rows = slice(side * 64, side * 64 + 64)
+            low = pair * 128 + side * 64
+            add_dq(slice(low, low + 64), both[rows, side * BLK : side * BLK + BLK])
+
+
+def tabulate(lists, counts, x, z, table):
+    cell = lax.broadcasted_iota(jnp.int32, (CELLS, KEY_SHARDS), 0)
+    shard = lax.broadcasted_iota(jnp.int32, (SLOTS, KEY_SHARDS), 1)
+    slot = lax.broadcasted_iota(jnp.int32, (SLOTS, KEY_SHARDS), 0)
+    used = jnp.zeros((CELLS, KEY_SHARDS), F32)
+    for owner in range(CORES):
+        queries = lists[owner, 0:SLOTS, :]
+        blocks = lists[owner, SLOTS : 2 * SLOTS, :]
+        column = lax.shift_right_logical(shard, 3)
+        ok = (slot < counts[owner]) & ((shard & 7) == z) & (lax.shift_right_logical(queries, 3) == x)
+        code = (blocks * NX + column) * QUERY_BLOCKS + (queries & 7) * CORES + owner
+        code = jnp.where(ok, code, -1)
+        for row in range(SLOTS):
+            used = jnp.where(cell == code[row : row + 1, :], 1.0, used)
+    used = jnp.max(used, axis=1, keepdims=True)
+    order = lax.broadcasted_iota(jnp.int32, (CELLS, 1), 0)
+    away = (lax.shift_right_logical(order & 15, 1) - z + 2 + NZ) & 7
+    near = jnp.where(away < NEAR, used, 0.0)
+    before = lax.broadcasted_iota(jnp.int32, (CELLS, CELLS), 0)
+    before = before > lax.broadcasted_iota(jnp.int32, (CELLS, CELLS), 1)
+    before = jnp.where(before, 1.0, 0.0).astype(BF16)
+    spread = jnp.zeros((CELLS, 128), F32)
+    near_rank = lax.dot_general(before, (near + spread).astype(BF16), NN, preferred_element_type=F32)
+    early = jnp.where(near_rank < EARLY, near + spread, 0.0)
+    others = (used + spread) - early
+    other_rank = lax.dot_general(before, others.astype(BF16), NN, preferred_element_type=F32)
+    lane = lax.broadcasted_iota(jnp.int32, (CELLS, 128), 1)
+    line = lax.broadcasted_iota(jnp.int32, (CELLS, 128), 0)
+    number = line.astype(F32)
+
+    def total(values):
+        return jnp.sum(values, axis=0, keepdims=True)
+
+    place = lane.astype(F32)
+    rows = [
+        total(jnp.where(near_rank == place, early * number, 0.0)),
+        total(jnp.where(other_rank == place, others * number, 0.0)),
+        total(jnp.where(other_rank == place + 128.0, others * number, 0.0)),
+        total(jnp.where(line < lane * QUERY_BLOCKS, early, 0.0)),
+        total(jnp.where(line < lane * QUERY_BLOCKS, others, 0.0)),
+    ]
+    table[...] = jnp.zeros(TABLE, jnp.int32)
+    for index, row in enumerate(rows):
+        table[index : index + 1, :] = row.astype(jnp.int32)
+
+
 def half_of(core, size):
     return pl.ds(pl.multiple_of(core * size, size), size)
 
@@ -108,8 +226,9 @@
 
 def gather_kernel(
     q_ref, do_ref, k_ref, v_ref, out_ref, lse_ref, list_ref, count_ref,
-    q_all, do_all, st_all, k_all, v_all, list_all, count_all,
-    do_buf, out_buf, lse_buf, st_buf, send_sems, recv_sems, local_sems,
+    q_all, do_all, st_all, k_all, v_all, table_out, dk_early, dv_early, dq_early,
+    do_buf, out_buf, lse_buf, st_buf, list_all, count_all, q_near, do_near, st_near,
+    k_turned, p_buf, ds_buf, table, table_s, send_sems, recv_sems, local_sems, near_sems,
 ):
     me = Place()
     x, y, z, core = me.x, me.y, me.z, me.core
@@ -180,6 +299,16 @@
         st_buf[side, OWN_HEADS : 2 * OWN_HEADS, :] = delta[heads, :]
     for own in owns:
         own.wait()
+    nears = []
+
+    def bring_near(arrays, distance):
+        for blocks, held in arrays:
+            copy = pltpu.make_async_copy(
+                blocks.at[me.zs(distance)], held.at[distance + 2], near_sems.at[len(nears)]
+            )
+            copy.start()
+            nears.append(copy)
+
     st_own = pltpu.make_async_copy(st_buf.at[core], st_all.at[z, core], local_sems.at[0])
     st_own.start()
     swaps.append(send(st_buf.at[1 - core], st_all.at[z, core], me.sibling))
@@ -225,10 +354,21 @@
 
     forward(1, 1, q_all, q_up)
     forward(1, -1, do_all, do_down)
+    arrived(swaps)
+    st_own.wait()
+    tabulate(list_all, count_all, x, z, table)
+    to_scalars = pltpu.make_async_copy(table, table_s, local_sems.at[1])
+    to_scalars.start()
+    table_store = pltpu.make_async_copy(table, table_out, local_sems.at[2])
+    table_store.start()
+    every_array = ((q_all, q_near), (do_all, do_near), (st_all, st_near))
+    bring_near(every_array, 0)
     forward(1, 1, do_all, do_up)
     forward(1, -1, q_all, q_down)
     forward(1, 1, st_all, st_up)
     forward(1, -1, st_all, st_down)
+    bring_near(every_array, 1)
+    bring_near(every_array, -1)
 
     def across(blocks, start, low, device):
         part = blocks.at[start, pl.ds(low, 2)]
@@ -250,11 +390,60 @@
     forward(2, 1, st_all, st_up)
     forward(2, -1, st_all, st_down)
 
+    bring_near(every_array, 2)
+    bring_near(every_array, -2)
     forward(3, 1, q_all, q_up)
     forward(3, -1, do_all, do_down)
+    arrived(k_far, v_far)
+    for copy in nears:
+        copy.wait()
+    to_scalars.wait()
+    halves = head_halves()
+    used = table_s[3, KEY_BLOCKS]
+
+    def early(index, carry):
+        entry = jnp.clip(table_s[0, index], 0, CELLS - 1)
+        block = lax.div(entry, QUERY_BLOCKS)
+        up_block, across_block = lax.div(block, NX), lax.rem(block, NX)
+        query = lax.rem(lax.div(lax.rem(entry, QUERY_BLOCKS), CORES) - z + 2 + NZ, NZ)
+        query = jnp.minimum(query, NEAR - 1)
+        owner = lax.rem(entry, CORES)
+
+        def keys(lanes):
+            return k_all[up_block, across_block, :, lanes]
+
+        def values(lanes):
+            return v_all[across_block, up_block, :, lanes]
+
+        def queries(lanes):
+            return q_near[query, owner, :, lanes]
+
+        def douts(lanes):
+            return do_near[query, owner, :, lanes]
+
+        def stats(row):
+            return st_near[query, owner, row : row + 1, :]
+
+        turn_keys(keys, k_turned)
+        pair_products(keys, values, queries, douts, stats, halves, p_buf, ds_buf, keep=index < used)
+
+        def put_dv(lanes, value):
+            dv_early[index, :, lanes] = value
+
+        def put_dk(lanes, value):
+            dk_early[index, :, lanes] = value
+
+        def put_dq(rows, value):
+            dq_early[index, rows, :] = value
+
+        pair_gradients(queries, douts, halves, p_buf, ds_buf, k_turned, put_dv, put_dk, put_dq)
+        return carry
+
+    lax.fori_loop(0, FIRST_EARLY, early, 0)
     forward(3, 1, st_all, st_up)
-    arrived(k_far, v_far, swaps, do_up[2], q_down[2], st_down[2], q_up[3], do_down[3], st_up[3])
-    st_own.wait()
+    lax.fori_loop(FIRST_EARLY, EARLY, early, 0)
+    arrived(do_up[2], q_down[2], st_down[2], q_up[3], do_down[3], st_up[3])
+    table_store.wait()
     send.finish()
     assert len(send.copies) == GATHER_COPIES, len(send.copies)
 
@@ -268,19 +457,32 @@
             jax.ShapeDtypeStruct((NZ, CORES, 2 * OWN_HEADS, BLK), F32),
             jax.ShapeDtypeStruct((NY, NX, BLK, COLS), BF16),
             jax.ShapeDtypeStruct((NX, NY, BLK, COLS), BF16),
-            jax.ShapeDtypeStruct((CORES, 2 * SLOTS, KEY_SHARDS), jnp.int32),
-            jax.ShapeDtypeStruct((CORES, 1, KEY_SHARDS), jnp.int32),
+            jax.ShapeDtypeStruct(TABLE, jnp.int32),
+            jax.ShapeDtypeStruct((EARLY, BLK, COLS), F32),
+            jax.ShapeDtypeStruct((EARLY, BLK, COLS), F32),
+            jax.ShapeDtypeStruct((EARLY, COLS, BLK), F32),
         ],
         in_specs=[HBM] * 8,
-        out_specs=[VMEM] * 5 + [HBM] * 2,
+        out_specs=[VMEM] * 5 + [HBM] + [VMEM] * 3,
         scratch_shapes=[
             pltpu.VMEM((BLK, WIDTH), BF16),
             pltpu.VMEM((BLK, WIDTH), BF16),
             pltpu.VMEM((HEADS, BLK), F32),
             pltpu.VMEM((CORES, 2 * OWN_HEADS, BLK), F32),
+            pltpu.VMEM((CORES, 2 * SLOTS, KEY_SHARDS), jnp.int32),
+            pltpu.VMEM((CORES, 1, KEY_SHARDS), jnp.int32),
+            pltpu.VMEM((NEAR, CORES, BLK, COLS), BF16),
+            pltpu.VMEM((NEAR, CORES, BLK, COLS), BF16),
+            pltpu.VMEM((NEAR, CORES, 2 * OWN_HEADS, BLK), F32),
+            pltpu.VMEM((COLS, BLK), BF16),
+            pltpu.VMEM((HEAD_PAIRS, BLK, 2 * BLK), BF16),
+            pltpu.VMEM((HEAD_PAIRS, BLK, 2 * BLK), BF16),
+            pltpu.VMEM(TABLE, jnp.int32),
+            pltpu.SMEM(TABLE, jnp.int32),
             pltpu.SemaphoreType.DMA((GATHER_COPIES,)),
             pltpu.SemaphoreType.DMA((GATHER_COPIES,)),
             pltpu.SemaphoreType.DMA((9,)),
+            pltpu.SemaphoreType.DMA((3 * NEAR,)),
         ],
         compiler_params=pltpu.CompilerParams(
             collective_id=0, has_side_effects=True, vmem_limit_bytes=GATHER_LIMIT
@@ -290,107 +492,78 @@
 
 
 def pair_kernel(
-    lists, counts, place, q_all, do_all, st_all, k_all, v_all,
+    table, q_all, do_all, st_all, k_all, v_all, dk_early, dv_early, dq_early,
     dq_out, dk_out, dv_out,
-    k_turned, p_buf, ds_buf, dq_sum, dk_sum, dv_sum, listed, filled,
+    k_turned, p_buf, ds_buf, dq_sum, dk_sum, dv_sum,
 ):
-    x = place[0]
-    z = place[1]
-    for block in range(KEY_BLOCKS):
-        filled[block] = 0
-    for owner in range(CORES):
-        for column in range(NX):
-            shard = column * NZ + z
-
-            def enlist(slot, carry, owner=owner, column=column, shard=shard):
-                query = lists[owner, slot, shard]
-                block = lists[owner, SLOTS + slot, shard] * NX + column
-                have = filled[block]
-                listed[block * BUCKET + have] = lax.rem(query, NZ) * CORES + owner
-                filled[block] = have + jnp.where(lax.div(query, NZ) == x, 1, 0)
-                return carry
-
-            lax.fori_loop(0, counts[owner, 0, shard], enlist, 0)
-
     def clear(query, carry):
         dq_sum[query] = jnp.zeros((COLS, BLK), F32)
         return carry
 
     lax.fori_loop(0, QUERY_BLOCKS, clear, 0)
-
-    lane = lax.broadcasted_iota(jnp.int32, (1, 128), 1)
-    first_half = jnp.where(lane < 64, 1.0, 0.0).astype(BF16)
-    second_half = jnp.where(lane < 64, 0.0, 1.0).astype(BF16)
-    nt = (((1,), (1,)), ((), ()))
-    nn = (((1,), (0,)), ((), ()))
+    halves = head_halves()
 
     def key_block(block, carry):
         up, across = lax.div(block, NX), lax.rem(block, NX)
-        have = filled[block]
+        early_low, early_high = table[3, block], table[3, block + 1]
+        low, high = table[4, block], table[4, block + 1]
+        have = (early_high - early_low) + (high - low)
 
         @pl.when(have == 0)
         def _():
             dk_out[up, across] = jnp.zeros((BLK, COLS), BF16)
             dv_out[across, up] = jnp.zeros((BLK, COLS), BF16)
 
+        def keys(lanes):
+            return k_all[up, across, :, lanes]
+
+        def values(lanes):
+            return v_all[across, up, :, lanes]
+
+        def take(slot, carry):
+            query = lax.rem(table[0, slot], QUERY_BLOCKS)
+            dk_sum[...] += dk_early[slot]
+            dv_sum[...] += dv_early[slot]
+            dq_sum[query] += dq_early[slot]
+            return carry
+
         def used(slot, carry):
-            query = listed[block * BUCKET + slot]
-
-            def forward(pair):
-                lanes = slice(pair * 128, pair * 128 + 128)
-                keys = k_all[up, across, :, lanes]
-                values = v_all[across, up, :, lanes]
-                queries = q_all[query, :, lanes]
-                douts = do_all[query, :, lanes]
-                q_two = jnp.concatenate([queries * first_half, queries * second_half], axis=0)
-                do_two = jnp.concatenate([douts * first_half, douts * second_half], axis=0)
-                scores = lax.dot_general(keys, q_two, nt, preferred_element_type=F32)
-                dprob = lax.dot_general(values, do_two, nt, preferred_element_type=F32)
-                for side in range(2):
-                    head = 2 * pair + side
-                    cut = slice(side * BLK, side * BLK + BLK)
-                    lse = st_all[query, head : head + 1, :]
-                    delta = st_all[query, OWN_HEADS + head : OWN_HEADS + head + 1, :]
-                    prob = jnp.exp2(scores[:, cut] * (SCALE * LOG2E) - lse)
-                    p_buf[pair, :, cut] = prob.astype(BF16)
-                    ds_buf[pair, :, cut] = (prob * (dprob[:, cut] - delta)).astype(BF16)
-
-            def backward(pair):
-                lanes = slice(pair * 128, pair * 128 + 128)
-                queries = q_all[query, :, lanes]
-                douts = do_all[query, :, lanes]
-                q_two = jnp.concatenate([queries * first_half, queries * second_half], axis=0)
-                do_two = jnp.concatenate([douts * first_half, douts * second_half], axis=0)
-                dv_sum[:, lanes] += lax.dot_general(
-                    p_buf[pair], do_two, nn, preferred_element_type=F32
-                )
-                dk_sum[:, lanes] += lax.dot_general(
-                    ds_buf[pair], q_two, nn, preferred_element_type=F32
-                )
-                both = lax.dot_general(
-                    k_turned[lanes, :], ds_buf[pair], nn, preferred_element_type=F32
-                )
-                for side in range(2):
-                    low = pair * 128 + side * 64
-                    dq_sum[query, low : low + 64, :] += both[
-                        side * 64 : side * 64 + 64, side * BLK : side * BLK + BLK
-                    ]
-
-            for pair in range(HEAD_PAIRS):
-                forward(pair)
-            for pair in range(HEAD_PAIRS):
-                backward(pair)
+            query = lax.rem(table[1 + lax.div(slot, 128), lax.rem(slot, 128)], QUERY_BLOCKS)
+
+            def queries(lanes):
+                return q_all[query, :, lanes]
+
+            def douts(lanes):
+                return do_all[query, :, lanes]
+
+            def stats(row):
+                return st_all[query, row : row + 1, :]
+
+            pair_products(keys, values, queries, douts, stats, halves, p_buf, ds_buf)
+
+            def add_dv(lanes, value):
+                dv_sum[:, lanes] += value
+
+            def add_dk(lanes, value):
+                dk_sum[:, lanes] += value
+
+            def add_dq(rows, value):
+                dq_sum[query, rows, :] += value
+
+            pair_gradients(queries, douts, halves, p_buf, ds_buf, k_turned, add_dv, add_dk, add_dq)
             return carry
 
         @pl.when(have > 0)
         def _():
             dk_sum[...] = jnp.zeros_like(dk_sum)
             dv_sum[...] = jnp.zeros_like(dv_sum)
-            for pair in range(HEAD_PAIRS):
-                lanes = slice(pair * 128, pair * 128 + 128)
-                turned = jnp.transpose(k_all[up, across, :, lanes].astype(F32)).astype(BF16)
-                k_turned[lanes, :] = turned
-            lax.fori_loop(0, have, used, 0)
+            lax.fori_loop(early_low, early_high, take, 0)
+
+            @pl.when(high > low)
+            def _():
+                turn_keys(keys, k_turned)
+
+            lax.fori_loop(low, high, used, 0)
             dk_out[up, across] = (dk_sum[...] * SCALE).astype(BF16)
             dv_out[across, up] = dv_sum[...].astype(BF16)
 
@@ -405,8 +578,7 @@
     lax.fori_loop(0, QUERY_BLOCKS, turn_in, 0)
 
 
-def pairs_over_blocks(q_all, do_all, st_all, k_all, v_all, lists, counts, place):
-    smem = pl.BlockSpec(memory_space=pltpu.SMEM)
+def pairs_over_blocks(q_all, do_all, st_all, k_all, v_all, table, dk_early, dv_early, dq_early):
     return pl.pallas_call(
         pair_kernel,
         out_shape=[
@@ -414,7 +586,7 @@
             jax.ShapeDtypeStruct((NY, NX, BLK, COLS), BF16),
             jax.ShapeDtypeStruct((NX, NY, BLK, COLS), BF16),
         ],
-        in_specs=[smem] * 3 + [VMEM] * 5,
+        in_specs=[pl.BlockSpec(memory_space=pltpu.SMEM)] + [VMEM] * 8,
         out_specs=[VMEM] * 3,
         scratch_shapes=[
             pltpu.VMEM((COLS, BLK), BF16),
@@ -423,20 +595,19 @@
             pltpu.VMEM((QUERY_BLOCKS, COLS, BLK), F32),
             pltpu.VMEM((BLK, COLS), F32),
             pltpu.VMEM((BLK, COLS), F32),
-            pltpu.SMEM((KEY_BLOCKS * BUCKET,), jnp.int32),
-            pltpu.SMEM((KEY_BLOCKS,), jnp.int32),
         ],
-        compiler_params=pltpu.CompilerParams(vmem_limit_bytes=VMEM_LIMIT),
+        compiler_params=pltpu.CompilerParams(vmem_limit_bytes=PAIR_LIMIT),
         name="used_pairs",
     )(
-        lists,
-        counts,
-        place,
+        table,
         q_all.reshape(QUERY_BLOCKS, BLK, COLS),
         do_all.reshape(QUERY_BLOCKS, BLK, COLS),
         st_all.reshape(QUERY_BLOCKS, 2 * OWN_HEADS, BLK),
         k_all,
         v_all,
+        dk_early,
+        dv_early,
+        dq_early,
     )
 
 
@@ -617,12 +788,10 @@
 
 
 def body(q, k, v, out, do, lse, block_pairs, counts):
-    ka = lax.axis_index("ka")
-    place = jnp.stack([ka // NZ, ka % NZ]).astype(jnp.int32)
     lists = block_pairs.transpose(0, 2, 3, 1).reshape(2 * SLOTS, KEY_SHARDS)
-    held = [pltpu.with_memory_space_constraint(array, pltpu.HBM) for array in (q, do, k, v, out, lse, lists, counts)]
-    gathered = gather(*held)
-    parts = pairs_over_blocks(*gathered, place)
+    arguments = (q, do, k, v, out, lse, lists, counts)
+    held = [pltpu.with_memory_space_constraint(array, pltpu.HBM) for array in arguments]
+    parts = pairs_over_blocks(*gather(*held))
     return tuple(reduce_parts(*parts))
 
 

time: 105 us -> 102 us (0.971)
  Pallas kernels: 102 us -> 99.6 us
    pallas_call x1, Pallas kernels: 11.4 us -> 5.78 us  [pairs_over_blocks(): pl.pallas_call(pair_kernel, out_shape=[jax.ShapeDtypeStruct((QUERY_BLOCKS...]
    pallas_call x1, Pallas kernels: 51.9 us -> 53.6 us  [gather(): pl.pallas_call(gather_kernel, out_shape=[jax.ShapeDtypeStruct((NZ, CORES,...]
    pallas_call x1, Pallas kernels: 39 us -> 40.2 us  [reduce_parts(): pl.pallas_call(reduce_kernel, out_shape=[jax.ShapeDtypeStruct((BLK, WIDTH...]
where the time goes in v5:
time: 102 us
  Pallas kernels  99.6 us (98%)
  local copies, waits for them, and re-layouts  2.01 us (2%)
    pallas_call x1, Pallas kernels, gather(): pl.pallas_call(gather_kernel, out_shape=[jax.ShapeDtypeStruct((NZ, CORES,...  53.6 us
    pallas_call x1, Pallas kernels, reduce_parts(): pl.pallas_call(reduce_kernel, out_shape=[jax.ShapeDtypeStruct((BLK, WIDTH...  40.2 us
    pallas_call x1, Pallas kernels, pairs_over_blocks(): pl.pallas_call(pair_kernel, out_shape=[jax.ShapeDtypeStruct((QUERY_BLOCKS...  5.78 us

profile of v5, /device:TPU:1, one launch (start us, length us, event | category | flops | bytes accessed | tf_op | source)
XLA Modules:
  0.0 102.3 jit_solution(3764798184723155326)
XLA Ops:
  0.6 53.6 %gather_blocks.1 = (bf16[8,2,128,512]{3,2,1,0:T(8,128)(2,1)S(1)}, bf16[8,2,128,512]{3,2,1,0:T(8,128)(2,1)S(1)}, f32[8,2,16,128]{3,2,1,0:T(8,128)S(1)}, bf16[4,4,...) custom-call(bf16[128,1024]{1,0:T(8,128)(2,1)} %q_ref.1, ...), custom_call_target="tpu_custom_call" | custom-call | tf_op jit(solution)/shard_map/gather_blocks/pallas_call | solution.py:452
  54.2 5.8 %used_pairs.1 = (bf16[16,512,128]{2,1,0:T(8,128)(2,1)S(1)}, bf16[4,4,128,512]{3,2,1,0:T(8,128)(2,1)S(1)}, bf16[4,4,128,512]{3,2,1,0:T(8,128)(2,1)S(1)}) custom-call(s32[8,128]{1,0:T(8,128)S(1)} %get-tuple-element.15.table, bf16[16,128,512]{2,1,0:T(8,128)(2,1)S(1)} %bitcast.8, bf16[16,128,512]{2,1,0:T(8,128)(2,1)S(1)} %bitcast.9, ...), custom_call_target="tpu_custom_call" | custom-call | tf_op jit(solution)/shard_map/used_pairs/pallas_call | solution.py:582
  60.0 40.2 %reduce_parts.1 = (bf16[128,1024]{1,0:T(8,128)(2,1)S(1)}, bf16[64,1024]{1,0:T(8,128)(2,1)S(1)}, bf16[64,1024]{1,0:T(8,128)(2,1)S(1)}) custom-call(bf16[8,2,512,128]{3,2,1,0:T(8,128)(2,1)S(1)} %bitcast.7, bf16[4,4,128,512]{3,2,1,0:T(8,128)(2,1)S(1)} %get-tuple-element.25.dk_part, bf16[4,4,128,512]{3,2,1,0:T(8,128)(2,1)S(1)} %get-tuple-element.26.dv_part), custom_call_target="tpu_custom_call" | custom-call | tf_op jit(solution)/shard_map/reduce_parts/pallas_call | solution.py:766
  100.3 0.7 copy.14
  101.0 0.7 copy.15
  101.6 0.7 copy.16

commit v6 on v5

--- a/solution.py
+++ b/solution.py
@@ -20,7 +20,7 @@
 CELLS = KEY_BLOCKS * QUERY_BLOCKS
 NEAR = 5
 EARLY = 20
-FIRST_EARLY = 8
+FIRST_EARLY = 9
 TABLE = (8, 128)
 SCALE = 64**-0.5
 LOG2E = 1.4426950408889634
@@ -221,7 +221,7 @@
     return pl.ds(pl.multiple_of(core * size, size), size)
 
 
-GATHER_COPIES = 54
+GATHER_COPIES = 58
 
 
 def gather_kernel(
@@ -340,12 +340,21 @@
     v_part = v_all.at[x, me.ys(1), lower]
     v_far.append(send(v_part, v_part, me.over_y(-1)))
 
+    first, second = pl.ds(0, 2), pl.ds(2, 2)
+
+    def lines(blocks, place, over):
+        ahead, back = [], []
+        for part_ahead, part_back in ((first, second), (second, first)):
+            part = blocks.at[place, part_ahead]
+            ahead.append(send(part, part, over(1)))
+            part = blocks.at[place, part_back]
+            back.append(send(part, part, over(-1)))
+        return ahead, back
+
     arrived([k_swap], k_far)
-    k_right = [send(k_all.at[y], k_all.at[y], me.over_y(1))]
-    k_left = [send(k_all.at[y], k_all.at[y], me.over_y(-1))]
+    k_right, k_left = lines(k_all, y, me.over_y)
     arrived([v_swap], v_far)
-    v_right = [send(v_all.at[x], v_all.at[x], me.over_x(1))]
-    v_left = [send(v_all.at[x], v_all.at[x], me.over_x(-1))]
+    v_right, v_left = lines(v_all, x, me.over_x)
 
     def forward(hop, sign, blocks, copies):
         arrived(copies[hop - 1])
@@ -363,6 +372,16 @@
     table_store.start()
     every_array = ((q_all, q_near), (do_all, do_near), (st_all, st_near))
     bring_near(every_array, 0)
+
+    def across(copies, blocks, start, part, device):
+        arrived(copies[:1])
+        part = blocks.at[start, part]
+        return send(part, part, device)
+
+    k_far = [across(k_right, k_all, me.ys(-1), first, me.over_y(1))]
+    v_far = [across(v_right, v_all, me.xs(-1), first, me.over_x(1))]
+    k_far.append(across(k_left, k_all, me.ys(1), second, me.over_y(-1)))
+    v_far.append(across(v_left, v_all, me.xs(1), second, me.over_x(-1)))
     forward(1, 1, do_all, do_up)
     forward(1, -1, q_all, q_down)
     forward(1, 1, st_all, st_up)
@@ -370,19 +389,6 @@
     bring_near(every_array, 1)
     bring_near(every_array, -1)
 
-    def across(blocks, start, low, device):
-        part = blocks.at[start, pl.ds(low, 2)]
-        return send(part, part, device)
-
-    arrived(k_right)
-    k_far = [across(k_all, me.ys(-1), 0, me.over_y(1))]
-    arrived(v_right)
-    v_far = [across(v_all, me.xs(-1), 0, me.over_x(1))]
-    arrived(k_left)
-    k_far.append(across(k_all, me.ys(1), 2, me.over_y(-1)))
-    arrived(v_left)
-    v_far.append(across(v_all, me.xs(1), 2, me.over_x(-1)))
-
     forward(2, 1, q_all, q_up)
     forward(2, -1, do_all, do_down)
     forward(2, 1, do_all, do_up)
@@ -392,9 +398,7 @@
 
     bring_near(every_array, 2)
     bring_near(every_array, -2)
-    forward(3, 1, q_all, q_up)
-    forward(3, -1, do_all, do_down)
-    arrived(k_far, v_far)
+    arrived(k_right[1:], k_left[1:], v_right[1:], v_left[1:], k_far, v_far)
     for copy in nears:
         copy.wait()
     to_scalars.wait()
@@ -440,6 +444,8 @@
         return carry
 
     lax.fori_loop(0, FIRST_EARLY, early, 0)
+    forward(3, 1, q_all, q_up)
+    forward(3, -1, do_all, do_down)
     forward(3, 1, st_all, st_up)
     lax.fori_loop(FIRST_EARLY, EARLY, early, 0)
     arrived(do_up[2], q_down[2], st_down[2], q_up[3], do_down[3], st_up[3])
@@ -697,20 +703,27 @@
 
     half_rows = (pl.ds(0, HALF), pl.ds(HALF, HALF))
 
-    def turn(arrivals, own, here, near, middle, far, end, sems, axis, over, place):
+    def mix(own, here, near, middle, row):
+        add_rows(middle.at[row], [own.at[here, row], near.at[0, row], near.at[1, row]], BLK)
+
+    def turn_far(arrivals, own, here, near, middle, far, axis, over):
         for arrival in arrivals:
             arrival.wait_recv()
-        for row in range(4):
-            add_rows(middle.at[row], [own.at[here, row], near.at[0, row], near.at[1, row]], BLK)
-        ahead, back = axis(1), axis(-1)
         farthest = axis(2)
+        mix(own, here, near, middle, farthest)
         far_a = send(middle.at[farthest, half_rows[0]], far.at[0], over(1))
         far_b = send(middle.at[farthest, half_rows[1]], far.at[1], over(-1))
-        send(middle.at[ahead, half_rows[1]], end.at[0, core], over(1, owner=1), sems.at[0, core])
-        send(middle.at[back, half_rows[0]], end.at[1, core], over(-1, owner=0), sems.at[1, core])
+        return far_a, far_b
+
+    def turn_near(own, here, near, middle, end, sems, axis, over, place):
+        for side, step in enumerate((1, -1)):
+            row, owner = axis(step), 1 - side
+            mix(own, here, near, middle, row)
+            part = middle.at[row, half_rows[owner]]
+            send(part, end.at[side, core], over(step, owner=owner), sems.at[side, core])
+        mix(own, here, near, middle, place)
         send(middle.at[place, half_of(1 - core, HALF)], end.at[2, core], me.sibling, sems.at[2, core])
         end[2, core] = middle[place, half_of(core, HALF), :]
-        return far_a, far_b
 
     def last(arrival, middle, at, half, far, end, sems, side, device):
         arrival.wait_recv()
@@ -718,12 +731,10 @@
         add_rows(part, [part, far], HALF)
         send(part, end.at[side, core], device, sems.at[side, core])
 
-    kx_a, kx_b = turn(
-        k_in, dk_part, y, k_near, k_mid, k_mid_far, k_end, k_end_sems, me.xs, me.over_x, x
-    )
-    vy_a, vy_b = turn(
-        v_in, dv_part, x, v_near, v_mid, v_mid_far, v_end, v_end_sems, me.ys, me.over_y, y
-    )
+    kx_a, kx_b = turn_far(k_in, dk_part, y, k_near, k_mid, k_mid_far, me.xs, me.over_x)
+    vy_a, vy_b = turn_far(v_in, dv_part, x, v_near, v_mid, v_mid_far, me.ys, me.over_y)
+    turn_near(dk_part, y, k_near, k_mid, k_end, k_end_sems, me.xs, me.over_x, x)
+    turn_near(dv_part, x, v_near, v_mid, v_end, v_end_sems, me.ys, me.over_y, y)
     last(kx_a, k_mid, me.xs(1), 0, k_mid_far.at[0], k_end, k_end_sems, 0, me.over_x(1, owner=0))
     last(kx_b, k_mid, me.xs(-1), 1, k_mid_far.at[1], k_end, k_end_sems, 1, me.over_x(-1, owner=1))
     last(vy_a, v_mid, me.ys(1), 0, v_mid_far.at[0], v_end, v_end_sems, 0, me.over_y(1, owner=0))

time: 102 us -> 97.9 us (0.960)
  Pallas kernels: 99.6 us -> 95.1 us
    pallas_call x1, Pallas kernels: 40.2 us -> 33.7 us  [reduce_parts(): pl.pallas_call(reduce_kernel, out_shape=[jax.ShapeDtypeStruct((BLK, WIDTH...]
    pallas_call x1, Pallas kernels: 5.78 us -> 8.57 us  [pairs_over_blocks(): pl.pallas_call(pair_kernel, out_shape=[jax.ShapeDtypeStruct((QUERY_BLOCKS...]
where the time goes in v6:
time: 97.9 us; the launch traced here: 97.8 us
  Pallas kernels  95.1 us (97%)
  local copies, waits for them, and re-layouts  2.01 us (2%)
    pallas_call x1, Pallas kernels, gather(): pl.pallas_call(gather_kernel, out_shape=[jax.ShapeDtypeStruct((NZ, CORES,...  52.9 us
    pallas_call x1, Pallas kernels, reduce_parts(): pl.pallas_call(reduce_kernel, out_shape=[jax.ShapeDtypeStruct((BLK, WIDTH...  33.7 us
    pallas_call x1, Pallas kernels, pairs_over_blocks(): pl.pallas_call(pair_kernel, out_shape=[jax.ShapeDtypeStruct((QUERY_BLOCKS...  8.57 us
    unnamed x3, local copies, waits for them, and re-layouts  2.01 us

profile of v6, /device:TPU:1, one launch (start us, length us, event | category | flops | bytes accessed | tf_op | source)
XLA Modules:
  0.0 97.8 jit_solution(17083494766361605310)
XLA Ops:
  0.6 52.9 %gather_blocks.1 = (bf16[8,2,128,512]{3,2,1,0:T(8,128)(2,1)S(1)}, bf16[8,2,128,512]{3,2,1,0:T(8,128)(2,1)S(1)}, f32[8,2,16,128]{3,2,1,0:T(8,128)S(1)}, bf16[4,4,...) custom-call(bf16[128,1024]{1,0:T(8,128)(2,1)} %q_ref.1, ...), custom_call_target="tpu_custom_call" | custom-call | tf_op jit(solution)/shard_map/gather_blocks/pallas_call | solution.py:458
  53.5 8.6 %used_pairs.1 = (bf16[16,512,128]{2,1,0:T(8,128)(2,1)S(1)}, bf16[4,4,128,512]{3,2,1,0:T(8,128)(2,1)S(1)}, bf16[4,4,128,512]{3,2,1,0:T(8,128)(2,1)S(1)}) custom-call(s32[8,128]{1,0:T(8,128)S(1)} %get-tuple-element.15.table, bf16[16,128,512]{2,1,0:T(8,128)(2,1)S(1)} %bitcast.8, bf16[16,128,512]{2,1,0:T(8,128)(2,1)S(1)} %bitcast.9, ...), custom_call_target="tpu_custom_call" | custom-call | tf_op jit(solution)/shard_map/used_pairs/pallas_call | solution.py:588
  62.1 33.7 %reduce_parts.1 = (bf16[128,1024]{1,0:T(8,128)(2,1)S(1)}, bf16[64,1024]{1,0:T(8,128)(2,1)S(1)}, bf16[64,1024]{1,0:T(8,128)(2,1)S(1)}) custom-call(bf16[8,2,512,128]{3,2,1,0:T(8,128)(2,1)S(1)} %bitcast.7, bf16[4,4,128,512]{3,2,1,0:T(8,128)(2,1)S(1)} %get-tuple-element.25.dk_part, bf16[4,4,128,512]{3,2,1,0:T(8,128)(2,1)S(1)} %get-tuple-element.26.dv_part), custom_call_target="tpu_custom_call" | custom-call | tf_op jit(solution)/shard_map/reduce_parts/pallas_call | solution.py:777
  95.8 0.7 copy.14
  96.5 0.7 copy.15
  97.1 0.7 copy.16

commit v7 on v6

--- a/solution.py
+++ b/solution.py
@@ -19,8 +19,11 @@
 KEY_BLOCKS = NX * NY
 CELLS = KEY_BLOCKS * QUERY_BLOCKS
 NEAR = 5
-EARLY = 20
-FIRST_EARLY = 9
+FIRST = 8
+SECOND = 17
+EARLY = FIRST + SECOND
+BEFORE_HOP = 5
+LINES = 3
 TABLE = (8, 128)
 SCALE = 64**-0.5
 LOG2E = 1.4426950408889634
@@ -171,7 +174,7 @@
             add_dq(slice(low, low + 64), both[rows, side * BLK : side * BLK + BLK])
 
 
-def tabulate(lists, counts, x, z, table):
+def tabulate(lists, counts, x, y, z, table):
     cell = lax.broadcasted_iota(jnp.int32, (CELLS, KEY_SHARDS), 0)
     shard = lax.broadcasted_iota(jnp.int32, (SLOTS, KEY_SHARDS), 1)
     slot = lax.broadcasted_iota(jnp.int32, (SLOTS, KEY_SHARDS), 0)
@@ -193,10 +196,21 @@
     before = before > lax.broadcasted_iota(jnp.int32, (CELLS, CELLS), 1)
     before = jnp.where(before, 1.0, 0.0).astype(BF16)
     spread = jnp.zeros((CELLS, 128), F32)
-    near_rank = lax.dot_general(before, (near + spread).astype(BF16), NN, preferred_element_type=F32)
-    early = jnp.where(near_rank < EARLY, near + spread, 0.0)
-    others = (used + spread) - early
-    other_rank = lax.dot_general(before, others.astype(BF16), NN, preferred_element_type=F32)
+    up_block = lax.shift_right_logical(order, 6)
+    across_block = lax.shift_right_logical(order, 4) & 3
+    close = (((up_block - y + 1 + NY) & 3) < LINES) & (((across_block - x + 1 + NX) & 3) < LINES)
+
+    def ranks(cells):
+        return lax.dot_general(before, cells.astype(BF16), NN, preferred_element_type=F32)
+
+    closest = jnp.where(close, near, 0.0) + spread
+    first_rank = ranks(closest)
+    first = jnp.where(first_rank < FIRST, closest, 0.0)
+    second = (near + spread) - first
+    second_rank = ranks(second)
+    second = jnp.where(second_rank < SECOND, second, 0.0)
+    others = (used + spread) - first - second
+    other_rank = ranks(others)
     lane = lax.broadcasted_iota(jnp.int32, (CELLS, 128), 1)
     line = lax.broadcasted_iota(jnp.int32, (CELLS, 128), 0)
     number = line.astype(F32)
@@ -206,11 +220,13 @@
 
     place = lane.astype(F32)
     rows = [
-        total(jnp.where(near_rank == place, early * number, 0.0)),
+        total(jnp.where(first_rank == place, first * number, 0.0))
+        + total(jnp.where(second_rank + FIRST == place, second * number, 0.0)),
         total(jnp.where(other_rank == place, others * number, 0.0)),
         total(jnp.where(other_rank == place + 128.0, others * number, 0.0)),
-        total(jnp.where(line < lane * QUERY_BLOCKS, early, 0.0)),
+        total(jnp.where(line < lane * QUERY_BLOCKS, first, 0.0)),
         total(jnp.where(line < lane * QUERY_BLOCKS, others, 0.0)),
+        total(jnp.where(line < lane * QUERY_BLOCKS, second, 0.0)),
     ]
     table[...] = jnp.zeros(TABLE, jnp.int32)
     for index, row in enumerate(rows):
@@ -227,7 +243,7 @@
 def gather_kernel(
     q_ref, do_ref, k_ref, v_ref, out_ref, lse_ref, list_ref, count_ref,
     q_all, do_all, st_all, k_all, v_all, table_out, dk_early, dv_early, dq_early,
-    do_buf, out_buf, lse_buf, st_buf, list_all, count_all, q_near, do_near, st_near,
+    do_buf, out_buf, lse_buf, st_buf, list_all, count_all, q_near, do_near, st_near, k_near, v_near,
     k_turned, p_buf, ds_buf, table, table_s, send_sems, recv_sems, local_sems, near_sems,
 ):
     me = Place()
@@ -365,7 +381,7 @@
     forward(1, -1, do_all, do_down)
     arrived(swaps)
     st_own.wait()
-    tabulate(list_all, count_all, x, z, table)
+    tabulate(list_all, count_all, x, y, z, table)
     to_scalars = pltpu.make_async_copy(table, table_s, local_sems.at[1])
     to_scalars.start()
     table_store = pltpu.make_async_copy(table, table_out, local_sems.at[2])
@@ -398,25 +414,37 @@
 
     bring_near(every_array, 2)
     bring_near(every_array, -2)
-    arrived(k_right[1:], k_left[1:], v_right[1:], v_left[1:], k_far, v_far)
+    arrived(k_right[1:], k_left[1:], v_right[1:], v_left[1:])
+    for step in (-1, 0, 1):
+        for blocks, line, held in ((k_all, me.ys(step), k_near), (v_all, me.xs(step), v_near)):
+            copy = pltpu.make_async_copy(blocks.at[line], held.at[step + 1], near_sems.at[len(nears)])
+            copy.start()
+            nears.append(copy)
     for copy in nears:
         copy.wait()
     to_scalars.wait()
     halves = head_halves()
-    used = table_s[3, KEY_BLOCKS]
-
-    def early(index, carry):
+    firsts, seconds = table_s[3, KEY_BLOCKS], table_s[5, KEY_BLOCKS]
+
+    def early(index, carry, close=False):
         entry = jnp.clip(table_s[0, index], 0, CELLS - 1)
         block = lax.div(entry, QUERY_BLOCKS)
         up_block, across_block = lax.div(block, NX), lax.rem(block, NX)
         query = lax.rem(lax.div(lax.rem(entry, QUERY_BLOCKS), CORES) - z + 2 + NZ, NZ)
         query = jnp.minimum(query, NEAR - 1)
         owner = lax.rem(entry, CORES)
+        keep = index < firsts if close else index - FIRST < seconds
+        up_line = jnp.minimum(lax.rem(up_block - y + 1 + NY, NY), LINES - 1)
+        across_line = jnp.minimum(lax.rem(across_block - x + 1 + NX, NX), LINES - 1)
 
         def keys(lanes):
+            if close:
+                return k_near[up_line, across_block, :, lanes]
             return k_all[up_block, across_block, :, lanes]
 
         def values(lanes):
+            if close:
+                return v_near[across_line, up_block, :, lanes]
             return v_all[across_block, up_block, :, lanes]
 
         def queries(lanes):
@@ -429,7 +457,7 @@
             return st_near[query, owner, row : row + 1, :]
 
         turn_keys(keys, k_turned)
-        pair_products(keys, values, queries, douts, stats, halves, p_buf, ds_buf, keep=index < used)
+        pair_products(keys, values, queries, douts, stats, halves, p_buf, ds_buf, keep=keep)
 
         def put_dv(lanes, value):
             dv_early[index, :, lanes] = value
@@ -443,11 +471,13 @@
         pair_gradients(queries, douts, halves, p_buf, ds_buf, k_turned, put_dv, put_dk, put_dq)
         return carry
 
-    lax.fori_loop(0, FIRST_EARLY, early, 0)
+    lax.fori_loop(0, FIRST, lambda index, carry: early(index, carry, close=True), 0)
+    arrived(k_far, v_far)
+    lax.fori_loop(FIRST, FIRST + BEFORE_HOP, early, 0)
     forward(3, 1, q_all, q_up)
     forward(3, -1, do_all, do_down)
     forward(3, 1, st_all, st_up)
-    lax.fori_loop(FIRST_EARLY, EARLY, early, 0)
+    lax.fori_loop(FIRST + BEFORE_HOP, EARLY, early, 0)
     arrived(do_up[2], q_down[2], st_down[2], q_up[3], do_down[3], st_up[3])
     table_store.wait()
     send.finish()
@@ -480,6 +510,8 @@
             pltpu.VMEM((NEAR, CORES, BLK, COLS), BF16),
             pltpu.VMEM((NEAR, CORES, BLK, COLS), BF16),
             pltpu.VMEM((NEAR, CORES, 2 * OWN_HEADS, BLK), F32),
+            pltpu.VMEM((LINES, 4, BLK, COLS), BF16),
+            pltpu.VMEM((LINES, 4, BLK, COLS), BF16),
             pltpu.VMEM((COLS, BLK), BF16),
             pltpu.VMEM((HEAD_PAIRS, BLK, 2 * BLK), BF16),
             pltpu.VMEM((HEAD_PAIRS, BLK, 2 * BLK), BF16),
@@ -488,7 +520,7 @@
             pltpu.SemaphoreType.DMA((GATHER_COPIES,)),
             pltpu.SemaphoreType.DMA((GATHER_COPIES,)),
             pltpu.SemaphoreType.DMA((9,)),
-            pltpu.SemaphoreType.DMA((3 * NEAR,)),
+            pltpu.SemaphoreType.DMA((3 * NEAR + 2 * LINES,)),
         ],
         compiler_params=pltpu.CompilerParams(
             collective_id=0, has_side_effects=True, vmem_limit_bytes=GATHER_LIMIT
@@ -511,9 +543,10 @@
 
     def key_block(block, carry):
         up, across = lax.div(block, NX), lax.rem(block, NX)
-        early_low, early_high = table[3, block], table[3, block + 1]
+        first_low, first_high = table[3, block], table[3, block + 1]
+        second_low, second_high = FIRST + table[5, block], FIRST + table[5, block + 1]
         low, high = table[4, block], table[4, block + 1]
-        have = (early_high - early_low) + (high - low)
+        have = (first_high - first_low) + (second_high - second_low) + (high - low)
 
         @pl.when(have == 0)
         def _():
@@ -563,7 +596,8 @@
         def _():
             dk_sum[...] = jnp.zeros_like(dk_sum)
             dv_sum[...] = jnp.zeros_like(dv_sum)
-            lax.fori_loop(early_low, early_high, take, 0)
+            lax.fori_loop(first_low, first_high, take, 0)
+            lax.fori_loop(second_low, second_high, take, 0)
 
             @pl.when(high > low)
             def _():

time: 97.9 us -> 99.5 us (1.016)
  Pallas kernels: 95.1 us -> 96.8 us
    pallas_call x1, Pallas kernels: 33.7 us -> 36.3 us  [reduce_parts(): pl.pallas_call(reduce_kernel, out_shape=[jax.ShapeDtypeStruct((BLK, WIDTH...]
    pallas_call x1, Pallas kernels: 8.57 us -> 7.51 us  [pairs_over_blocks(): pl.pallas_call(pair_kernel, out_shape=[jax.ShapeDtypeStruct((QUERY_BLOCKS...]
where the time goes in v7:
time: 99.5 us; the launch traced here: 99.4 us
  Pallas kernels  96.8 us (97%)
  local copies, waits for them, and re-layouts  2.01 us (2%)
    pallas_call x1, Pallas kernels, gather(): pl.pallas_call(gather_kernel, out_shape=[jax.ShapeDtypeStruct((NZ, CORES,...  52.9 us
    pallas_call x1, Pallas kernels, reduce_parts(): pl.pallas_call(reduce_kernel, out_shape=[jax.ShapeDtypeStruct((BLK, WIDTH...  36.3 us
    pallas_call x1, Pallas kernels, pairs_over_blocks(): pl.pallas_call(pair_kernel, out_shape=[jax.ShapeDtypeStruct((QUERY_BLOCKS...  7.51 us
    unnamed x3, local copies, waits for them, and re-layouts  2.01 us

profile of v7, /device:TPU:1, one launch (start us, length us, event | category | flops | bytes accessed | tf_op | source)
XLA Modules:
  0.0 99.4 jit_solution(9959864826521086988)
XLA Ops:
  0.6 52.9 %gather_blocks.1 = (bf16[8,2,128,512]{3,2,1,0:T(8,128)(2,1)S(1)}, bf16[8,2,128,512]{3,2,1,0:T(8,128)(2,1)S(1)}, f32[8,2,16,128]{3,2,1,0:T(8,128)S(1)}, bf16[4,4,...) custom-call(bf16[128,1024]{1,0:T(8,128)(2,1)} %q_ref.1, ...), custom_call_target="tpu_custom_call" | custom-call | tf_op jit(solution)/shard_map/gather_blocks/pallas_call | solution.py:488
  53.5 7.5 %used_pairs.1 = (bf16[16,512,128]{2,1,0:T(8,128)(2,1)S(1)}, bf16[4,4,128,512]{3,2,1,0:T(8,128)(2,1)S(1)}, bf16[4,4,128,512]{3,2,1,0:T(8,128)(2,1)S(1)}) custom-call(s32[8,128]{1,0:T(8,128)S(1)} %get-tuple-element.15.table, bf16[16,128,512]{2,1,0:T(8,128)(2,1)S(1)} %bitcast.8, bf16[16,128,512]{2,1,0:T(8,128)(2,1)S(1)} %bitcast.9, ...), custom_call_target="tpu_custom_call" | custom-call | tf_op jit(solution)/shard_map/used_pairs/pallas_call | solution.py:622
  61.1 36.3 %reduce_parts.1 = (bf16[128,1024]{1,0:T(8,128)(2,1)S(1)}, bf16[64,1024]{1,0:T(8,128)(2,1)S(1)}, bf16[64,1024]{1,0:T(8,128)(2,1)S(1)}) custom-call(bf16[8,2,512,128]{3,2,1,0:T(8,128)(2,1)S(1)} %bitcast.7, bf16[4,4,128,512]{3,2,1,0:T(8,128)(2,1)S(1)} %get-tuple-element.25.dk_part, bf16[4,4,128,512]{3,2,1,0:T(8,128)(2,1)S(1)} %get-tuple-element.26.dv_part), custom_call_target="tpu_custom_call" | custom-call | tf_op jit(solution)/shard_map/reduce_parts/pallas_call | solution.py:811
  97.4 0.7 copy.14
  98.1 0.7 copy.15
  98.8 0.7 copy.16

commit v8 on v7

--- a/solution.py
+++ b/solution.py
@@ -18,11 +18,11 @@
 QUERY_BLOCKS = NZ * CORES
 KEY_BLOCKS = NX * NY
 CELLS = KEY_BLOCKS * QUERY_BLOCKS
-NEAR = 5
+REACH = 3
+NEAR = 2 * REACH + 1
 FIRST = 8
 SECOND = 17
 EARLY = FIRST + SECOND
-BEFORE_HOP = 5
 LINES = 3
 TABLE = (8, 128)
 SCALE = 64**-0.5
@@ -190,8 +190,9 @@
             used = jnp.where(cell == code[row : row + 1, :], 1.0, used)
     used = jnp.max(used, axis=1, keepdims=True)
     order = lax.broadcasted_iota(jnp.int32, (CELLS, 1), 0)
-    away = (lax.shift_right_logical(order & 15, 1) - z + 2 + NZ) & 7
+    away = (lax.shift_right_logical(order & 15, 1) - z + REACH + NZ) & 7
     near = jnp.where(away < NEAR, used, 0.0)
+    nearer = jnp.where((away > 0) & (away < NEAR - 1), used, 0.0)
     before = lax.broadcasted_iota(jnp.int32, (CELLS, CELLS), 0)
     before = before > lax.broadcasted_iota(jnp.int32, (CELLS, CELLS), 1)
     before = jnp.where(before, 1.0, 0.0).astype(BF16)
@@ -203,7 +204,7 @@
     def ranks(cells):
         return lax.dot_general(before, cells.astype(BF16), NN, preferred_element_type=F32)
 
-    closest = jnp.where(close, near, 0.0) + spread
+    closest = jnp.where(close, nearer, 0.0) + spread
     first_rank = ranks(closest)
     first = jnp.where(first_rank < FIRST, closest, 0.0)
     second = (near + spread) - first
@@ -244,7 +245,7 @@
     q_ref, do_ref, k_ref, v_ref, out_ref, lse_ref, list_ref, count_ref,
     q_all, do_all, st_all, k_all, v_all, table_out, dk_early, dv_early, dq_early,
     do_buf, out_buf, lse_buf, st_buf, list_all, count_all, q_near, do_near, st_near, k_near, v_near,
-    k_turned, p_buf, ds_buf, table, table_s, send_sems, recv_sems, local_sems, near_sems,
+    k_turned, p_buf, ds_buf, table, table_s, send_sems, recv_sems, local_sems, near_sems, far_sems,
 ):
     me = Place()
     x, y, z, core = me.x, me.y, me.z, me.core
@@ -320,7 +321,7 @@
     def bring_near(arrays, distance):
         for blocks, held in arrays:
             copy = pltpu.make_async_copy(
-                blocks.at[me.zs(distance)], held.at[distance + 2], near_sems.at[len(nears)]
+                blocks.at[me.zs(distance)], held.at[distance + REACH], near_sems.at[len(nears)]
             )
             copy.start()
             nears.append(copy)
@@ -430,7 +431,7 @@
         entry = jnp.clip(table_s[0, index], 0, CELLS - 1)
         block = lax.div(entry, QUERY_BLOCKS)
         up_block, across_block = lax.div(block, NX), lax.rem(block, NX)
-        query = lax.rem(lax.div(lax.rem(entry, QUERY_BLOCKS), CORES) - z + 2 + NZ, NZ)
+        query = lax.rem(lax.div(lax.rem(entry, QUERY_BLOCKS), CORES) - z + REACH + NZ, NZ)
         query = jnp.minimum(query, NEAR - 1)
         owner = lax.rem(entry, CORES)
         keep = index < firsts if close else index - FIRST < seconds
@@ -473,12 +474,22 @@
 
     lax.fori_loop(0, FIRST, lambda index, carry: early(index, carry, close=True), 0)
     arrived(k_far, v_far)
-    lax.fori_loop(FIRST, FIRST + BEFORE_HOP, early, 0)
     forward(3, 1, q_all, q_up)
     forward(3, -1, do_all, do_down)
     forward(3, 1, st_all, st_up)
-    lax.fori_loop(FIRST + BEFORE_HOP, EARLY, early, 0)
-    arrived(do_up[2], q_down[2], st_down[2], q_up[3], do_down[3], st_up[3])
+    arrived(do_up[2], q_down[2], st_down[2])
+    nears.clear()
+    for distance in (REACH, -REACH):
+        for blocks, held in every_array:
+            copy = pltpu.make_async_copy(
+                blocks.at[me.zs(distance)], held.at[distance + REACH], far_sems.at[len(nears)]
+            )
+            copy.start()
+            nears.append(copy)
+    for copy in nears:
+        copy.wait()
+    lax.fori_loop(FIRST, EARLY, early, 0)
+    arrived(q_up[3], do_down[3], st_up[3])
     table_store.wait()
     send.finish()
     assert len(send.copies) == GATHER_COPIES, len(send.copies)
@@ -520,7 +531,8 @@
             pltpu.SemaphoreType.DMA((GATHER_COPIES,)),
             pltpu.SemaphoreType.DMA((GATHER_COPIES,)),
             pltpu.SemaphoreType.DMA((9,)),
-            pltpu.SemaphoreType.DMA((3 * NEAR + 2 * LINES,)),
+            pltpu.SemaphoreType.DMA((3 * (NEAR - 2) + 2 * LINES,)),
+            pltpu.SemaphoreType.DMA((6,)),
         ],
         compiler_params=pltpu.CompilerParams(
             collective_id=0, has_side_effects=True, vmem_limit_bytes=GATHER_LIMIT

time: 99.5 us -> 101 us (1.015)
  Pallas kernels: 96.8 us -> 98.6 us
    pallas_call x1, Pallas kernels: 52.9 us -> 56.3 us  [gather(): pl.pallas_call(gather_kernel, out_shape=[jax.ShapeDtypeStruct((NZ, CORES,...]
    pallas_call x1, Pallas kernels: 7.51 us -> 5.9 us  [pairs_over_blocks(): pl.pallas_call(pair_kernel, out_shape=[jax.ShapeDtypeStruct((QUERY_BLOCKS...]
where the time goes in v8:
time: 101 us
  Pallas kernels  98.6 us (98%)
  local copies, waits for them, and re-layouts  2.01 us (2%)
    pallas_call x1, Pallas kernels, gather(): pl.pallas_call(gather_kernel, out_shape=[jax.ShapeDtypeStruct((NZ, CORES,...  56.3 us
    pallas_call x1, Pallas kernels, reduce_parts(): pl.pallas_call(reduce_kernel, out_shape=[jax.ShapeDtypeStruct((BLK, WIDTH...  36.4 us
    pallas_call x1, Pallas kernels, pairs_over_blocks(): pl.pallas_call(pair_kernel, out_shape=[jax.ShapeDtypeStruct((QUERY_BLOCKS...  5.9 us

profile of v8, /device:TPU:1, one launch (start us, length us, event | category | flops | bytes accessed | tf_op | source)
XLA Modules:
  0.0 101.3 jit_solution(14709622363102375486)
XLA Ops:
  0.6 56.3 %gather_blocks.1 = (bf16[8,2,128,512]{3,2,1,0:T(8,128)(2,1)S(1)}, bf16[8,2,128,512]{3,2,1,0:T(8,128)(2,1)S(1)}, f32[8,2,16,128]{3,2,1,0:T(8,128)S(1)}, bf16[4,4,...) custom-call(bf16[128,1024]{1,0:T(8,128)(2,1)} %q_ref.1, ...), custom_call_target="tpu_custom_call" | custom-call | tf_op jit(solution)/shard_map/gather_blocks/pallas_call | solution.py:499
  56.9 5.9 %used_pairs.1 = (bf16[16,512,128]{2,1,0:T(8,128)(2,1)S(1)}, bf16[4,4,128,512]{3,2,1,0:T(8,128)(2,1)S(1)}, bf16[4,4,128,512]{3,2,1,0:T(8,128)(2,1)S(1)}) custom-call(s32[8,128]{1,0:T(8,128)S(1)} %get-tuple-element.15.table, bf16[16,128,512]{2,1,0:T(8,128)(2,1)S(1)} %bitcast.8, bf16[16,128,512]{2,1,0:T(8,128)(2,1)S(1)} %bitcast.9, ...), custom_call_target="tpu_custom_call" | custom-call | tf_op jit(solution)/shard_map/used_pairs/pallas_call | solution.py:634
  62.8 36.4 %reduce_parts.1 = (bf16[128,1024]{1,0:T(8,128)(2,1)S(1)}, bf16[64,1024]{1,0:T(8,128)(2,1)S(1)}, bf16[64,1024]{1,0:T(8,128)(2,1)S(1)}) custom-call(bf16[8,2,512,128]{3,2,1,0:T(8,128)(2,1)S(1)} %bitcast.7, bf16[4,4,128,512]{3,2,1,0:T(8,128)(2,1)S(1)} %get-tuple-element.25.dk_part, bf16[4,4,128,512]{3,2,1,0:T(8,128)(2,1)S(1)} %get-tuple-element.26.dv_part), custom_call_target="tpu_custom_call" | custom-call | tf_op jit(solution)/shard_map/reduce_parts/pallas_call | solution.py:823
  99.2 0.7 copy.14
  99.9 0.7 copy.15
  100.6 0.7 copy.16
